TPU v7x, 128 devices: a whole 4x4x4 slice. The times are simulated.
128 devices in a mesh: real: 8 (over y_lo, z), gen: 16 (over x, y_hi, core).
Axes of the slice: x: 4, y: 4 (y_hi: 2, y_lo: 2; y = y_hi * 2 + y_lo), z: 4, core: 2. Of those that a mesh axis runs over, the one named last changes fastest.
Arguments:
- hidden: float32 [4096, 256], P('gen'), may hold values from -6 to 6
- weight: float32 [256, 512], P(None, 'real'), may hold values from -0.375 to 0.375
- lengths: int32 [4096], P('gen'), may hold values from 1 to 512
- real_rows: float32 [131072, 256], P('real')
Outputs:
- update: float32 [256, 512], P(None, 'real')
- loss: float32 [], replicated
All inputs are finite; a program needn't handle non-finite values.
Results may differ from a plain program's by a relative error of at most 0.0003.
Values sent between devices are 32-bit elements; how exact they have to be, the bound alone decides.
No kernel may reach another device: no remote copies, remote signals or barrier semaphores. Data moves between devices by JAX's collectives and lax.ppermute only.
A program may use at most 128 MiB of HBM per device.

v0:
```python
import jax
import jax.numpy as jnp
from jax import lax
from jax.sharding import PartitionSpec as P

NUM_BINS = 256
SEQ_STEPS = 512
HID_WIDTH = 256


highest = lax.Precision.HIGHEST
scale_factors = (0.25, 0.5, 1.0, 2.0, 4.0)


def bin_table():
    spacing = 6.0 / NUM_BINS
    centers = (jnp.arange(NUM_BINS, dtype=jnp.float32) + 0.5) * spacing
    return (centers, spacing)


def pair_terms(left, left_sq, right, spread):
    inner_prod = jnp.einsum("ib,jb->ij", left, right, precision=highest)
    right_sq = jnp.sum(right * right, 1)
    distance = left_sq[:, None] + right_sq[None, :] - 2.0 * inner_prod
    kernel = jnp.zeros_like(distance)
    weights = jnp.zeros_like(distance)
    for factor in scale_factors:
        kernel_width = factor * spread
        decayed = jnp.exp(-distance / kernel_width)
        kernel = kernel + decayed
        weights = weights + decayed / kernel_width
    return (jnp.sum(kernel), jnp.sum(weights, 1), jnp.dot(weights, right, precision=highest))


def per_device(hidden, weight, lengths, real_rows):
    centers, spacing = bin_table()
    real_count = lax.axis_size("real")
    gen_count = lax.axis_size("gen")
    real_index = lax.axis_index("real")
    flows = hidden.shape[0]
    local_steps = weight.shape[1]
    total_flows = flows * gen_count
    total_real = real_rows.shape[0] * real_count
    pre = jnp.dot(hidden, weight, precision=highest)
    values = jax.nn.softplus(pre)
    positions = real_index * local_steps + jnp.arange(local_steps, dtype=jnp.int32)
    mask = (positions[None, :] < lengths[:, None]).astype(jnp.float32)
    length_f = lengths.astype(jnp.float32)
    offset = values[:, :, None] - centers
    bumps = jnp.exp(-offset * offset / (2.0 * spacing * spacing))
    partial_counts = jnp.einsum("gt,gtb->gb", mask, bumps, precision=highest)
    counts = lax.psum(partial_counts, "real")
    hist = counts / length_f[:, None]
    gen_sq = jnp.sum(hist * hist)
    gen_sum = jnp.sum(hist, 0)
    real_sq = jnp.sum(real_rows * real_rows)
    real_sum = jnp.sum(real_rows, 0)
    gen_sq, gen_sum = lax.psum((gen_sq, gen_sum), "gen")
    real_sq, real_sum = lax.psum((real_sq, real_sum), "real")
    spread = (
        gen_sq / total_flows
        + real_sq / total_real
        - 2.0 * jnp.dot(gen_sum / total_flows, real_sum / total_real, precision=highest)
    )
    hist_sq = jnp.sum(hist * hist, 1)
    block_rows = min(real_rows.shape[0], 2048)
    stacked = real_rows.reshape(-1, block_rows, real_rows.shape[1])
    start = (
        jnp.zeros((), jnp.float32),
        jnp.zeros((flows,), jnp.float32),
        jnp.zeros((flows, NUM_BINS), jnp.float32),
    )

    def cross_step(carry, rows):
        part_k, part_row, part_mat = pair_terms(hist, hist_sq, rows, spread)
        return ((carry[0] + part_k, carry[1] + part_row, carry[2] + part_mat), None)

    (cross_k, cross_row, cross_mat), _ = lax.scan(cross_step, start, stacked)
    cross_term = 4.0 / total_real * (cross_row[:, None] * hist - cross_mat)
    part_k, part_row, part_mat = pair_terms(
        hist, hist_sq, lax.all_gather(hist, "gen", axis=0, tiled=True), spread
    )
    pair_term = -4.0 / total_flows * (part_row[:, None] * hist - part_mat)
    grad_hist = lax.psum(cross_term, "real") + pair_term
    loss_part = part_k / (total_flows * total_flows * real_count) - 2.0 * cross_k / (
        total_flows * total_real
    )
    loss = lax.psum(loss_part, ("real", "gen"))
    grad_counts = grad_hist / length_f[:, None]
    slope = jnp.einsum("gtb,gb->gt", bumps * -offset, grad_counts, precision=highest)
    grad_pre = mask * slope / (spacing * spacing) * jax.nn.sigmoid(pre)
    partial_grad = jnp.einsum("gz,gt->zt", hidden, grad_pre, precision=highest)
    grad_weight = lax.psum(partial_grad, "gen")
    square_sum = lax.psum(jnp.sum(grad_weight * grad_weight), "real")
    mean_sq = square_sum / (HID_WIDTH * SEQ_STEPS)
    update = grad_weight / jnp.sqrt(mean_sq + 1e-06)
    return (update, loss)


def solution(mesh):
    in_specs = (P("gen", None), P(None, "real"), P("gen"), P("real", None))
    out_specs = (P(None, "real"), P())
    return jax.shard_map(
        per_device, mesh=mesh, in_specs=in_specs, out_specs=out_specs, check_vma=False
    )
```

profile of v0, /device:TPU:0, one launch (start us, length us, event | category | flops | bytes accessed | tf_op | source)
XLA Modules:
  0.0 565.8 jit_solution(14848601514917474657)
XLA Ops:
  7.7 0.8 compare_bitcast_fusion
  8.8 1.9 compare_select_fusion
  10.7 10.1 %fusion.16 = f32[256,1,256]{2,1,0:T(1,128)S(1)} fusion(pred[256,64,1]{1,2,0:T(4,128)(4,1)S(1)} %copy.7, f32[256]{0:T(256)S(1)} %add_multiply_fusion, f32[256,64]{1,0:T(8,128)S(1)} %copy.6), kind=kOutput, calls=%fused_computation.26 | convolution fusion | flops 67108864 | bytes 345088 | tf_op jit(solution)/shard_map/gt,gtb->gb/dot_general | solution.py:51
  20.9 0.7 copy.16
  21.7 8.7 %fusion.50 = (f32[256]{0:T(256)S(1)}, f32[]{:T(128)}) fusion(f32[16384,256]{1,0:T(8,128)} %param.9), kind=kLoop, calls=%fused_computation.83 | loop fusion | flops 12582655 | bytes 16778244 | tf_op jit(solution)/shard_map/reduce_sum | solution.py:57
  30.4 21.8 %all-reduce.1 = (f32[]{:T(128)}, f32[256]{0:T(256)S(1)}) all-reduce(f32[]{:T(128)} %get-tuple-element.135, f32[256]{0:T(256)S(1)} %get-tuple-element.134), channel_id=1, replica_groups=mesh['real'=8,'gen'=16] {'real'}, use_global_device_ids=true, to_apply=%region_5.6 | all-reduce | flops 257 | bytes 2056 | tf_op jit(solution)/shard_map/psum | solution.py:59
  52.8 45.7 %all-reduce.6.cloned.1.call-done = f32[256,256]{1,0:T(8,128)} async-done(((f32[256,256]{1,0:T(8,128)}), f32[256,256]{1,0:T(8,128)}) %all-reduce.6.cloned.1.call-update) | async-done | bytes 262160 | tf_op jit(solution)/shard_map/psum | solution.py:52
  98.5 2.4 fusion.51
  100.9 33.8 %all-reduce = (f32[]{:T(128)}, f32[256]{0:T(256)S(1)}) all-reduce(f32[]{:T(128)} %get-tuple-element.137, f32[256]{0:T(256)S(1)} %get-tuple-element.136), channel_id=1, replica_groups=mesh['real'=8,'gen'=16] {'gen'}, use_global_device_ids=true, to_apply=%region_3.4 | all-reduce | flops 257 | bytes 2056 | tf_op jit(solution)/shard_map/psum | solution.py:58
  135.4 0.7 multiply_reduce_fusion.5
  136.8 111.0 %while.16 = (s32[]{:T(128)}, f32[]{:T(128)}, f32[256]{0:T(256)S(1)}, f32[256,256]{1,0:T(8,128)S(1)}, f32[256]{0:T(256)S(1)}, /*index=5*/f32[8,2048,256]{2,1,0:T(...) while((s32[]{:T(128)}, f32[]{:T(128)}, ...), condition=%wide.region_14.15_spmd.clone, body=%wide.region_10.14_spmd.clone.sunk | while | flops 3234986240 | bytes 11296436 | solution.py:78
  136.8 1.9 fusion.73
  138.8 6.2 %fusion.74 = (f32[256]{0:T(256)S(1)}, f32[256,2048]{0,1:T(8,128)S(1)}, f32[]{:T(128)}) fusion(f32[]{:T(128)} %get-tuple-element.294, f32[]{:T(128)} %get-tuple-element.293, f32[]{:T(128)} %get-tuple-element.292, f32[]{:T(128)} %get-tuple-element.291, f32[]{:T(128)} %get-tuple-element.290, f32[256,256]{1,0:T(8,128)} %get-tuple-element.289, ...), kind=kOutput, calls=%fused_computation.85.clone.1 | convolution fusion | flops 1623195392 | bytes 4469256 | tf_op jit(solution)/shard_map/while/body/eval_jaxpr/ib,jb->ij/dot_general | solution.py:22
  145.6 5.1 fusion.75
  150.7 1.9 fusion.73
  152.6 6.2 %fusion.74 = (f32[256]{0:T(256)S(1)}, f32[256,2048]{0,1:T(8,128)S(1)}, f32[]{:T(128)}) fusion(f32[]{:T(128)} %get-tuple-element.294, f32[]{:T(128)} %get-tuple-element.293, f32[]{:T(128)} %get-tuple-element.292, f32[]{:T(128)} %get-tuple-element.291, f32[]{:T(128)} %get-tuple-element.290, f32[256,256]{1,0:T(8,128)} %get-tuple-element.289, ...), kind=kOutput, calls=%fused_computation.85.clone.1 | convolution fusion | flops 1623195392 | bytes 4469256 | tf_op jit(solution)/shard_map/while/body/eval_jaxpr/ib,jb->ij/dot_general | solution.py:22
  159.5 5.1 fusion.75
  164.6 1.9 fusion.73
  166.5 6.2 %fusion.74 = (f32[256]{0:T(256)S(1)}, f32[256,2048]{0,1:T(8,128)S(1)}, f32[]{:T(128)}) fusion(f32[]{:T(128)} %get-tuple-element.294, f32[]{:T(128)} %get-tuple-element.293, f32[]{:T(128)} %get-tuple-element.292, f32[]{:T(128)} %get-tuple-element.291, f32[]{:T(128)} %get-tuple-element.290, f32[256,256]{1,0:T(8,128)} %get-tuple-element.289, ...), kind=kOutput, calls=%fused_computation.85.clone.1 | convolution fusion | flops 1623195392 | bytes 4469256 | tf_op jit(solution)/shard_map/while/body/eval_jaxpr/ib,jb->ij/dot_general | solution.py:22
  173.3 5.1 fusion.75
  178.5 2.0 fusion.73
  180.5 6.2 %fusion.74 = (f32[256]{0:T(256)S(1)}, f32[256,2048]{0,1:T(8,128)S(1)}, f32[]{:T(128)}) fusion(f32[]{:T(128)} %get-tuple-element.294, f32[]{:T(128)} %get-tuple-element.293, f32[]{:T(128)} %get-tuple-element.292, f32[]{:T(128)} %get-tuple-element.291, f32[]{:T(128)} %get-tuple-element.290, f32[256,256]{1,0:T(8,128)} %get-tuple-element.289, ...), kind=kOutput, calls=%fused_computation.85.clone.1 | convolution fusion | flops 1623195392 | bytes 4469256 | tf_op jit(solution)/shard_map/while/body/eval_jaxpr/ib,jb->ij/dot_general | solution.py:22
  187.2 5.1 fusion.75
  192.4 1.9 fusion.73
  194.3 6.2 %fusion.74 = (f32[256]{0:T(256)S(1)}, f32[256,2048]{0,1:T(8,128)S(1)}, f32[]{:T(128)}) fusion(f32[]{:T(128)} %get-tuple-element.294, f32[]{:T(128)} %get-tuple-element.293, f32[]{:T(128)} %get-tuple-element.292, f32[]{:T(128)} %get-tuple-element.291, f32[]{:T(128)} %get-tuple-element.290, f32[256,256]{1,0:T(8,128)} %get-tuple-element.289, ...), kind=kOutput, calls=%fused_computation.85.clone.1 | convolution fusion | flops 1623195392 | bytes 4469256 | tf_op jit(solution)/shard_map/while/body/eval_jaxpr/ib,jb->ij/dot_general | solution.py:22
  201.1 5.1 fusion.75
  206.2 1.9 fusion.73
  208.2 6.2 %fusion.74 = (f32[256]{0:T(256)S(1)}, f32[256,2048]{0,1:T(8,128)S(1)}, f32[]{:T(128)}) fusion(f32[]{:T(128)} %get-tuple-element.294, f32[]{:T(128)} %get-tuple-element.293, f32[]{:T(128)} %get-tuple-element.292, f32[]{:T(128)} %get-tuple-element.291, f32[]{:T(128)} %get-tuple-element.290, f32[256,256]{1,0:T(8,128)} %get-tuple-element.289, ...), kind=kOutput, calls=%fused_computation.85.clone.1 | convolution fusion | flops 1623195392 | bytes 4469256 | tf_op jit(solution)/shard_map/while/body/eval_jaxpr/ib,jb->ij/dot_general | solution.py:22
  215.0 5.1 fusion.75
  220.1 1.9 fusion.73
  222.0 6.2 %fusion.74 = (f32[256]{0:T(256)S(1)}, f32[256,2048]{0,1:T(8,128)S(1)}, f32[]{:T(128)}) fusion(f32[]{:T(128)} %get-tuple-element.294, f32[]{:T(128)} %get-tuple-element.293, f32[]{:T(128)} %get-tuple-element.292, f32[]{:T(128)} %get-tuple-element.291, f32[]{:T(128)} %get-tuple-element.290, f32[256,256]{1,0:T(8,128)} %get-tuple-element.289, ...), kind=kOutput, calls=%fused_computation.85.clone.1 | convolution fusion | flops 1623195392 | bytes 4469256 | tf_op jit(solution)/shard_map/while/body/eval_jaxpr/ib,jb->ij/dot_general | solution.py:22
  228.8 5.1 fusion.75
  233.9 1.9 fusion.73
  235.9 6.2 %fusion.74 = (f32[256]{0:T(256)S(1)}, f32[256,2048]{0,1:T(8,128)S(1)}, f32[]{:T(128)}) fusion(f32[]{:T(128)} %get-tuple-element.294, f32[]{:T(128)} %get-tuple-element.293, f32[]{:T(128)} %get-tuple-element.292, f32[]{:T(128)} %get-tuple-element.291, f32[]{:T(128)} %get-tuple-element.290, f32[256,256]{1,0:T(8,128)} %get-tuple-element.289, ...), kind=kOutput, calls=%fused_computation.85.clone.1 | convolution fusion | flops 1623195392 | bytes 4469256 | tf_op jit(solution)/shard_map/while/body/eval_jaxpr/ib,jb->ij/dot_general | solution.py:22
  242.7 5.1 fusion.75
  247.8 1.8 subtract_multiply_fusion
  249.9 3.0 multiply_reduce_fusion.1
  252.9 0.5 copy-done.1
  253.4 14.9 %fusion.53 = (f32[256]{0:T(256)S(1)}, f32[256,4096]{1,0:T(8,128)}, f32[]{:T(128)}) fusion(f32[]{:T(128)} %mul.122, f32[]{:T(128)} %mul.121, f32[]{:T(128)} %sub.35, f32[]{:T(128)} %mul.120, f32[]{:T(128)} %mul.119, f32[256,256]{1,0:T(8,128)S(1)} %copy-done.2, f32[4096,256]{1,0:T(8,128)S(1)} %copy-done.1, f32[4096]{0:T(1024)S(1)} %multiply_reduce_fusion.1, ...), kind=kOutput, calls=%fused_computation.86 | convolution fusion | flops 3246391040 | bytes 8669208 | tf_op jit(solution)/shard_map/ib,jb->ij/dot_general | solution.py:22
  268.2 51.1 %all-reduce.8.cloned.1.call-done = f32[256,256]{1,0:T(8,128)} async-done(((f32[256,256]{1,0:T(8,128)}), f32[256,256]{1,0:T(8,128)}) %all-reduce.8.cloned.1.call-update) | async-done | bytes 262160 | tf_op jit(solution)/shard_map/psum | solution.py:84
  319.4 7.1 %fusion.30 = f32[256,256,1]{1,0,2:T(8,128)S(1)} fusion(f32[256,256]{1,0:T(8,128)} %all-reduce.8.cloned.1.call-done, f32[256,4096]{1,0:T(8,128)} %get-tuple-element.170, f32[4096,256]{1,0:T(8,128)} %all-gather.2.cloned.1.call-done, f32[256,256]{1,0:T(8,128)S(1)} %copy-done.2, f32[256]{0:T(256)S(1)} %get-tuple-element.169, f32[256]{0:T(256)S(1)} %copy-done.7), kind=kOutput, calls=%fused_computation.50 | convolution fusion | flops 3221553152 | bytes 9177088 | tf_op jit(solution)/shard_map/dot_general | solution.py:32
  326.5 18.6 %fusion.18 = f32[256,1,64]{2,1,0:T(1,128)S(1)} fusion(f32[256]{0:T(256)S(1)} %copy-done.13, f32[256,64]{1,0:T(8,128)S(1)} %copy-done.5, f32[256,256,1]{1,0,2:T(8,128)S(1)} %fusion.30), kind=kOutput, calls=%fused_computation.28 | convolution fusion | flops 71303168 | bytes 394240 | tf_op jit(solution)/shard_map/gtb,gb->gt/dot_general | solution.py:90
  345.2 0.9 convolution_bitcast_fusion
  346.8 126.1 %all-reduce.10.cloned.1.call-done = f32[256,64]{0,1:T(8,128)} async-done(((f32[256,64]{0,1:T(8,128)}), f32[256,64]{0,1:T(8,128)}) %all-reduce.10.cloned.1.call-update) | async-done | bytes 65552 | tf_op jit(solution)/shard_map/psum | solution.py:93
  472.9 1.5 multiply_reduce_fusion.4
  474.4 64.7 %psum.71 = f32[]{:T(128)} all-reduce(f32[]{:T(128)S(6)} %sub.39), channel_id=1, replica_groups=mesh['real'=8,'gen'=16] {'real','gen'}, use_global_device_ids=true, to_apply=%region_22.23 | all-reduce | flops 1 | bytes 8 | tf_op jit(solution)/shard_map/psum | solution.py:88
  539.1 18.0 %psum.70 = f32[]{:T(128)} all-reduce(f32[]{:T(128)} %multiply_reduce_fusion.4), channel_id=1, replica_groups=mesh['real'=8,'gen'=16] {'real'}, use_global_device_ids=true, to_apply=%region_20.21 | all-reduce | flops 1 | bytes 8 | tf_op jit(solution)/shard_map/psum | solution.py:94
  557.8 1.5 broadcast_divide_fusion.1
  (52 shorter events, 1.5 us)
Async XLA Ops:
  7.2 1.6 copy-start
  7.2 91.3 %all-reduce.6.cloned.1.call-start = ((), (), s32[]{:S(2)}) async-start(), calls=%async_computation | async-start | bytes 524288 | tf_op jit(solution)/shard_map/psum | solution.py:52
  7.2 13.7 %copy-start.12 = (f32[256]{0:T(256)}, f32[256]{0:T(256)S(1)}, u32[]{:S(2)}) copy-start(f32[256]{0:T(256)S(1)} %add_multiply_fusion) | copy-start | bytes 3076
  7.3 0.5 copy-start.10
  10.7 10.2 %copy-start.4 = (f32[256,64]{1,0:T(8,128)}, f32[256,64]{1,0:T(8,128)S(1)}, u32[]{:S(2)}) copy-start(f32[256,64]{1,0:T(8,128)S(1)} %copy.6) | copy-start | bytes 196612
  21.7 30.5 %copy-start.8 = (s32[256]{0:T(256)S(1)}, s32[256]{0:T(256)}, u32[]{:S(2)}) copy-start(s32[256]{0:T(256)} %param.8) | copy-start | bytes 3076
  21.7 228.2 %all-gather.2.cloned.1.call-start = ((), (), s32[]{:S(2)}) async-start(), calls=%async_computation.2 | async-start | bytes 4456448 | tf_op jit(solution)/shard_map/all_gather | solution.py:81
  52.2 84.6 %copy-start.6 = (f32[256]{0:T(256)}, f32[256]{0:T(256)S(1)}, u32[]{:S(2)}) copy-start(f32[256]{0:T(256)S(1)} %convert_element_type.4) | copy-start | bytes 3076
  136.8 182.6 %all-reduce.8.cloned.1.call-start = ((), (), s32[]{:S(2)}) async-start(), calls=%async_computation.1 | async-start | bytes 524288 | tf_op jit(solution)/shard_map/psum | solution.py:84
  247.8 5.1 copy-start.2
  249.7 223.2 %all-reduce.10.cloned.1.call-start = ((), (), s32[]{:S(2)}) async-start(), calls=%async_computation.3 | async-start | bytes 131072 | tf_op jit(solution)/shard_map/psum | solution.py:93
  249.9 3.5 copy-start.1
  253.4 66.0 %copy-start.7 = (f32[256]{0:T(256)S(1)}, f32[256]{0:T(256)}, u32[]{:S(2)}) copy-start(f32[256]{0:T(256)} %copy-done.6) | copy-start | bytes 3076
  319.3 7.1 %copy-start.5 = (f32[256,64]{1,0:T(8,128)S(1)}, f32[256,64]{1,0:T(8,128)}, u32[]{:S(2)}) copy-start(f32[256,64]{1,0:T(8,128)} %copy-done.4) | copy-start | bytes 196612
  319.4 7.1 %copy-start.13 = (f32[256]{0:T(256)S(1)}, f32[256]{0:T(256)}, u32[]{:S(2)}) copy-start(f32[256]{0:T(256)} %copy-done.12) | copy-start | bytes 3076
  326.5 18.7 %copy-start.3 = (f32[256,64]{0,1:T(8,128)S(1)}, f32[256,64]{0,1:T(8,128)}, u32[]{:S(2)}) copy-start(f32[256,64]{0,1:T(8,128)} %get-tuple-element.175) | copy-start | bytes 196612
  326.5 18.7 %copy-start.9 = (s32[256]{0:T(256)S(1)}, s32[256]{0:T(256)}, u32[]{:S(2)}) copy-start(s32[256]{0:T(256)} %param.8) | copy-start | bytes 3076
  326.5 18.7 %copy-start.11 = (s32[64]{0:T(128)S(1)}, s32[64]{0:T(128)}, u32[]{:S(2)}) copy-start(s32[64]{0:T(128)} %copy-done.10) | copy-start | bytes 772
Sparse Core Ops, SparseCore 0:
  21.8 76.6 all-reduce.5
  136.9 51.4 all-gather.1
  249.8 69.5 all-reduce.7
  346.3 126.5 all-reduce.9
where the time goes:
time: 567 us; the launch traced here: 566 us
  waiting for transfers between devices  223 us (39%)
  matrix products  144 us (25%)
  blocking collectives  138 us (24%)
  other arithmetic  35.9 us (6%)
  between operations  17.3 us (3%)
    psum x1, waiting for transfers between devices, per_device(): grad_weight = lax.psum(partial_grad, 'gen')  126 us
    psum x1, blocking collectives, per_device(): loss = lax.psum(loss_part, ('real', 'gen'))  64.7 us
    dot_general x9, matrix products, pair_terms(): inner_prod = jnp.einsum('ib,jb->ij', left, right, precision=highest)  64.5 us
    psum x1, waiting for transfers between devices, per_device(): grad_hist = lax.psum(cross_term, 'real') + pair_term  51.1 us
    dot_general x9, matrix products, pair_terms(): jnp.dot(weights, right, precision=highest)  47.9 us
    psum x1, waiting for transfers between devices, per_device(): counts = lax.psum(partial_counts, 'real')  45.7 us
    psum x1, blocking collectives, per_device(): gen_sq, gen_sum = lax.psum((gen_sq, gen_sum), 'gen')  33.8 us
    psum x1, blocking collectives, per_device(): real_sq, real_sum = lax.psum((real_sq, real_sum), 'real')  21.8 us
  transfers between devices with their start and end apart: 4, of which 3 were waited for; matrix products, arithmetic and copies ran while one was open for 24% of the time, Pallas kernels for 0%

commit v1 on v0

v1 whole, which is shorter than its diff:
```python
import functools
import math

import jax
import jax.numpy as jnp
from jax import lax
from jax.experimental import pallas as pl
from jax.experimental.pallas import tpu as pltpu
from jax.sharding import PartitionSpec as P

NUM_BINS = 256
SEQ_STEPS = 512
HID_WIDTH = 256
SPACING = 6.0 / NUM_BINS
LOG2E = math.log2(math.e)
UNIT = math.sqrt(LOG2E / 2.0) / SPACING
STEP = UNIT * SPACING
FAR = 1.0e6

highest = lax.Precision.HIGHEST
f32 = jnp.float32
bf16 = jnp.bfloat16
NT = (((1,), (1,)), ((), ()))
NN = (((1,), (0,)), ((), ()))
VMEM = pltpu.VMEM
SMEM = pltpu.SMEM


def params(limit=48 << 20):
    return pltpu.CompilerParams(vmem_limit_bytes=limit)


def whole(space=VMEM):
    return pl.BlockSpec(memory_space=space)


def split(x):
    hi = x.astype(bf16)
    return hi, (x - hi.astype(f32)).astype(bf16)


def dot(a, b, dims):
    return lax.dot_general(a, b, dims, preferred_element_type=f32)


def count_kernel(first_ref, wt_ref, hid_ref, len_ref, out_ref, val_ref, sig_ref):
    pre = lax.dot_general(
        wt_ref[...], hid_ref[...], NT, precision=highest, preferred_element_type=f32
    )
    small = jnp.exp(-jnp.abs(pre))
    steps = jnp.maximum(pre, 0.0) + jnp.log1p(small)
    at = first_ref[0] + lax.broadcasted_iota(jnp.int32, pre.shape, 0)
    lens = len_ref[...]
    val = jnp.where(at < lens, steps * UNIT, FAR)
    val_ref[...] = val
    sig = 1.0 / (1.0 + jnp.exp(-pre))
    sig_ref[...] = sig / (lens.astype(f32) * (UNIT * SPACING * SPACING))
    tall, wide = val.shape

    @pl.loop(0, NUM_BINS // 8)
    def _(i):
        base = (8 * i).astype(f32) + 0.5
        rows = []
        for j in range(8):
            off = (base + j) * STEP - val
            e = jnp.exp2(-(off * off))
            rows.append(jnp.sum(e, 0, keepdims=True))
        out_ref[pl.ds(pl.multiple_of(8 * i, 8), 8), :] = jnp.concatenate(rows, 0)


def count_steps(first, wt, hidden, lens):
    t, g = wt.shape[0], hidden.shape[0]
    return pl.pallas_call(
        count_kernel,
        out_shape=[
            jax.ShapeDtypeStruct((NUM_BINS, g), f32),
            jax.ShapeDtypeStruct((t, g), f32),
            jax.ShapeDtypeStruct((t, g), f32),
        ],
        in_specs=[whole(SMEM), whole(), whole(), whole()],
        out_specs=[whole(), whole(), whole()],
        compiler_params=params(),
    )(first, wt, hidden, lens)


def back_kernel(gh_ref, val_ref, sig_ref, hid_ref, out_ref):
    val = val_ref[...]

    def bins(i, acc):
        base = (8 * i).astype(f32) + 0.5
        rows = gh_ref[pl.ds(pl.multiple_of(8 * i, 8), 8), :]
        for j in range(8):
            off = (base + j) * STEP - val
            e = jnp.exp2(-(off * off))
            acc = acc + (e * off) * rows[j : j + 1, :]
        return acc

    slope = lax.fori_loop(0, NUM_BINS // 8, bins, jnp.zeros_like(val))
    out_ref[...] = lax.dot_general(
        slope * sig_ref[...], hid_ref[...], NN, precision=highest, preferred_element_type=f32
    )


def back_steps(gh, val, sig, hidden):
    return pl.pallas_call(
        back_kernel,
        out_shape=jax.ShapeDtypeStruct((val.shape[0], hidden.shape[1]), f32),
        in_specs=[whole()] * 4,
        out_specs=whole(),
        compiler_params=params(),
    )(gh, val, sig, hidden)


def stat_kernel(rows_ref, sum_ref, sq_ref):
    rows = rows_ref[...]
    hi, lo = split(rows * rows)
    ones = jnp.ones((8, rows.shape[1]), bf16)
    sq_ref[...] = dot(ones, hi, NT) + dot(ones, lo, NT)
    part = jnp.sum(rows.reshape(-1, 8, rows.shape[1]), 0)

    @pl.when(pl.program_id(0) == 0)
    def _():
        sum_ref[...] = part

    @pl.when(pl.program_id(0) > 0)
    def _():
        sum_ref[...] += part


def row_stats(rows, block):
    n, w = rows.shape
    block = min(block, n)
    return pl.pallas_call(
        stat_kernel,
        grid=(n // block,),
        out_shape=[
            jax.ShapeDtypeStruct((8, w), f32),
            jax.ShapeDtypeStruct((8, n), f32),
        ],
        in_specs=[pl.BlockSpec((block, w), lambda i: (i, 0))],
        out_specs=[
            pl.BlockSpec((8, w), lambda i: (0, 0)),
            pl.BlockSpec((8, block), lambda i: (0, i)),
        ],
        compiler_params=params(),
    )(rows)


def pair_kernel(
    cols, rate_ref, ht_ref, rows_ref, sq_ref, out_ref, ker_ref,
    hh_ref, hl_ref, hs_ref, ip_ref, wh_ref, wl_ref, mat_ref, sum_ref, kacc_ref,
):
    flows = ht_ref.shape[1]
    rate = rate_ref[0]

    @pl.when(pl.program_id(0) == 0)
    def _():
        h = ht_ref[...].T
        hh, hl = split(h * (2.0 * rate))
        hh_ref[...] = hh
        hl_ref[...] = hl
        hs_ref[...] = jnp.broadcast_to(
            jnp.sum(h * h, 1, keepdims=True) * rate, hs_ref.shape
        )
        mat_ref[...] = jnp.zeros_like(mat_ref)
        sum_ref[...] = jnp.zeros_like(sum_ref)
        kacc_ref[...] = jnp.zeros_like(kacc_ref)

    parts = rows_ref.shape[0] // cols
    kacc = kacc_ref[...]
    for p in range(parts):
        rh, rl = split(rows_ref[p * cols : (p + 1) * cols, :])
        hh = hh_ref[...]
        slot = p % 2
        ip_ref[slot] = dot(hh, rh, NT) + dot(hl_ref[...], rh, NT) + dot(hh, rl, NT)
        sq = sq_ref[0:1, p * cols : (p + 1) * cols] * rate
        for c in range(flows // 16):
            at = slice(16 * c, 16 * c + 16)
            x = ip_ref[slot, at, :] - sq - jnp.tile(hs_ref[at, :], (1, cols // 128))
            u = jnp.exp2(x)
            u2 = u * u
            u4 = u2 * u2
            u8 = u4 * u4
            u16 = u8 * u8
            w = u16 + u16 + u8
            w = w + w + u4
            w = w + w + u2
            w = w + w + u
            k = ((u16 + u8) + (u4 + u2)) + u
            wh = w.astype(bf16)
            wh_ref[slot, at, :] = wh
            wl_ref[slot, at, :] = (w - wh.astype(f32)).astype(bf16)
            ws = w[:, 0:128]
            ks = k[:, 0:128]
            for q in range(1, cols // 128):
                ws = ws + w[:, 128 * q : 128 * q + 128]
                ks = ks + k[:, 128 * q : 128 * q + 128]
            sum_ref[at, :] += ws
            kacc = kacc + ks
        wh = wh_ref[slot]
        mat_ref[...] += dot(wh, rh, NN) + dot(wl_ref[slot], rh, NN) + dot(wh, rl, NN)
    kacc_ref[...] = kacc

    @pl.when(pl.program_id(0) == pl.num_programs(0) - 1)
    def _():
        h = ht_ref[...].T
        total = jnp.sum(sum_ref[...], 1, keepdims=True)
        out_ref[...] = ((total * h - mat_ref[...]) * rate).T
        ker_ref[...] = kacc_ref[...]


def pair_sums(rate, ht, rows, sq, block, cols):
    n, w = rows.shape
    flows = ht.shape[1]
    block = min(block, n)
    return pl.pallas_call(
        functools.partial(pair_kernel, cols),
        grid=(n // block,),
        out_shape=[
            jax.ShapeDtypeStruct((w, flows), f32),
            jax.ShapeDtypeStruct((16, 128), f32),
        ],
        in_specs=[
            whole(SMEM),
            pl.BlockSpec((w, flows), lambda i: (0, 0)),
            pl.BlockSpec((block, w), lambda i: (i, 0)),
            pl.BlockSpec((8, block), lambda i: (0, i)),
        ],
        out_specs=[
            pl.BlockSpec((w, flows), lambda i: (0, 0)),
            pl.BlockSpec((16, 128), lambda i: (0, 0)),
        ],
        scratch_shapes=[
            VMEM((flows, w), bf16),
            VMEM((flows, w), bf16),
            VMEM((flows, 128), f32),
            VMEM((2, flows, cols), f32),
            VMEM((2, flows, cols), bf16),
            VMEM((2, flows, cols), bf16),
            VMEM((flows, w), f32),
            VMEM((flows, 128), f32),
            VMEM((16, 128), f32),
        ],
        compiler_params=params(),
        cost_estimate=pl.CostEstimate(
            flops=4 * n * w * flows * 3,
            bytes_accessed=4 * n * w,
            transcendentals=n * flows,
        ),
    )(rate, ht, rows, sq)


def swap_sum(x, axis, count):
    hop = 1
    while hop < count:
        x = x + lax.ppermute(x, axis, [(i, i ^ hop) for i in range(count)])
        hop *= 2
    return x


def block_sum(x, axis, count):
    parts = x.reshape(count, x.shape[0] // count, x.shape[1])
    own = jnp.sum(lax.all_to_all(parts, axis, 0, 0, tiled=True), 0)
    every = lax.all_to_all(
        jnp.broadcast_to(own[None], parts.shape), axis, 0, 0, tiled=True
    )
    return every.reshape(x.shape)


def per_device(real_count, gen_count, hidden, weight, lengths, real_rows):
    real_index = lax.axis_index("real")
    flows = hidden.shape[0]
    local_steps = weight.shape[1]
    total_flows = flows * gen_count
    total_real = real_rows.shape[0] * real_count
    lens = lengths[None, :]
    first = jnp.full((1,), real_index * local_steps, jnp.int32)
    part_counts, val, sig = count_steps(first, weight.T, hidden, lens)
    real_sum, real_sq = row_stats(real_rows, 2048)
    real_vec = jnp.concatenate(
        [jnp.sum(real_sum, 0), jnp.full((128,), jnp.sum(real_sq[0]))]
    )[None, :]
    counts = block_sum(part_counts, "real", real_count)
    real_vec = swap_sum(real_vec, "real", real_count)
    hist_t = counts / lens.astype(f32)
    gen_vec = jnp.concatenate(
        [jnp.sum(hist_t, 1), jnp.full((128,), jnp.sum(hist_t * hist_t))]
    )[None, :]
    gen_vec = swap_sum(gen_vec, "gen", gen_count)
    spread = (
        gen_vec[0, NUM_BINS] / total_flows
        + real_vec[0, NUM_BINS] / total_real
        - 2.0
        * jnp.sum(
            (gen_vec[0, :NUM_BINS] / total_flows) * (real_vec[0, :NUM_BINS] / total_real)
        )
    )
    share = flows // real_count
    own = lax.dynamic_slice_in_dim(hist_t, real_index * share, share, 1).T
    others = lax.all_gather(own, "gen", axis=0, tiled=True)
    rate = (LOG2E / (4.0 * spread)).reshape(1)
    cross_g, cross_k = pair_sums(rate, hist_t, real_rows, real_sq, 1024, 256)
    _, other_sq = row_stats(others, 512)
    pair_g, pair_k = pair_sums(rate, hist_t, others, other_sq, 512, 256)
    grad_part = (cross_g * (4.0 / total_real) - pair_g * (4.0 / total_flows)) * (1.0 / LOG2E)
    loss_part = jnp.sum(pair_k) / (total_flows * total_flows) - 2.0 * jnp.sum(
        cross_k
    ) / (total_flows * total_real)
    grad_hist = block_sum(grad_part, "real", real_count)
    part = back_steps(grad_hist, val, sig, hidden)
    grad_weight = swap_sum(part, "gen", gen_count)
    loss_vec = swap_sum(jnp.full((1, 128), loss_part), "gen", gen_count)
    tail = jnp.concatenate(
        [jnp.full((1, 128), jnp.sum(grad_weight * grad_weight)), loss_vec], 1
    )
    tail = swap_sum(tail, "real", real_count)
    mean_sq = tail[0, 0] / (HID_WIDTH * SEQ_STEPS)
    update = grad_weight / jnp.sqrt(mean_sq + 1e-06)
    return (update.T, tail[0, 128])


def solution(mesh):
    in_specs = (P("gen", None), P(None, "real"), P("gen"), P("real", None))
    out_specs = (P(None, "real"), P())
    body = functools.partial(per_device, mesh.shape["real"], mesh.shape["gen"])
    return jax.shard_map(
        body, mesh=mesh, in_specs=in_specs, out_specs=out_specs, check_vma=False
    )
```

time: 567 us -> 181 us (0.32)
  waiting for transfers between devices: 223 us -> 28.6 us
  matrix products: 144 us -> 0 us
  blocking collectives: 138 us -> 46.2 us
  Pallas kernels: 0 us -> 50.7 us
  starting transfers between devices: 0.34 us -> 37 us
  other arithmetic: 35.9 us -> 5.44 us
  between operations: 17.3 us -> 4.89 us
    psum x3 -> x0, waiting for transfers between devices: 223 us -> none  [the longest x1 126 us: per_device(): grad_weight = lax.psum(partial_grad, 'gen')]
    dot_general x22 -> x0, matrix products: 144 us -> none  [the longest x9 64.5 us: pair_terms(): inner_prod = jnp.einsum('ib,jb->ij', left, right, precision=highest)]
    psum x4 -> x0, blocking collectives: 138 us -> none  [the longest x1 64.7 us: per_device(): loss = lax.psum(loss_part, ('real', 'gen'))]
    pallas_call x0 -> x6, Pallas kernels: none -> 50.7 us  [the longest x2 30.5 us: pair_sums(): pl.pallas_call(functools.partial(pair_kernel, cols), grid=(n // block,),...]
    ppermute x0 -> x18, waiting for transfers between devices: none -> 28.6 us  [swap_sum(): x = x + lax.ppermute(x, axis, [(i, i ^ hop) for i in range(count)])]
    reduce_sum x12 -> x9, other arithmetic: 31 us -> 3.9 us  [the longest x1 0.73 us: per_device(): jnp.sum(real_sq[0])]
    ppermute x0 -> x18, starting transfers between devices: none -> 24.9 us  [swap_sum(): x = x + lax.ppermute(x, axis, [(i, i ^ hop) for i in range(count)])]
    all_gather x0 -> x1, blocking collectives: none -> 23.8 us  [per_device(): others = lax.all_gather(own, 'gen', axis=0, tiled=True)]
  transfers between devices with their start and end apart: 4 -> 20, of which waited for: 3 -> 14; matrix products, arithmetic and copies ran while one was open for 24% -> 3% of each run, Pallas kernels for 0% -> 6%
where the time goes in v1:
time: 181 us; the launch traced here: 180 us
  Pallas kernels  50.7 us (28%)
  blocking collectives  46.2 us (26%)
  starting transfers between devices  37 us (20%)
  waiting for transfers between devices  28.6 us (16%)
  local copies, waits for them, and re-layouts  7.05 us (4%)
  other arithmetic  5.44 us (3%)
  between operations  4.89 us (3%)
    pallas_call x2, Pallas kernels, pair_sums(): pl.pallas_call(functools.partial(pair_kernel, cols), grid=(n // block,),...  30.5 us
    ppermute x18, waiting for transfers between devices, swap_sum(): x = x + lax.ppermute(x, axis, [(i, i ^ hop) for i in range(count)])  28.6 us
    ppermute x18, starting transfers between devices, swap_sum(): x = x + lax.ppermute(x, axis, [(i, i ^ hop) for i in range(count)])  24.9 us
    all_gather x1, blocking collectives, per_device(): others = lax.all_gather(own, 'gen', axis=0, tiled=True)  23.8 us
    all_to_all x1, blocking collectives, block_sum(): own = jnp.sum(lax.all_to_all(parts, axis, 0, 0, tiled=True), 0)  12.4 us
    pallas_call x2, Pallas kernels, row_stats(): pl.pallas_call(stat_kernel, grid=(n // block,), out_shape=[jax.ShapeDtype...  11.2 us
    all_to_all x1, blocking collectives, block_sum(): lax.all_to_all(jnp.broadcast_to(own[None], parts.shape), axis, 0, 0, tile...  9.94 us
    all_to_all x1, starting transfers between devices, block_sum(): own = jnp.sum(lax.all_to_all(parts, axis, 0, 0, tiled=True), 0)  6.41 us
  transfers between devices with their start and end apart: 20, of which 14 were waited for; matrix products, arithmetic and copies ran while one was open for 3% of the time, Pallas kernels for 6%

profile of v1, /device:TPU:0, one launch (start us, length us, event | category | flops | bytes accessed | tf_op | source)
XLA Modules:
  0.0 179.9 jit_solution(12659893171224393344)
XLA Ops:
  0.7 0.9 copy-done
  1.6 0.8 copy-done.2
  2.4 0.7 copy-done.3
  3.1 4.7 %shard_map.59 = (f32[256,256]{1,0:T(8,128)}, f32[64,256]{1,0:T(8,128)S(1)}, f32[64,256]{1,0:T(8,128)S(1)}) custom-call(s32[1]{0:T(128)} %bitcast.first_ref, f32[64,256]{1,0:T(8,128)S(1)} %bitcast.16, f32[256,256]{1,0:T(8,128)S(1)} %copy-done, s32[1,256]{1,0:T(1,128)S(1)} %bitcast.17), custom_call_target="tpu_custom_call" | custom-call | tf_op jit(solution)/shard_map/pallas_call | solution.py:73
  7.8 6.4 %all-to-all-start = ((f32[8,32,256]{2,1,0:T(8,128)}), f32[8,32,256]{2,1,0:T(8,128)S(1)}, u32[]{:S(2)}, u32[]{:S(2)}) async-start(f32[8,32,256]{2,1,0:T(8,128)} %bitcast.3), calls=%async_computation | async-start | bytes 524288 | tf_op jit(solution)/shard_map/all_to_all | solution.py:263
  14.2 10.4 %shard_map.60 = (f32[8,256]{1,0:T(8,128)S(1)}, f32[8,16384]{1,0:T(8,128)S(1)}) custom-call(f32[16384,256]{1,0:T(8,128)} %rows_ref.3), custom_call_target="tpu_custom_call" | custom-call | tf_op jit(solution)/shard_map/pallas_call | solution.py:133
  24.7 0.7 broadcast_in_dim.32
  25.4 5.7 %all-to-all-start.1 = ((f32[8,32,256]{2,1,0:T(8,128)}), f32[8,32,256]{2,1,0:T(8,128)S(1)}, u32[]{:S(2)}, u32[]{:S(2)}) async-start(f32[8,32,256]{2,1,0:T(8,128)} %broadcast_in_dim.32), calls=%async_computation.1 | async-start | bytes 524288 | tf_op jit(solution)/shard_map/all_to_all | solution.py:264
  31.1 0.7 slice_reduce_fusion
  31.9 0.6 concatenate.10
  32.5 2.1 %collective-permute-start.4 = (f32[1,384]{1,0:T(1,128)S(1)}, f32[1,384]{1,0:T(1,128)S(1)}, u32[]{:S(2)}, u32[]{:S(2)}) collective-permute-start(f32[1,384]{1,0:T(1,128)S(1)} %broadcast_in_dim.34), channel_id=1, source_target_pairs={{0,16},{16,0},{32,48},{48,32},{64,80},{80,64},{96,112},{112,96},{1... | collective-permute-start | bytes 4616 | tf_op jit(solution)/shard_map/ppermute | solution.py:256
  34.6 1.7 collective-permute-done.4
  36.3 3.4 %collective-permute-start.5 = (f32[1,384]{1,0:T(1,128)S(1)}, f32[1,384]{1,0:T(1,128)S(1)}, u32[]{:S(2)}, u32[]{:S(2)}) collective-permute-start(f32[1,384]{1,0:T(1,128)S(1)} %reshape_add_fusion), channel_id=1, source_target_pairs={{0,32},{16,48},{32,0},{48,16},{64,96},{80,112},{96,64},{112,80},{1... | collective-permute-start | bytes 4616 | tf_op jit(solution)/shard_map/ppermute | solution.py:256
  39.7 1.7 collective-permute-done.5
  41.4 1.9 %collective-permute-start.6 = (f32[1,384]{1,0:T(1,128)S(1)}, f32[1,384]{1,0:T(1,128)S(1)}, u32[]{:S(2)}, u32[]{:S(2)}) collective-permute-start(f32[1,384]{1,0:T(1,128)S(1)} %add.78), channel_id=1, source_target_pairs={{0,64},{16,80},{32,96},{48,112},{64,0},{80,16},{96,32},{112,48},{1... | collective-permute-start | bytes 4616 | tf_op jit(solution)/shard_map/ppermute | solution.py:256
  43.3 0.7 multiply_reduce_fusion
  44.1 0.6 concatenate.9
  46.3 3.0 %collective-permute-start.1 = (f32[1,384]{1,0:T(1,128)S(1)}, f32[1,384]{1,0:T(1,128)S(1)}, u32[]{:S(2)}, u32[]{:S(2)}) collective-permute-start(f32[1,384]{1,0:T(1,128)S(1)} %reshape_add_fusion.1), channel_id=1, source_target_pairs={{0,2},{1,3},{2,0},{3,1},{4,6},{5,7},{6,4},{7,5},{8,10},{9,11},{10,... | collective-permute-start | bytes 4616 | tf_op jit(solution)/shard_map/ppermute | solution.py:256
  49.4 2.1 %collective-permute-done.1 = f32[1,384]{1,0:T(1,128)S(1)} collective-permute-done((f32[1,384]{1,0:T(1,128)S(1)}, f32[1,384]{1,0:T(1,128)S(1)}, u32[]{:S(2)}, u32[]{:S(2)}) %collective-permute-start.1) | collective-permute-done | bytes 1568 | tf_op jit(solution)/shard_map/ppermute | solution.py:256
  51.5 1.5 collective-permute-start.2
  53.0 2.1 %collective-permute-done.2 = f32[1,384]{1,0:T(1,128)S(1)} collective-permute-done((f32[1,384]{1,0:T(1,128)S(1)}, f32[1,384]{1,0:T(1,128)S(1)}, u32[]{:S(2)}, u32[]{:S(2)}) %collective-permute-start.2) | collective-permute-done | bytes 1568 | tf_op jit(solution)/shard_map/ppermute | solution.py:256
  55.1 3.0 %collective-permute-start.3 = (f32[1,384]{1,0:T(1,128)S(1)}, f32[1,384]{1,0:T(1,128)S(1)}, u32[]{:S(2)}, u32[]{:S(2)}) collective-permute-start(f32[1,384]{1,0:T(1,128)S(1)} %add.75), channel_id=1, source_target_pairs={{0,8},{1,9},{2,10},{3,11},{4,12},{5,13},{6,14},{7,15},{8,0},{9,1},... | collective-permute-start | bytes 4616 | tf_op jit(solution)/shard_map/ppermute | solution.py:256
  58.1 23.8 %all_gather.3.rows_ref = f32[512,256]{1,0:T(8,128)S(1)} all-gather(f32[32,256]{1,0:T(8,128)S(1)} %dynamic-slice_bitcast_fusion), channel_id=1, replica_groups=mesh['real'=8,'gen'=16] {'gen'}, dimensions={0}, use_global_device_ids=true | all-gather | bytes 557056 | tf_op jit(solution)/shard_map/all_gather | solution.py:300
  82.1 0.7 shard_map.62
  82.8 0.6 fusion.2
  85.3 29.2 %shard_map.61 = (f32[256,256]{1,0:T(8,128)S(1)}, f32[16,128]{1,0:T(8,128)S(1)}) custom-call(f32[1]{0:T(128)} %bitcast.5.rate_ref, f32[256,256]{1,0:T(8,128)S(1)} %copy.12.ht_ref, f32[16384,256]{1,0:T(8,128)} %rows_ref.3, f32[8,16384]{1,0:T(8,128)S(1)} %get-tuple-element.14.sq_ref), custom_call_target="tpu_custom_call" | custom-call | flops 12884901888 | bytes 16777216 | tf_op jit(solution)/shard_map/pallas_call | solution.py:216
  114.5 1.3 shard_map.63
  115.9 12.4 %all_to_all.20 = f32[8,32,256]{2,1,0:T(8,128)S(1)} all-to-all(f32[8,32,256]{2,1,0:T(8,128)S(1)} %bitcast.19), channel_id=1, replica_groups=mesh['real'=8,'gen'=16] {'real'}, dimensions={0} | all-to-all | bytes 524288 | tf_op jit(solution)/shard_map/all_to_all | solution.py:263
  128.4 9.9 %all_to_all.21 = f32[8,32,256]{2,1,0:T(8,128)S(1)} all-to-all(f32[8,32,256]{2,1,0:T(8,128)S(1)} %broadcast_in_dim.35), channel_id=1, replica_groups=mesh['real'=8,'gen'=16] {'real'}, dimensions={0} | all-to-all | bytes 524288 | tf_op jit(solution)/shard_map/all_to_all | solution.py:264
  138.3 4.4 %shard_map.64 = f32[64,256]{1,0:T(8,128)S(1)} custom-call(f32[256,256]{1,0:T(8,128)S(1)} %bitcast.15, f32[64,256]{1,0:T(8,128)S(1)} %get-tuple-element.18.val_ref, f32[64,256]{1,0:T(8,128)S(1)} %get-tuple-element.19.sig_ref, f32[256,256]{1,0:T(8,128)S(1)} %copy-done.1), custom_call_target="tpu_custom_call" | custom-call | tf_op jit(solution)/shard_map/pallas_call | solution.py:105
  142.8 1.2 collective-permute-done.7
  144.0 1.3 collective-permute-start.8
  148.0 1.9 %collective-permute-done.8 = f32[64,256]{1,0:T(8,128)S(1)} collective-permute-done((f32[64,256]{1,0:T(8,128)S(1)}, f32[64,256]{1,0:T(8,128)S(1)}, u32[]{:S(2)}, u32[]{:S(2)}) %collective-permute-start.8) | collective-permute-done | bytes 65568 | tf_op jit(solution)/shard_map/ppermute | solution.py:256
  150.0 1.3 collective-permute-start.12
  151.3 3.3 %collective-permute-done.9 = f32[64,256]{1,0:T(8,128)S(1)} collective-permute-done((f32[64,256]{1,0:T(8,128)S(1)}, f32[64,256]{1,0:T(8,128)S(1)}, u32[]{:S(2)}, u32[]{:S(2)}) %collective-permute-start.9) | collective-permute-done | bytes 65568 | tf_op jit(solution)/shard_map/ppermute | solution.py:256
  155.1 1.9 %collective-permute-start.13 = (f32[1,128]{1,0:T(1,128)S(1)}, f32[1,128]{1,0:T(1,128)S(1)}, u32[]{:S(2)}, u32[]{:S(2)}) collective-permute-start(f32[1,128]{1,0:T(1,128)S(1)} %fusion.4), channel_id=1, source_target_pairs={{0,4},{1,5},{2,6},{3,7},{4,0},{5,1},{6,2},{7,3},{8,12},{9,13},{10,... | collective-permute-start | bytes 1544 | tf_op jit(solution)/shard_map/ppermute | solution.py:256
  157.0 1.6 collective-permute-done.13
  158.7 3.1 %collective-permute-start.14 = (f32[1,128]{1,0:T(1,128)S(1)}, f32[1,128]{1,0:T(1,128)S(1)}, u32[]{:S(2)}, u32[]{:S(2)}) collective-permute-start(f32[1,128]{1,0:T(1,128)S(1)} %add.89), channel_id=1, source_target_pairs={{0,8},{1,9},{2,10},{3,11},{4,12},{5,13},{6,14},{7,15},{8,0},{9,1},... | collective-permute-start | bytes 1544 | tf_op jit(solution)/shard_map/ppermute | solution.py:256
  161.8 1.9 %collective-permute-done.14 = f32[1,128]{1,0:T(1,128)S(1)} collective-permute-done((f32[1,128]{1,0:T(1,128)S(1)}, f32[1,128]{1,0:T(1,128)S(1)}, u32[]{:S(2)}, u32[]{:S(2)}) %collective-permute-start.14) | collective-permute-done | bytes 544 | tf_op jit(solution)/shard_map/ppermute | solution.py:256
  163.7 0.6 multiply_reduce_fusion.1
  164.3 0.6 concatenate.11
  165.3 3.4 %collective-permute-done.15 = f32[1,256]{1,0:T(1,128)S(1)} collective-permute-done((f32[1,256]{1,0:T(1,128)S(1)}, f32[1,256]{1,0:T(1,128)S(1)}, u32[]{:S(2)}, u32[]{:S(2)}) %collective-permute-start.15) | collective-permute-done | bytes 1056 | tf_op jit(solution)/shard_map/ppermute | solution.py:256
  168.6 0.6 pad_add_fusion
  169.3 1.0 collective-permute-start.16
  170.3 4.2 %collective-permute-done.16 = f32[1,256]{1,0:T(1,128)S(1)} collective-permute-done((f32[1,256]{1,0:T(1,128)S(1)}, f32[1,256]{1,0:T(1,128)S(1)}, u32[]{:S(2)}, u32[]{:S(2)}) %collective-permute-start.16) | collective-permute-done | bytes 1056 | tf_op jit(solution)/shard_map/ppermute | solution.py:256
  174.4 0.6 collective-permute-start.17
  175.1 2.9 %collective-permute-done.17 = f32[1,256]{1,0:T(1,128)S(1)} collective-permute-done((f32[1,256]{1,0:T(1,128)S(1)}, f32[1,256]{1,0:T(1,128)S(1)}, u32[]{:S(2)}, u32[]{:S(2)}) %collective-permute-start.17) | collective-permute-done | bytes 1056 | tf_op jit(solution)/shard_map/ppermute | solution.py:256
  179.2 0.6 divide_bitcast_fusion
  (56 shorter events, 4.8 us)
Async XLA Ops:
  0.6 39.1 %copy-start.4 = (s32[256]{0:T(256)S(1)}, s32[256]{0:T(256)}, u32[]{:S(2)}) copy-start(s32[256]{0:T(256)} %param.6) | copy-start | bytes 3076
  0.6 1.0 copy-start
  1.6 0.8 copy-start.2
  2.4 0.7 copy-start.3
  7.8 16.9 %all-to-all-start = ((f32[8,32,256]{2,1,0:T(8,128)}), f32[8,32,256]{2,1,0:T(8,128)S(1)}, u32[]{:S(2)}, u32[]{:S(2)}) async-start(f32[8,32,256]{2,1,0:T(8,128)} %bitcast.3), calls=%async_computation | async-start | bytes 524288 | tf_op jit(solution)/shard_map/all_to_all | solution.py:263
  25.4 17.9 %all-to-all-start.1 = ((f32[8,32,256]{2,1,0:T(8,128)}), f32[8,32,256]{2,1,0:T(8,128)S(1)}, u32[]{:S(2)}, u32[]{:S(2)}) async-start(f32[8,32,256]{2,1,0:T(8,128)} %broadcast_in_dim.32), calls=%async_computation.1 | async-start | bytes 524288 | tf_op jit(solution)/shard_map/all_to_all | solution.py:264
  32.5 3.8 %collective-permute-start.4 = (f32[1,384]{1,0:T(1,128)S(1)}, f32[1,384]{1,0:T(1,128)S(1)}, u32[]{:S(2)}, u32[]{:S(2)}) collective-permute-start(f32[1,384]{1,0:T(1,128)S(1)} %broadcast_in_dim.34), channel_id=1, source_target_pairs={{0,16},{16,0},{32,48},{48,32},{64,80},{80,64},{96,112},{112,96},{1... | collective-permute-start | bytes 4616 | tf_op jit(solution)/shard_map/ppermute | solution.py:256
  36.3 5.1 %collective-permute-start.5 = (f32[1,384]{1,0:T(1,128)S(1)}, f32[1,384]{1,0:T(1,128)S(1)}, u32[]{:S(2)}, u32[]{:S(2)}) collective-permute-start(f32[1,384]{1,0:T(1,128)S(1)} %reshape_add_fusion), channel_id=1, source_target_pairs={{0,32},{16,48},{32,0},{48,16},{64,96},{80,112},{96,64},{112,80},{1... | collective-permute-start | bytes 4616 | tf_op jit(solution)/shard_map/ppermute | solution.py:256
  41.4 3.6 %collective-permute-start.6 = (f32[1,384]{1,0:T(1,128)S(1)}, f32[1,384]{1,0:T(1,128)S(1)}, u32[]{:S(2)}, u32[]{:S(2)}) collective-permute-start(f32[1,384]{1,0:T(1,128)S(1)} %add.78), channel_id=1, source_target_pairs={{0,64},{16,80},{32,96},{48,112},{64,0},{80,16},{96,32},{112,48},{1... | collective-permute-start | bytes 4616 | tf_op jit(solution)/shard_map/ppermute | solution.py:256
  44.7 1.6 collective-permute-start
  46.3 5.2 %collective-permute-start.1 = (f32[1,384]{1,0:T(1,128)S(1)}, f32[1,384]{1,0:T(1,128)S(1)}, u32[]{:S(2)}, u32[]{:S(2)}) collective-permute-start(f32[1,384]{1,0:T(1,128)S(1)} %reshape_add_fusion.1), channel_id=1, source_target_pairs={{0,2},{1,3},{2,0},{3,1},{4,6},{5,7},{6,4},{7,5},{8,10},{9,11},{10,... | collective-permute-start | bytes 4616 | tf_op jit(solution)/shard_map/ppermute | solution.py:256
  51.5 3.6 %collective-permute-start.2 = (f32[1,384]{1,0:T(1,128)S(1)}, f32[1,384]{1,0:T(1,128)S(1)}, u32[]{:S(2)}, u32[]{:S(2)}) collective-permute-start(f32[1,384]{1,0:T(1,128)S(1)} %add.74), channel_id=1, source_target_pairs={{0,4},{1,5},{2,6},{3,7},{4,0},{5,1},{6,2},{7,3},{8,12},{9,13},{10,... | collective-permute-start | bytes 4616 | tf_op jit(solution)/shard_map/ppermute | solution.py:256
  55.1 27.7 %collective-permute-start.3 = (f32[1,384]{1,0:T(1,128)S(1)}, f32[1,384]{1,0:T(1,128)S(1)}, u32[]{:S(2)}, u32[]{:S(2)}) collective-permute-start(f32[1,384]{1,0:T(1,128)S(1)} %add.75), channel_id=1, source_target_pairs={{0,8},{1,9},{2,10},{3,11},{4,12},{5,13},{6,14},{7,15},{8,0},{9,1},... | collective-permute-start | bytes 4616 | tf_op jit(solution)/shard_map/ppermute | solution.py:256
  85.3 53.0 %copy-start.1 = (f32[256,256]{1,0:T(8,128)S(1)}, f32[256,256]{1,0:T(8,128)}, u32[]{:S(2)}) copy-start(f32[256,256]{1,0:T(8,128)} %hid_ref.3) | copy-start | bytes 786436
  142.7 1.3 collective-permute-start.7
  144.0 5.8 %collective-permute-start.8 = (f32[64,256]{1,0:T(8,128)S(1)}, f32[64,256]{1,0:T(8,128)S(1)}, u32[]{:S(2)}, u32[]{:S(2)}) collective-permute-start(f32[64,256]{1,0:T(8,128)S(1)} %add.83), channel_id=1, source_target_pairs={{0,2},{1,3},{2,0},{3,1},{4,6},{5,7},{6,4},{7,5},{8,10},{9,11},{10,... | collective-permute-start | bytes 196616 | tf_op jit(solution)/shard_map/ppermute | solution.py:256
  147.9 2.1 %collective-permute-start.11 = (f32[1,128]{1,0:T(1,128)S(1)}, f32[1,128]{1,0:T(1,128)S(1)}, u32[]{:S(2)}, u32[]{:S(2)}) collective-permute-start(f32[1,128]{1,0:T(1,128)S(1)} %broadcast_in_dim.36), channel_id=1, source_target_pairs={{0,1},{1,0},{2,3},{3,2},{4,5},{5,4},{6,7},{7,6},{8,9},{9,8},{10,11... | collective-permute-start | bytes 1544 | tf_op jit(solution)/shard_map/ppermute | solution.py:256
  149.9 4.8 %collective-permute-start.9 = (f32[64,256]{1,0:T(8,128)S(1)}, f32[64,256]{1,0:T(8,128)S(1)}, u32[]{:S(2)}, u32[]{:S(2)}) collective-permute-start(f32[64,256]{1,0:T(8,128)S(1)} %add.84), channel_id=1, source_target_pairs={{0,4},{1,5},{2,6},{3,7},{4,0},{5,1},{6,2},{7,3},{8,12},{9,13},{10,... | collective-permute-start | bytes 196616 | tf_op jit(solution)/shard_map/ppermute | solution.py:256
  150.0 5.1 %collective-permute-start.12 = (f32[1,128]{1,0:T(1,128)S(1)}, f32[1,128]{1,0:T(1,128)S(1)}, u32[]{:S(2)}, u32[]{:S(2)}) collective-permute-start(f32[1,128]{1,0:T(1,128)S(1)} %broadcast_add_fusion), channel_id=1, source_target_pairs={{0,2},{1,3},{2,0},{3,1},{4,6},{5,7},{6,4},{7,5},{8,10},{9,11},{10,... | collective-permute-start | bytes 1544 | tf_op jit(solution)/shard_map/ppermute | solution.py:256
  154.6 9.1 %collective-permute-start.10 = (f32[64,256]{1,0:T(8,128)S(1)}, f32[64,256]{1,0:T(8,128)S(1)}, u32[]{:S(2)}, u32[]{:S(2)}) collective-permute-start(f32[64,256]{1,0:T(8,128)S(1)} %add.85), channel_id=1, source_target_pairs={{0,8},{1,9},{2,10},{3,11},{4,12},{5,13},{6,14},{7,15},{8,0},{9,1},... | collective-permute-start | bytes 196616 | tf_op jit(solution)/shard_map/ppermute | solution.py:256
  155.1 3.5 %collective-permute-start.13 = (f32[1,128]{1,0:T(1,128)S(1)}, f32[1,128]{1,0:T(1,128)S(1)}, u32[]{:S(2)}, u32[]{:S(2)}) collective-permute-start(f32[1,128]{1,0:T(1,128)S(1)} %fusion.4), channel_id=1, source_target_pairs={{0,4},{1,5},{2,6},{3,7},{4,0},{5,1},{6,2},{7,3},{8,12},{9,13},{10,... | collective-permute-start | bytes 1544 | tf_op jit(solution)/shard_map/ppermute | solution.py:256
  158.7 5.0 %collective-permute-start.14 = (f32[1,128]{1,0:T(1,128)S(1)}, f32[1,128]{1,0:T(1,128)S(1)}, u32[]{:S(2)}, u32[]{:S(2)}) collective-permute-start(f32[1,128]{1,0:T(1,128)S(1)} %add.89), channel_id=1, source_target_pairs={{0,8},{1,9},{2,10},{3,11},{4,12},{5,13},{6,14},{7,15},{8,0},{9,1},... | collective-permute-start | bytes 1544 | tf_op jit(solution)/shard_map/ppermute | solution.py:256
  165.0 3.6 %collective-permute-start.15 = (f32[1,256]{1,0:T(1,128)S(1)}, f32[1,256]{1,0:T(1,128)S(1)}, u32[]{:S(2)}, u32[]{:S(2)}) collective-permute-start(f32[1,256]{1,0:T(1,128)S(1)} %concatenate.11), channel_id=1, source_target_pairs={{0,16},{16,0},{32,48},{48,32},{64,80},{80,64},{96,112},{112,96},{1... | collective-permute-start | bytes 3080 | tf_op jit(solution)/shard_map/ppermute | solution.py:256
  169.3 5.2 %collective-permute-start.16 = (f32[1,256]{1,0:T(1,128)S(1)}, f32[1,256]{1,0:T(1,128)S(1)}, u32[]{:S(2)}, u32[]{:S(2)}) collective-permute-start(f32[1,256]{1,0:T(1,128)S(1)} %pad_add_fusion), channel_id=1, source_target_pairs={{0,32},{16,48},{32,0},{48,16},{64,96},{80,112},{96,64},{112,80},{1... | collective-permute-start | bytes 3080 | tf_op jit(solution)/shard_map/ppermute | solution.py:256
  174.4 3.6 %collective-permute-start.17 = (f32[1,256]{1,0:T(1,128)S(1)}, f32[1,256]{1,0:T(1,128)S(1)}, u32[]{:S(2)}, u32[]{:S(2)}) collective-permute-start(f32[1,256]{1,0:T(1,128)S(1)} %add.92), channel_id=1, source_target_pairs={{0,64},{16,80},{32,96},{48,112},{64,0},{80,16},{96,32},{112,48},{1... | collective-permute-start | bytes 3080 | tf_op jit(solution)/shard_map/ppermute | solution.py:256

commit v2 on v1

v2 whole, which is shorter than its diff:
```python
import functools
import math

import jax
import jax.numpy as jnp
from jax import lax
from jax.experimental import pallas as pl
from jax.experimental.pallas import tpu as pltpu
from jax.sharding import PartitionSpec as P

NUM_BINS = 256
SEQ_STEPS = 512
HID_WIDTH = 256
SPACING = 6.0 / NUM_BINS
LOG2E = math.log2(math.e)
UNIT = math.sqrt(LOG2E / 2.0) / SPACING
STEP = UNIT * SPACING
FAR = 1.0e6
EXTRA = 8

highest = lax.Precision.HIGHEST
f32 = jnp.float32
bf16 = jnp.bfloat16
NT = (((1,), (1,)), ((), ()))
NN = (((1,), (0,)), ((), ()))
VMEM = pltpu.VMEM
SMEM = pltpu.SMEM


def params(limit=48 << 20):
    return pltpu.CompilerParams(vmem_limit_bytes=limit)


def fixed(shape):
    return pl.BlockSpec(shape, lambda i: (0,) * len(shape))


def call_once(kernel, outs, *args, scalars=0):
    return pl.pallas_call(
        kernel,
        grid=(1,),
        out_shape=[jax.ShapeDtypeStruct(s, f32) for s in outs],
        in_specs=[
            pl.BlockSpec(memory_space=SMEM) if i < scalars else fixed(a.shape)
            for i, a in enumerate(args)
        ],
        out_specs=[fixed(s) for s in outs],
        compiler_params=params(),
    )(*args)


def split(x):
    hi = x.astype(bf16)
    return hi, (x - hi.astype(f32)).astype(bf16)


def dot(a, b, dims):
    return lax.dot_general(a, b, dims, preferred_element_type=f32)


def count_kernel(first_ref, wt_ref, hid_ref, len_ref, out_ref, val_ref, sig_ref):
    pre = lax.dot_general(
        wt_ref[...], hid_ref[...], NT, precision=highest, preferred_element_type=f32
    )
    small = jnp.exp(-jnp.abs(pre))
    steps = jnp.maximum(pre, 0.0) + jnp.log1p(small)
    at = first_ref[0] + lax.broadcasted_iota(jnp.int32, pre.shape, 0)
    lens = len_ref[...]
    val = jnp.where(at < lens, steps * UNIT, FAR)
    val_ref[...] = val
    sig = 1.0 / (1.0 + jnp.exp(-pre))
    sig_ref[...] = sig / (lens.astype(f32) * (UNIT * SPACING * SPACING))

    def bins(i, carry):
        base = (8 * i).astype(f32) + 0.5
        rows = []
        for j in range(8):
            off = (base + j) * STEP - val
            e = jnp.exp2(-(off * off))
            rows.append(jnp.sum(e, 0, keepdims=True))
        out_ref[pl.ds(pl.multiple_of(8 * i, 8), 8), :] = jnp.concatenate(rows, 0)
        return carry

    lax.fori_loop(0, NUM_BINS // 8, bins, 0)
    out_ref[...] = out_ref[...].T


def back_kernel(gh_ref, val_ref, sig_ref, hid_ref, out_ref, ght_ref):
    parts, share = gh_ref.shape[0], gh_ref.shape[1] - EXTRA
    tall = val_ref.shape[0]
    gh = jnp.concatenate([gh_ref[p, :share, :] for p in range(parts)], 0)
    ght_ref[...] = gh.T
    val = val_ref[...]

    def bins(i, acc):
        base = (8 * i).astype(f32) + 0.5
        rows = ght_ref[pl.ds(pl.multiple_of(8 * i, 8), 8), :]
        for j in range(8):
            off = (base + j) * STEP - val
            e = jnp.exp2(-(off * off))
            acc = acc + (e * off) * rows[j : j + 1, :]
        return acc

    slope = lax.fori_loop(0, NUM_BINS // 8, bins, jnp.zeros_like(val))
    out_ref[0:tall, :] = lax.dot_general(
        slope * sig_ref[...], hid_ref[...], NN, precision=highest, preferred_element_type=f32
    )
    out_ref[tall:, :] = gh_ref[0, share:, :]


def back_steps(gh, val, sig, hidden):
    t, g = val.shape
    z = hidden.shape[1]
    return pl.pallas_call(
        back_kernel,
        grid=(1,),
        out_shape=jax.ShapeDtypeStruct((t + EXTRA, z), f32),
        in_specs=[fixed(gh.shape), fixed((t, g)), fixed((t, g)), fixed((g, z))],
        out_specs=fixed((t + EXTRA, z)),
        scratch_shapes=[VMEM((NUM_BINS, g), f32)],
        compiler_params=params(),
    )(gh, val, sig, hidden)


def row_squares(rows):
    hi, lo = split(rows * rows)
    ones = jnp.ones((8, 2 * rows.shape[1]), bf16)
    return dot(ones, jnp.concatenate([hi, lo], 1), NT)


def stat_kernel(rows_ref, sum_ref, near_ref, sq_ref):
    rows = rows_ref[...]
    near = rows.astype(bf16)
    near_ref[...] = near
    sq_ref[...] = row_squares(near.astype(f32))
    w = rows.shape[1]
    part = jnp.concatenate(
        [
            jnp.sum(rows.reshape(-1, 8, w), 0),
            jnp.sum((rows * rows).reshape(-1, 8, w), 0),
        ],
        0,
    )

    @pl.when(pl.program_id(0) == 0)
    def _():
        sum_ref[...] = part

    @pl.when(pl.program_id(0) > 0)
    def _():
        sum_ref[...] += part


def row_stats(rows, block):
    n, w = rows.shape
    block = min(block, n)
    return pl.pallas_call(
        stat_kernel,
        grid=(n // block,),
        out_shape=[
            jax.ShapeDtypeStruct((16, w), f32),
            jax.ShapeDtypeStruct((n, w), bf16),
            jax.ShapeDtypeStruct((8, n), f32),
        ],
        in_specs=[pl.BlockSpec((block, w), lambda i: (i, 0))],
        out_specs=[
            fixed((16, w)),
            pl.BlockSpec((block, w), lambda i: (i, 0)),
            pl.BlockSpec((8, block), lambda i: (0, i)),
        ],
        compiler_params=params(),
        cost_estimate=pl.CostEstimate(
            flops=32 * n * w, bytes_accessed=6 * n * w, transcendentals=0
        ),
    )(rows)


def share_kernel(parts_ref, len_ref, out_ref):
    count = jnp.sum(parts_ref[...], 0)
    hist = count / len_ref[...].astype(f32)
    out_ref[...] = jnp.broadcast_to(hist[None], out_ref.shape)


def load_kernel(others_ref, own_ref, real_ref, out_ref):
    parts, share, w = others_ref.shape
    rows = others_ref[...].reshape(parts * share, w)
    stats = jnp.concatenate(
        [
            jnp.sum(rows, 0, keepdims=True),
            jnp.sum(rows * rows, 0, keepdims=True),
            jnp.sum(real_ref[0:8, :], 0, keepdims=True),
            jnp.sum(real_ref[8:16, :], 0, keepdims=True),
            jnp.zeros((EXTRA - 4, w), f32),
        ],
        0,
    )
    load = jnp.concatenate([own_ref[0], stats], 0)
    out_ref[...] = jnp.broadcast_to(load[None], out_ref.shape)


def pair_kernel(
    cols, total_flows, total_real, hall_ref, others_ref, near_ref, sq_ref, out_ref,
    rate_ref, h_ref, hc_ref, hs_ref, ip_ref, wh_ref, mat_ref, sum_ref, kacc_ref,
):
    parts, tall, width = hall_ref.shape
    share = tall - EXTRA
    flows = parts * share

    @pl.when(pl.program_id(0) == 0)
    def _():
        h = jnp.concatenate([hall_ref[p, :share, :] for p in range(parts)], 0)
        h_ref[...] = h
        stats = hall_ref[0, share:, :]
        for p in range(1, parts):
            stats = stats + hall_ref[p, share:, :]
        line = (
            stats[1:2, :] / total_flows
            + stats[3:4, :] / total_real
            - 2.0 * ((stats[0:1, :] / total_flows) * (stats[2:3, :] / total_real))
        )
        spread = jnp.sum(line, 1, keepdims=True)
        rate = jnp.broadcast_to(LOG2E / (4.0 * spread), (8, 128))
        rate_ref[...] = rate
        one = rate[0:1, 0:1]
        hh, hl = split(h * (2.0 * one))
        hc_ref[...] = jnp.concatenate([hh, hl], 1)
        hs_ref[...] = jnp.broadcast_to(
            jnp.sum(h * h, 1, keepdims=True) * one, hs_ref.shape
        )
        mat_ref[...] = jnp.zeros_like(mat_ref)
        sum_ref[...] = jnp.zeros_like(sum_ref)
        kacc_ref[...] = jnp.zeros_like(kacc_ref)

    rate = rate_ref[0:1, 0:1]

    def weigh(x, at, kacc):
        u = jnp.exp2(x)
        u2 = u * u
        u4 = u2 * u2
        u8 = u4 * u4
        u16 = u8 * u8
        t4 = u16 + u16 + u8
        t3 = t4 + t4 + u4
        t2 = t3 + t3 + u2
        w = t2 + t2 + u
        k = (t4 + u16) + (t3 + t2)
        ws = w[:, 0:128]
        ks = k[:, 0:128]
        for q in range(1, w.shape[1] // 128):
            ws = ws + w[:, 128 * q : 128 * q + 128]
            ks = ks + k[:, 128 * q : 128 * q + 128]
        sum_ref[at, :] += ws
        for q in range(ks.shape[0] // 8):
            kacc = kacc + ks[8 * q : 8 * q + 8]
        return w, kacc

    def first(p):
        r = near_ref[p * cols : (p + 1) * cols, :]
        ip_ref[p % 2] = dot(hc_ref[...], jnp.concatenate([r, r], 1), NT)

    def second(p, kacc):
        sq = sq_ref[0:1, p * cols : (p + 1) * cols] * rate
        for c in range(flows // 16):
            at = slice(16 * c, 16 * c + 16)
            x = (ip_ref[p % 2, at, :] - sq) - jnp.tile(hs_ref[at, :], (1, cols // 128))
            w, kacc = weigh(x, at, kacc)
            wh_ref[p % 2, at, :] = w.astype(bf16)
        return kacc

    def third(p):
        mat_ref[...] += dot(wh_ref[p % 2], near_ref[p * cols : (p + 1) * cols, :], NN)

    count = near_ref.shape[0] // cols
    kacc = jnp.zeros((8, 128), f32)
    first(0)
    for p in range(count):
        if p + 1 < count:
            first(p + 1)
        kacc = second(p, kacc)
        if p > 0:
            third(p - 1)
    third(count - 1)
    kacc_ref[...] += kacc

    @pl.when(pl.program_id(0) == pl.num_programs(0) - 1)
    def _():
        h = h_ref[...]

        def finish(scale):
            total = jnp.sum(sum_ref[...], 1, keepdims=True)
            grad = (total * h - mat_ref[...]) * (rate * scale)
            lanes = jnp.sum(sum_ref[...], 0, keepdims=True) - jnp.sum(
                kacc_ref[...], 0, keepdims=True
            )
            return grad, jnp.sum(lanes, 1, keepdims=True)

        cross_g, cross_k = finish(4.0 / (total_real * LOG2E))
        mat_ref[...] = jnp.zeros_like(mat_ref)
        sum_ref[...] = jnp.zeros_like(sum_ref)
        kacc = jnp.zeros((8, 128), f32)
        rows_all = others_ref[...].reshape(-1, width)
        for p in range(rows_all.shape[0] // cols):
            rows = rows_all[p * cols : (p + 1) * cols]
            rh, rl = split(rows)
            hc = hc_ref[...]
            ip_ref[0] = dot(
                jnp.concatenate([hc, hc[:, :width]], 1),
                jnp.concatenate([rh, rh, rl], 1),
                NT,
            )
            sq = row_squares(rows)[0:1, :] * rate
            lows = []
            for c in range(flows // 16):
                at = slice(16 * c, 16 * c + 16)
                x = (ip_ref[0, at, :] - sq) - jnp.tile(hs_ref[at, :], (1, cols // 128))
                w, kacc = weigh(x, at, kacc)
                wh, wl = split(w)
                wh_ref[0, at, :] = wh
                wh_ref[1, at, :] = wl
            wh, wl = wh_ref[0], wh_ref[1]
            mat_ref[...] += dot(
                jnp.concatenate([wh, wl, wh], 1), jnp.concatenate([rh, rh, rl], 0), NN
            )
        kacc_ref[...] = kacc
        pair_g, pair_k = finish(-4.0 / (total_flows * LOG2E))
        grad = cross_g + pair_g
        loss = pair_k / (float(total_flows) * total_flows) - 2.0 * cross_k / (
            float(total_flows) * total_real
        )
        line = jnp.broadcast_to(loss, (EXTRA, width))
        for p in range(parts):
            out_ref[p, :share, :] = grad[p * share : (p + 1) * share]
            out_ref[p, share:, :] = line


def pair_sums(hall, others, near, sq, total_flows, total_real, block, cols):
    n, w = near.shape
    flows = hall.shape[0] * (hall.shape[1] - EXTRA)
    block = min(block, n)
    return pl.pallas_call(
        functools.partial(pair_kernel, cols, total_flows, total_real),
        grid=(n // block,),
        out_shape=jax.ShapeDtypeStruct(hall.shape, f32),
        in_specs=[
            fixed(hall.shape),
            fixed(others.shape),
            pl.BlockSpec((block, w), lambda i: (i, 0)),
            pl.BlockSpec((8, block), lambda i: (0, i)),
        ],
        out_specs=fixed(hall.shape),
        scratch_shapes=[
            VMEM((8, 128), f32),
            VMEM((flows, w), f32),
            VMEM((flows, 2 * w), bf16),
            VMEM((flows, 128), f32),
            VMEM((2, flows, cols), f32),
            VMEM((2, flows, cols), bf16),
            VMEM((flows, w), f32),
            VMEM((flows, 128), f32),
            VMEM((8, 128), f32),
        ],
        compiler_params=params(),
        cost_estimate=pl.CostEstimate(
            flops=6 * n * w * flows, bytes_accessed=2 * n * w, transcendentals=n * flows
        ),
    )(hall, others, near, sq)


def sum_kernel(parts_ref, out_ref):
    out_ref[...] = jnp.broadcast_to(jnp.sum(parts_ref[...], 0)[None], out_ref.shape)


def square_kernel(grad_ref, out_ref):
    grad = grad_ref[0 : grad_ref.shape[0] - EXTRA, :]
    lanes = jnp.sum(grad * grad, 0, keepdims=True)
    out_ref[...] = jnp.broadcast_to(jnp.sum(lanes, 1, keepdims=True), out_ref.shape)


def scale_kernel(grad_ref, sq_ref, out_ref, loss_ref):
    mean_sq = sq_ref[0:1, 0:1] * (1.0 / (HID_WIDTH * SEQ_STEPS))
    tall = out_ref.shape[0]
    out_ref[...] = grad_ref[0:tall, :] / jnp.sqrt(mean_sq + 1e-06)
    loss_ref[...] = grad_ref[tall:, 0:128]


def swap_sum(x, axis, count):
    hop = 1
    while hop < count:
        x = x + lax.ppermute(x, axis, [(i, i ^ hop) for i in range(count)])
        hop *= 2
    return x


def trade(x, axis):
    return lax.all_to_all(x, axis, 0, 0, tiled=True)


def per_device(real_count, gen_count, hidden, weight, lengths, real_rows):
    real_index = lax.axis_index("real")
    flows, width = hidden.shape
    local_steps = weight.shape[1]
    total_flows = flows * gen_count
    total_real = real_rows.shape[0] * real_count
    share = flows // real_count
    first = jnp.full((1,), real_index * local_steps, jnp.int32)
    counts, val, sig = call_once(
        count_kernel,
        [(flows, NUM_BINS), (local_steps, flows), (local_steps, flows)],
        first, weight.T, hidden, lengths[None, :], scalars=1,
    )
    parts = trade(counts.reshape(real_count, share, NUM_BINS), "real")
    own_len = lax.dynamic_slice_in_dim(lengths, real_index * share, share)[:, None]
    (own,) = call_once(share_kernel, [(gen_count, share, NUM_BINS)], parts, own_len)
    real_rows, own = lax.optimization_barrier((real_rows, own))
    others = trade(own, "gen")
    real_sums, near, sq = row_stats(real_rows, 2048)
    (load,) = call_once(
        load_kernel, [(real_count, share + EXTRA, NUM_BINS)], others, own, real_sums
    )
    hall = trade(load, "real")
    grad_part = pair_sums(hall, others, near, sq, total_flows, total_real, 4096, 256)
    (grad_own,) = call_once(sum_kernel, [grad_part.shape], trade(grad_part, "real"))
    part = back_steps(trade(grad_own, "real"), val, sig, hidden)
    grad = swap_sum(part, "gen", gen_count)
    (square,) = call_once(square_kernel, [(8, 128)], grad)
    square = swap_sum(square, "real", real_count)
    update, loss = call_once(
        scale_kernel, [(local_steps, width), (EXTRA, 128)], grad, square
    )
    return (update.T, loss[0, 0])


def solution(mesh):
    in_specs = (P("gen", None), P(None, "real"), P("gen"), P("real", None))
    out_specs = (P(None, "real"), P())
    body = functools.partial(per_device, mesh.shape["real"], mesh.shape["gen"])
    return jax.shard_map(
        body, mesh=mesh, in_specs=in_specs, out_specs=out_specs, check_vma=False
    )
```

time: 181 us -> 129 us (0.71)
  starting transfers between devices: 37 us -> 22.7 us
  blocking collectives: 46.2 us -> 32.2 us
  Pallas kernels: 50.7 us -> 42.5 us
  other arithmetic: 5.44 us -> 0.06 us
  between operations: 4.89 us -> 0.71 us
  local copies, waits for them, and re-layouts: 7.05 us -> 3.82 us
    all_gather x1 -> x0, blocking collectives: 23.8 us -> none  [per_device(): others = lax.all_gather(own, 'gen', axis=0, tiled=True)]
    ppermute x18 -> x7, starting transfers between devices: 24.9 us -> 9.54 us  [swap_sum(): x = x + lax.ppermute(x, axis, [(i, i ^ hop) for i in range(count)])]
    pallas_call x4 -> x8, Pallas kernels: 39.6 us -> 28.8 us  [the longest x1 16.6 us: pair_sums(): pl.pallas_call(functools.partial(pair_kernel, cols, total_flows, total_re...]
    all_to_all x2 -> x3, blocking collectives: 22.3 us -> 32.2 us  [trade(): return lax.all_to_all(x, axis, 0, 0, tiled=True)]
    ppermute x18 -> x7, waiting for transfers between devices: 28.6 us -> 20.4 us  [swap_sum(): x = x + lax.ppermute(x, axis, [(i, i ^ hop) for i in range(count)])]
    all_to_all x2, waiting for transfers between devices: 0.01 us -> 6.39 us  [trade(): return lax.all_to_all(x, axis, 0, 0, tiled=True)]
    reduce_sum x9 -> x0, other arithmetic: 3.9 us -> none  [the longest x1 0.73 us: per_device(): jnp.sum(real_sq[0])]
    pallas_call x2 -> x1, Pallas kernels: 11.2 us -> 13.7 us  [row_stats(): pl.pallas_call(stat_kernel, grid=(n // block,), out_shape=[jax.ShapeDtype...]
  transfers between devices with their start and end apart: 20 -> 9, of which waited for: 14 -> 8; matrix products, arithmetic and copies ran while one was open for 3% -> 1% of each run, Pallas kernels for 6% -> 11%
where the time goes in v2:
time: 129 us
  Pallas kernels  42.5 us (33%)
  blocking collectives  32.2 us (25%)
  waiting for transfers between devices  26.8 us (21%)
  starting transfers between devices  22.7 us (18%)
  local copies, waits for them, and re-layouts  3.82 us (3%)
    all_to_all x3, blocking collectives, trade(): return lax.all_to_all(x, axis, 0, 0, tiled=True)  32.2 us
    ppermute x7, waiting for transfers between devices, swap_sum(): x = x + lax.ppermute(x, axis, [(i, i ^ hop) for i in range(count)])  20.4 us
    pallas_call x1, Pallas kernels, pair_sums(): pl.pallas_call(functools.partial(pair_kernel, cols, total_flows, total_re...  16.6 us
    pallas_call x1, Pallas kernels, row_stats(): pl.pallas_call(stat_kernel, grid=(n // block,), out_shape=[jax.ShapeDtype...  13.7 us
    all_to_all x2, starting transfers between devices, trade(): return lax.all_to_all(x, axis, 0, 0, tiled=True)  13.2 us
    ppermute x7, starting transfers between devices, swap_sum(): x = x + lax.ppermute(x, axis, [(i, i ^ hop) for i in range(count)])  9.54 us
    pallas_call x6, Pallas kernels, call_once(): pl.pallas_call(kernel, grid=(1,), out_shape=[jax.ShapeDtypeStruct(s, f32)...  7.74 us
    all_to_all x2, waiting for transfers between devices, trade(): return lax.all_to_all(x, axis, 0, 0, tiled=True)  6.39 us
  transfers between devices with their start and end apart: 9, of which 8 were waited for; matrix products, arithmetic and copies ran while one was open for 1% of the time, Pallas kernels for 11%

profile of v2, /device:TPU:0, one launch (start us, length us, event | category | flops | bytes accessed | tf_op | source)
XLA Modules:
  0.0 128.8 jit_solution(9542000008842258084)
XLA Ops:
  0.6 0.0 copy-start
  0.6 0.9 copy-done
  1.6 0.0 copy-start.2
  1.6 0.8 copy-done.2
  2.4 0.0 copy-start.3
  2.4 0.7 copy-done.3
  3.1 4.8 %shard_map.59 = (f32[256,256]{1,0:T(8,128)}, f32[64,256]{1,0:T(8,128)S(1)}, f32[64,256]{1,0:T(8,128)S(1)}) custom-call(s32[1]{0:T(128)} %bitcast.first_ref, f32[64,256]{1,0:T(8,128)S(1)} %bitcast.8, f32[256,256]{1,0:T(8,128)S(1)} %copy-done, s32[1,256]{1,0:T(1,128)S(1)} %bitcast.9), custom_call_target="tpu_custom_call" | custom-call | tf_op jit(solution)/shard_map/pallas_call | solution.py:39
  7.9 6.4 %all-to-all-start = ((f32[8,32,256]{2,1,0:T(8,128)}), f32[8,32,256]{2,1,0:T(8,128)S(1)}, u32[]{:S(2)}, u32[]{:S(2)}) async-start(f32[8,32,256]{2,1,0:T(8,128)} %bitcast.3), calls=%async_computation | async-start | bytes 524288 | tf_op jit(solution)/shard_map/all_to_all | solution.py:395
  14.3 0.8 dynamic-slice_bitcast_fusion
  15.1 0.1 copy.6.len_ref
  15.2 6.4 %all-to-all-done.parts_ref = f32[8,32,256]{2,1,0:T(8,128)S(1)} async-done(((f32[8,32,256]{2,1,0:T(8,128)}), f32[8,32,256]{2,1,0:T(8,128)S(1)}, u32[]{:S(2)}, u32[]{:S(2)}) %all-to-all-start) | async-done | bytes 262176 | tf_op jit(solution)/shard_map/all_to_all | solution.py:395
  21.5 1.0 shard_map.60.own_ref
  22.5 6.7 %all-to-all-start.1 = ((f32[16,32,256]{2,1,0:T(8,128)}), f32[16,32,256]{2,1,0:T(8,128)S(1)}, u32[]{:S(2)}, u32[]{:S(2)}) async-start(f32[16,32,256]{2,1,0:T(8,128)} %shard_map.60.own_ref), calls=%async_computation.1 | async-start | bytes 1048576 | tf_op jit(solution)/shard_map/all_to_all | solution.py:395
  29.2 13.7 %shard_map.61 = (f32[16,256]{1,0:T(8,128)S(1)}, bf16[16384,256]{1,0:T(8,128)(2,1)}, f32[8,16384]{1,0:T(8,128)S(1)}) custom-call(f32[16384,256]{1,0:T(8,128)} %rows_ref), custom_call_target="tpu_custom_call" | custom-call | flops 134217728 | bytes 25165824 | tf_op jit(solution)/shard_map/pallas_call | solution.py:157
  42.9 0.0 copy-start.1
  42.9 0.0 all-to-all-done.1.others_ref
  42.9 1.2 shard_map.62
  44.1 11.3 %all_to_all.25.hall_ref = f32[8,40,256]{2,1,0:T(8,128)S(1)} all-to-all(f32[8,40,256]{2,1,0:T(8,128)S(1)} %shard_map.62), channel_id=1, replica_groups=mesh['real'=8,'gen'=16] {'real'}, dimensions={0} | all-to-all | bytes 655360 | tf_op jit(solution)/shard_map/all_to_all | solution.py:395
  55.4 16.6 %shard_map.63 = f32[8,40,256]{2,1,0:T(8,128)S(1)} custom-call(f32[8,40,256]{2,1,0:T(8,128)S(1)} %all_to_all.25.hall_ref, f32[16,32,256]{2,1,0:T(8,128)S(1)} %all-to-all-done.1.others_ref, bf16[16384,256]{1,0:T(8,128)(2,1)} %get-tuple-element.16.near_ref, f32[8,16384]{1,0:T(8,128)S(1)} %get-tuple-element.17.sq_ref), custom_call_target="tpu_custom_call" | custom-call | flops 6442450944 | bytes 8388608 | tf_op jit(solution)/shard_map/pallas_call | solution.py:340
  72.1 10.7 %all_to_all.26.parts_ref = f32[8,40,256]{2,1,0:T(8,128)S(1)} all-to-all(f32[8,40,256]{2,1,0:T(8,128)S(1)} %shard_map.63), channel_id=1, replica_groups=mesh['real'=8,'gen'=16] {'real'}, dimensions={0} | all-to-all | bytes 655360 | tf_op jit(solution)/shard_map/all_to_all | solution.py:395
  82.8 10.2 %all_to_all.27.gh_ref = f32[8,40,256]{2,1,0:T(8,128)S(1)} all-to-all(f32[8,40,256]{2,1,0:T(8,128)S(1)} %shard_map.64), channel_id=1, replica_groups=mesh['real'=8,'gen'=16] {'real'}, dimensions={0} | all-to-all | bytes 655360 | tf_op jit(solution)/shard_map/all_to_all | solution.py:395
  93.0 0.0 copy-done.1
  93.0 4.5 %shard_map.65 = f32[72,256]{1,0:T(8,128)S(1)} custom-call(f32[8,40,256]{2,1,0:T(8,128)S(1)} %all_to_all.27.gh_ref, f32[64,256]{1,0:T(8,128)S(1)} %get-tuple-element.18.val_ref, f32[64,256]{1,0:T(8,128)S(1)} %get-tuple-element.19.sig_ref, f32[256,256]{1,0:T(8,128)S(1)} %copy-done.1), custom_call_target="tpu_custom_call" | custom-call | tf_op jit(solution)/shard_map/pallas_call | solution.py:114
  97.5 0.1 collective-permute-start
  97.6 1.3 collective-permute-done
  98.8 2.8 %collective-permute-start.1 = (f32[72,256]{1,0:T(8,128)S(1)}, f32[72,256]{1,0:T(8,128)S(1)}, u32[]{:S(2)}, u32[]{:S(2)}) collective-permute-start(f32[72,256]{1,0:T(8,128)S(1)} %add.25), channel_id=1, source_target_pairs={{0,2},{1,3},{2,0},{3,1},{4,6},{5,7},{6,4},{7,5},{8,10},{9,11},{10,... | collective-permute-start | bytes 221192 | tf_op jit(solution)/shard_map/ppermute | solution.py:389
  101.6 3.2 %collective-permute-done.1 = f32[72,256]{1,0:T(8,128)S(1)} collective-permute-done((f32[72,256]{1,0:T(8,128)S(1)}, f32[72,256]{1,0:T(8,128)S(1)}, u32[]{:S(2)}, u32[]{:S(2)}) %collective-permute-start.1) | collective-permute-done | bytes 73760 | tf_op jit(solution)/shard_map/ppermute | solution.py:389
  104.8 1.5 %collective-permute-start.2 = (f32[72,256]{1,0:T(8,128)S(1)}, f32[72,256]{1,0:T(8,128)S(1)}, u32[]{:S(2)}, u32[]{:S(2)}) collective-permute-start(f32[72,256]{1,0:T(8,128)S(1)} %add.26), channel_id=1, source_target_pairs={{0,4},{1,5},{2,6},{3,7},{4,0},{5,1},{6,2},{7,3},{8,12},{9,13},{10,... | collective-permute-start | bytes 221192 | tf_op jit(solution)/shard_map/ppermute | solution.py:389
  106.3 2.9 %collective-permute-done.2 = f32[72,256]{1,0:T(8,128)S(1)} collective-permute-done((f32[72,256]{1,0:T(8,128)S(1)}, f32[72,256]{1,0:T(8,128)S(1)}, u32[]{:S(2)}, u32[]{:S(2)}) %collective-permute-start.2) | collective-permute-done | bytes 73760 | tf_op jit(solution)/shard_map/ppermute | solution.py:389
  109.2 3.0 %collective-permute-start.3 = (f32[72,256]{1,0:T(8,128)S(1)}, f32[72,256]{1,0:T(8,128)S(1)}, u32[]{:S(2)}, u32[]{:S(2)}) collective-permute-start(f32[72,256]{1,0:T(8,128)S(1)} %add.27), channel_id=1, source_target_pairs={{0,8},{1,9},{2,10},{3,11},{4,12},{5,13},{6,14},{7,15},{8,0},{9,1},... | collective-permute-start | bytes 221192 | tf_op jit(solution)/shard_map/ppermute | solution.py:389
  112.2 2.9 %collective-permute-done.3 = f32[72,256]{1,0:T(8,128)S(1)} collective-permute-done((f32[72,256]{1,0:T(8,128)S(1)}, f32[72,256]{1,0:T(8,128)S(1)}, u32[]{:S(2)}, u32[]{:S(2)}) %collective-permute-start.3) | collective-permute-done | bytes 73760 | tf_op jit(solution)/shard_map/ppermute | solution.py:389
  115.2 0.1 shard_map.66
  115.3 0.6 collective-permute-start.4
  115.9 3.0 %collective-permute-done.4 = f32[8,128]{1,0:T(8,128)S(1)} collective-permute-done((f32[8,128]{1,0:T(8,128)S(1)}, f32[8,128]{1,0:T(8,128)S(1)}, u32[]{:S(2)}, u32[]{:S(2)}) %collective-permute-start.4) | collective-permute-done | bytes 4128 | tf_op jit(solution)/shard_map/ppermute | solution.py:389
  118.9 1.1 collective-permute-start.5
  120.0 4.0 %collective-permute-done.5 = f32[8,128]{1,0:T(8,128)S(1)} collective-permute-done((f32[8,128]{1,0:T(8,128)S(1)}, f32[8,128]{1,0:T(8,128)S(1)}, u32[]{:S(2)}, u32[]{:S(2)}) %collective-permute-start.5) | collective-permute-done | bytes 4128 | tf_op jit(solution)/shard_map/ppermute | solution.py:389
  124.0 0.6 collective-permute-start.6
  124.6 3.0 %collective-permute-done.6 = f32[8,128]{1,0:T(8,128)S(1)} collective-permute-done((f32[8,128]{1,0:T(8,128)S(1)}, f32[8,128]{1,0:T(8,128)S(1)}, u32[]{:S(2)}, u32[]{:S(2)}) %collective-permute-start.6) | collective-permute-done | bytes 4128 | tf_op jit(solution)/shard_map/ppermute | solution.py:389
  127.6 0.7 shard_map.67
  128.3 0.5 slice.3
  (8 shorter events, 0.1 us)
Async XLA Ops:
  0.6 1.0 copy-start
  1.6 0.8 copy-start.2
  2.4 0.7 copy-start.3
  7.9 13.6 %all-to-all-start = ((f32[8,32,256]{2,1,0:T(8,128)}), f32[8,32,256]{2,1,0:T(8,128)S(1)}, u32[]{:S(2)}, u32[]{:S(2)}) async-start(f32[8,32,256]{2,1,0:T(8,128)} %bitcast.3), calls=%async_computation | async-start | bytes 524288 | tf_op jit(solution)/shard_map/all_to_all | solution.py:395
  22.5 20.4 %all-to-all-start.1 = ((f32[16,32,256]{2,1,0:T(8,128)}), f32[16,32,256]{2,1,0:T(8,128)S(1)}, u32[]{:S(2)}, u32[]{:S(2)}) async-start(f32[16,32,256]{2,1,0:T(8,128)} %shard_map.60.own_ref), calls=%async_computation.1 | async-start | bytes 1048576 | tf_op jit(solution)/shard_map/all_to_all | solution.py:395
  42.9 50.1 %copy-start.1 = (f32[256,256]{1,0:T(8,128)S(1)}, f32[256,256]{1,0:T(8,128)}, u32[]{:S(2)}) copy-start(f32[256,256]{1,0:T(8,128)} %hid_ref.3) | copy-start | bytes 786436
  97.5 1.3 %collective-permute-start = (f32[72,256]{1,0:T(8,128)S(1)}, f32[72,256]{1,0:T(8,128)S(1)}, u32[]{:S(2)}, u32[]{:S(2)}) collective-permute-start(f32[72,256]{1,0:T(8,128)S(1)} %shard_map.65), channel_id=1, source_target_pairs={{0,1},{1,0},{2,3},{3,2},{4,5},{5,4},{6,7},{7,6},{8,9},{9,8},{10,11... | collective-permute-start | bytes 221192 | tf_op jit(solution)/shard_map/ppermute | solution.py:389
  98.8 5.9 %collective-permute-start.1 = (f32[72,256]{1,0:T(8,128)S(1)}, f32[72,256]{1,0:T(8,128)S(1)}, u32[]{:S(2)}, u32[]{:S(2)}) collective-permute-start(f32[72,256]{1,0:T(8,128)S(1)} %add.25), channel_id=1, source_target_pairs={{0,2},{1,3},{2,0},{3,1},{4,6},{5,7},{6,4},{7,5},{8,10},{9,11},{10,... | collective-permute-start | bytes 221192 | tf_op jit(solution)/shard_map/ppermute | solution.py:389
  104.8 4.4 %collective-permute-start.2 = (f32[72,256]{1,0:T(8,128)S(1)}, f32[72,256]{1,0:T(8,128)S(1)}, u32[]{:S(2)}, u32[]{:S(2)}) collective-permute-start(f32[72,256]{1,0:T(8,128)S(1)} %add.26), channel_id=1, source_target_pairs={{0,4},{1,5},{2,6},{3,7},{4,0},{5,1},{6,2},{7,3},{8,12},{9,13},{10,... | collective-permute-start | bytes 221192 | tf_op jit(solution)/shard_map/ppermute | solution.py:389
  109.2 5.9 %collective-permute-start.3 = (f32[72,256]{1,0:T(8,128)S(1)}, f32[72,256]{1,0:T(8,128)S(1)}, u32[]{:S(2)}, u32[]{:S(2)}) collective-permute-start(f32[72,256]{1,0:T(8,128)S(1)} %add.27), channel_id=1, source_target_pairs={{0,8},{1,9},{2,10},{3,11},{4,12},{5,13},{6,14},{7,15},{8,0},{9,1},... | collective-permute-start | bytes 221192 | tf_op jit(solution)/shard_map/ppermute | solution.py:389
  115.3 3.6 %collective-permute-start.4 = (f32[8,128]{1,0:T(8,128)S(1)}, f32[8,128]{1,0:T(8,128)S(1)}, u32[]{:S(2)}, u32[]{:S(2)}) collective-permute-start(f32[8,128]{1,0:T(8,128)S(1)} %shard_map.66), channel_id=1, source_target_pairs={{0,16},{16,0},{32,48},{48,32},{64,80},{80,64},{96,112},{112,96},{1... | collective-permute-start | bytes 12296 | tf_op jit(solution)/shard_map/ppermute | solution.py:389
  118.9 5.1 %collective-permute-start.5 = (f32[8,128]{1,0:T(8,128)S(1)}, f32[8,128]{1,0:T(8,128)S(1)}, u32[]{:S(2)}, u32[]{:S(2)}) collective-permute-start(f32[8,128]{1,0:T(8,128)S(1)} %add.29), channel_id=1, source_target_pairs={{0,32},{16,48},{32,0},{48,16},{64,96},{80,112},{96,64},{112,80},{1... | collective-permute-start | bytes 12296 | tf_op jit(solution)/shard_map/ppermute | solution.py:389
  124.0 3.6 %collective-permute-start.6 = (f32[8,128]{1,0:T(8,128)S(1)}, f32[8,128]{1,0:T(8,128)S(1)}, u32[]{:S(2)}, u32[]{:S(2)}) collective-permute-start(f32[8,128]{1,0:T(8,128)S(1)} %add.30), channel_id=1, source_target_pairs={{0,64},{16,80},{32,96},{48,112},{64,0},{80,16},{96,32},{112,48},{1... | collective-permute-start | bytes 12296 | tf_op jit(solution)/shard_map/ppermute | solution.py:389

commit v3 on v2

--- a/solution.py
+++ b/solution.py
@@ -35,7 +35,7 @@
     return pl.BlockSpec(shape, lambda i: (0,) * len(shape))
 
 
-def call_once(kernel, outs, *args, scalars=0):
+def call_once(kernel, outs, *args, scalars=0, limit=48 << 20):
     return pl.pallas_call(
         kernel,
         grid=(1,),
@@ -45,7 +45,7 @@
             for i, a in enumerate(args)
         ],
         out_specs=[fixed(s) for s in outs],
-        compiler_params=params(),
+        compiler_params=params(limit),
     )(*args)
 
 
@@ -122,18 +122,19 @@
     )(gh, val, sig, hidden)
 
 
-def row_squares(rows):
-    hi, lo = split(rows * rows)
-    ones = jnp.ones((8, 2 * rows.shape[1]), bf16)
+def row_squares(squares):
+    hi, lo = split(squares)
+    ones = jnp.ones((8, 2 * squares.shape[1]), bf16)
     return dot(ones, jnp.concatenate([hi, lo], 1), NT)
 
 
-def stat_kernel(rows_ref, sum_ref, near_ref, sq_ref):
+def stat_kernel(rows_ref, sum_ref, sq_ref):
     rows = rows_ref[...]
-    near = rows.astype(bf16)
-    near_ref[...] = near
-    sq_ref[...] = row_squares(near.astype(f32))
     w = rows.shape[1]
+    near = rows.astype(bf16).astype(f32)
+    near = near * near
+    half = w // 2
+    sq_ref[...] = row_squares(near[:, :half] + near[:, half:])
     part = jnp.concatenate(
         [
             jnp.sum(rows.reshape(-1, 8, w), 0),
@@ -151,26 +152,23 @@
         sum_ref[...] += part
 
 
-def row_stats(rows, block):
-    n, w = rows.shape
-    block = min(block, n)
+def row_stats(rows, block, start, count):
+    w = rows.shape[1]
     return pl.pallas_call(
         stat_kernel,
-        grid=(n // block,),
+        grid=(count,),
         out_shape=[
             jax.ShapeDtypeStruct((16, w), f32),
-            jax.ShapeDtypeStruct((n, w), bf16),
-            jax.ShapeDtypeStruct((8, n), f32),
-        ],
-        in_specs=[pl.BlockSpec((block, w), lambda i: (i, 0))],
+            jax.ShapeDtypeStruct((8, count * block), f32),
+        ],
+        in_specs=[pl.BlockSpec((block, w), lambda i: (start + i, 0))],
         out_specs=[
             fixed((16, w)),
-            pl.BlockSpec((block, w), lambda i: (i, 0)),
             pl.BlockSpec((8, block), lambda i: (0, i)),
         ],
         compiler_params=params(),
         cost_estimate=pl.CostEstimate(
-            flops=32 * n * w, bytes_accessed=6 * n * w, transcendentals=0
+            flops=16 * count * block * w, bytes_accessed=4 * count * block * w, transcendentals=0
         ),
     )(rows)
 
@@ -181,15 +179,17 @@
     out_ref[...] = jnp.broadcast_to(hist[None], out_ref.shape)
 
 
-def load_kernel(others_ref, own_ref, real_ref, out_ref):
+def load_kernel(others_ref, more_ref, own_ref, front_ref, back_ref, out_ref):
     parts, share, w = others_ref.shape
-    rows = others_ref[...].reshape(parts * share, w)
+    rows = jnp.concatenate(
+        [r[...].reshape(parts * share, w) for r in (others_ref, more_ref)], 0
+    )
     stats = jnp.concatenate(
         [
             jnp.sum(rows, 0, keepdims=True),
             jnp.sum(rows * rows, 0, keepdims=True),
-            jnp.sum(real_ref[0:8, :], 0, keepdims=True),
-            jnp.sum(real_ref[8:16, :], 0, keepdims=True),
+            jnp.sum(front_ref[0:8, :] + back_ref[0:8, :], 0, keepdims=True),
+            jnp.sum(front_ref[8:16, :] + back_ref[8:16, :], 0, keepdims=True),
             jnp.zeros((EXTRA - 4, w), f32),
         ],
         0,
@@ -199,8 +199,8 @@
 
 
 def pair_kernel(
-    cols, total_flows, total_real, hall_ref, others_ref, near_ref, sq_ref, out_ref,
-    rate_ref, h_ref, hc_ref, hs_ref, ip_ref, wh_ref, mat_ref, sum_ref, kacc_ref,
+    cols, total_flows, total_real, hall_ref, others_ref, more_ref, rows_ref, front_ref, back_ref, out_ref,
+    rate_ref, h_ref, hc_ref, hs_ref, ip_ref, wh_ref, mat_ref, sum_ref, kacc_ref, near_ref, sq_ref,
 ):
     parts, tall, width = hall_ref.shape
     share = tall - EXTRA
@@ -254,12 +254,16 @@
             kacc = kacc + ks[8 * q : 8 * q + 8]
         return w, kacc
 
+    early = pl.program_id(0) < pl.num_programs(0) // 2
+    sq_ref[...] = jnp.where(early, front_ref[0:1, :], back_ref[0:1, :]) * rate
+
     def first(p):
-        r = near_ref[p * cols : (p + 1) * cols, :]
+        r = rows_ref[p * cols : (p + 1) * cols, :].astype(bf16)
+        near_ref[p % 3] = r
         ip_ref[p % 2] = dot(hc_ref[...], jnp.concatenate([r, r], 1), NT)
 
     def second(p, kacc):
-        sq = sq_ref[0:1, p * cols : (p + 1) * cols] * rate
+        sq = sq_ref[0:1, p * cols : (p + 1) * cols]
         for c in range(flows // 16):
             at = slice(16 * c, 16 * c + 16)
             x = (ip_ref[p % 2, at, :] - sq) - jnp.tile(hs_ref[at, :], (1, cols // 128))
@@ -268,9 +272,9 @@
         return kacc
 
     def third(p):
-        mat_ref[...] += dot(wh_ref[p % 2], near_ref[p * cols : (p + 1) * cols, :], NN)
-
-    count = near_ref.shape[0] // cols
+        mat_ref[...] += dot(wh_ref[p % 2], near_ref[p % 3], NN)
+
+    count = rows_ref.shape[0] // cols
     kacc = jnp.zeros((8, 128), f32)
     first(0)
     for p in range(count):
@@ -298,7 +302,9 @@
         mat_ref[...] = jnp.zeros_like(mat_ref)
         sum_ref[...] = jnp.zeros_like(sum_ref)
         kacc = jnp.zeros((8, 128), f32)
-        rows_all = others_ref[...].reshape(-1, width)
+        rows_all = jnp.concatenate(
+            [r[...].reshape(-1, width) for r in (others_ref, more_ref)], 0
+        )
         for p in range(rows_all.shape[0] // cols):
             rows = rows_all[p * cols : (p + 1) * cols]
             rh, rl = split(rows)
@@ -308,7 +314,7 @@
                 jnp.concatenate([rh, rh, rl], 1),
                 NT,
             )
-            sq = row_squares(rows)[0:1, :] * rate
+            sq = row_squares(rows * rows)[0:1, :] * rate
             lows = []
             for c in range(flows // 16):
                 at = slice(16 * c, 16 * c + 16)
@@ -333,19 +339,21 @@
             out_ref[p, share:, :] = line
 
 
-def pair_sums(hall, others, near, sq, total_flows, total_real, block, cols):
-    n, w = near.shape
+def pair_sums(hall, others, more, rows, front, back, total_flows, total_real, block, cols):
+    n, w = rows.shape
     flows = hall.shape[0] * (hall.shape[1] - EXTRA)
-    block = min(block, n)
+    half = n // block // 2
     return pl.pallas_call(
         functools.partial(pair_kernel, cols, total_flows, total_real),
-        grid=(n // block,),
+        grid=(2 * half,),
         out_shape=jax.ShapeDtypeStruct(hall.shape, f32),
         in_specs=[
             fixed(hall.shape),
             fixed(others.shape),
+            fixed(more.shape),
             pl.BlockSpec((block, w), lambda i: (i, 0)),
-            pl.BlockSpec((8, block), lambda i: (0, i)),
+            pl.BlockSpec((8, block), lambda i: (0, jnp.minimum(i, half - 1))),
+            pl.BlockSpec((8, block), lambda i: (0, jnp.maximum(i - half, 0))),
         ],
         out_specs=fixed(hall.shape),
         scratch_shapes=[
@@ -358,12 +366,14 @@
             VMEM((flows, w), f32),
             VMEM((flows, 128), f32),
             VMEM((8, 128), f32),
+            VMEM((3, cols, w), bf16),
+            VMEM((1, block), f32),
         ],
         compiler_params=params(),
         cost_estimate=pl.CostEstimate(
-            flops=6 * n * w * flows, bytes_accessed=2 * n * w, transcendentals=n * flows
+            flops=6 * n * w * flows, bytes_accessed=4 * n * w, transcendentals=n * flows
         ),
-    )(hall, others, near, sq)
+    )(hall, others, more, rows, front, back)
 
 
 def sum_kernel(parts_ref, out_ref):
@@ -373,26 +383,26 @@
 def square_kernel(grad_ref, out_ref):
     grad = grad_ref[0 : grad_ref.shape[0] - EXTRA, :]
     lanes = jnp.sum(grad * grad, 0, keepdims=True)
-    out_ref[...] = jnp.broadcast_to(jnp.sum(lanes, 1, keepdims=True), out_ref.shape)
+    out_ref[...] = jnp.broadcast_to(jnp.sum(lanes, 1, keepdims=True)[None], out_ref.shape)
 
 
 def scale_kernel(grad_ref, sq_ref, out_ref, loss_ref):
-    mean_sq = sq_ref[0:1, 0:1] * (1.0 / (HID_WIDTH * SEQ_STEPS))
+    mean_sq = jnp.sum(sq_ref[...], 0)[0:1, 0:1] * (1.0 / (HID_WIDTH * SEQ_STEPS))
     tall = out_ref.shape[0]
     out_ref[...] = grad_ref[0:tall, :] / jnp.sqrt(mean_sq + 1e-06)
-    loss_ref[...] = grad_ref[tall:, 0:128]
-
-
-def swap_sum(x, axis, count):
-    hop = 1
-    while hop < count:
-        x = x + lax.ppermute(x, axis, [(i, i ^ hop) for i in range(count)])
-        hop *= 2
+    loss_ref[0] = jnp.max(grad_ref[tall : tall + 1, 0:128])
+
+
+def swap_sum(x, axis, count, groups):
+    for hops in groups:
+        sent = [lax.ppermute(x, axis, [(i, i ^ hop) for i in range(count)]) for hop in hops]
+        for other in sent:
+            x = x + other
     return x
 
 
-def trade(x, axis):
-    return lax.all_to_all(x, axis, 0, 0, tiled=True)
+def trade(x, axis, groups=None):
+    return lax.all_to_all(x, axis, 0, 0, axis_index_groups=groups, tiled=True)
 
 
 def per_device(real_count, gen_count, hidden, weight, lengths, real_rows):
@@ -402,32 +412,51 @@
     total_flows = flows * gen_count
     total_real = real_rows.shape[0] * real_count
     share = flows // real_count
+    block = min(4096, real_rows.shape[0] // 2)
+    half = real_rows.shape[0] // block // 2
     first = jnp.full((1,), real_index * local_steps, jnp.int32)
     counts, val, sig = call_once(
         count_kernel,
         [(flows, NUM_BINS), (local_steps, flows), (local_steps, flows)],
-        first, weight.T, hidden, lengths[None, :], scalars=1,
-    )
+        first, weight.T, hidden, lengths[None, :], scalars=1, limit=60 << 20,
+    )
+    rows_early, counts = lax.optimization_barrier((real_rows, counts))
     parts = trade(counts.reshape(real_count, share, NUM_BINS), "real")
+    front_sums, front_sq = row_stats(rows_early, block, 0, half)
     own_len = lax.dynamic_slice_in_dim(lengths, real_index * share, share)[:, None]
-    (own,) = call_once(share_kernel, [(gen_count, share, NUM_BINS)], parts, own_len)
-    real_rows, own = lax.optimization_barrier((real_rows, own))
-    others = trade(own, "gen")
-    real_sums, near, sq = row_stats(real_rows, 2048)
+    own_len, front_sums = lax.optimization_barrier((own_len, front_sums))
+    (own,) = call_once(share_kernel, [(gen_count // 2, share, NUM_BINS)], parts, own_len)
+    same = [list(range(c, gen_count, 2)) for c in range(2)]
+    rows_late, own = lax.optimization_barrier((real_rows, own))
+    near_rows = trade(own, "gen", same)
+    back_sums, back_sq = row_stats(rows_late, block, half, half)
+    near_rows, back_sums = lax.optimization_barrier((near_rows, back_sums))
+    far_rows = lax.ppermute(near_rows, "gen", [(i, i ^ 1) for i in range(gen_count)])
     (load,) = call_once(
-        load_kernel, [(real_count, share + EXTRA, NUM_BINS)], others, own, real_sums
+        load_kernel,
+        [(real_count, share + EXTRA, NUM_BINS)],
+        near_rows, far_rows, own, front_sums, back_sums,
     )
     hall = trade(load, "real")
-    grad_part = pair_sums(hall, others, near, sq, total_flows, total_real, 4096, 256)
+    grad_part = pair_sums(
+        hall, near_rows, far_rows, real_rows, front_sq, back_sq, total_flows, total_real, block, 256
+    )
     (grad_own,) = call_once(sum_kernel, [grad_part.shape], trade(grad_part, "real"))
     part = back_steps(trade(grad_own, "real"), val, sig, hidden)
-    grad = swap_sum(part, "gen", gen_count)
-    (square,) = call_once(square_kernel, [(8, 128)], grad)
-    square = swap_sum(square, "real", real_count)
-    update, loss = call_once(
-        scale_kernel, [(local_steps, width), (EXTRA, 128)], grad, square
-    )
-    return (update.T, loss[0, 0])
+    grad = swap_sum(part, "gen", gen_count, ((1,), (2,), (4, 8, 12)))
+    (square,) = call_once(square_kernel, [(real_count, 8, 128)], grad)
+    update, loss = pl.pallas_call(
+        scale_kernel,
+        grid=(1,),
+        out_shape=[
+            jax.ShapeDtypeStruct((local_steps, width), f32),
+            jax.ShapeDtypeStruct((1,), f32),
+        ],
+        in_specs=[fixed(grad.shape), fixed(square.shape)],
+        out_specs=[fixed((local_steps, width)), pl.BlockSpec(memory_space=SMEM)],
+        compiler_params=params(),
+    )(grad, trade(square, "real"))
+    return (update.T, loss.reshape(()))
 
 
 def solution(mesh):

time: 129 us -> 117 us (0.907)
  waiting for transfers between devices: 26.8 us -> 16.6 us
  blocking collectives: 32.2 us -> 40.3 us
  starting transfers between devices: 22.7 us -> 18.8 us
  local copies, waits for them, and re-layouts: 3.82 us -> 0.19 us
  Pallas kernels: 42.5 us -> 39.9 us
    ppermute x7 -> x6, waiting for transfers between devices: 20.4 us -> 10.4 us  [the longest x5 8.84 us: swap_sum(): lax.ppermute(x, axis, [(i, i ^ hop) for i in range(count)])]
    all_to_all x3 -> x4, blocking collectives: 32.2 us -> 40.3 us  [trade(): return lax.all_to_all(x, axis, 0, 0, axis_index_groups=groups, tiled=True)]
    ppermute x7 -> x6, starting transfers between devices: 9.54 us -> 5.73 us  [the longest x5 5.72 us: swap_sum(): lax.ppermute(x, axis, [(i, i ^ hop) for i in range(count)])]
    pallas_call x1 -> x3, Pallas kernels: 13.7 us -> 9.91 us  [the longest x2 9.21 us: row_stats(): pl.pallas_call(stat_kernel, grid=(count,), out_shape=[jax.ShapeDtypeStruc...]
    unnamed x8, local copies, waits for them, and re-layouts: 2.47 us -> 0.02 us
    pallas_call x6 -> x5, Pallas kernels: 7.74 us -> 7.7 us  [call_once(): pl.pallas_call(kernel, grid=(1,), out_shape=[jax.ShapeDtypeStruct(s, f32)...]
  transfers between devices with their start and end apart: 9 -> 8, of which waited for: 8 -> 8; matrix products, arithmetic and copies ran while one was open for 1% -> 0% of each run, Pallas kernels for 11% -> 8%
where the time goes in v3:
time: 117 us
  blocking collectives  40.3 us (34%)
  Pallas kernels  39.9 us (34%)
  starting transfers between devices  18.8 us (16%)
  waiting for transfers between devices  16.6 us (14%)
    all_to_all x4, blocking collectives, trade(): return lax.all_to_all(x, axis, 0, 0, axis_index_groups=groups, tiled=True)  40.3 us
    pallas_call x1, Pallas kernels, pair_sums(): pl.pallas_call(functools.partial(pair_kernel, cols, total_flows, total_re...  17.9 us
    all_to_all x2, starting transfers between devices, trade(): return lax.all_to_all(x, axis, 0, 0, axis_index_groups=groups, tiled=True)  13.1 us
    pallas_call x2, Pallas kernels, row_stats(): pl.pallas_call(stat_kernel, grid=(count,), out_shape=[jax.ShapeDtypeStruc...  9.21 us
    ppermute x5, waiting for transfers between devices, swap_sum(): lax.ppermute(x, axis, [(i, i ^ hop) for i in range(count)])  8.84 us
    pallas_call x5, Pallas kernels, call_once(): pl.pallas_call(kernel, grid=(1,), out_shape=[jax.ShapeDtypeStruct(s, f32)...  7.7 us
    all_to_all x2, waiting for transfers between devices, trade(): return lax.all_to_all(x, axis, 0, 0, axis_index_groups=groups, tiled=True)  6.26 us
    ppermute x5, starting transfers between devices, swap_sum(): lax.ppermute(x, axis, [(i, i ^ hop) for i in range(count)])  5.72 us
  transfers between devices with their start and end apart: 8, of which 8 were waited for; matrix products, arithmetic and copies ran while one was open for 0% of the time, Pallas kernels for 8%

profile of v3, /device:TPU:0, one launch (start us, length us, event | category | flops | bytes accessed | tf_op | source)
XLA Modules:
  0.0 116.6 jit_solution(14427624134124669446)
XLA Ops:
  0.6 0.0 copy-start.3
  0.6 5.7 %shard_map.59 = (f32[256,256]{1,0:T(8,128)}, f32[64,256]{1,0:T(8,128)}, f32[64,256]{1,0:T(8,128)}) custom-call(s32[1]{0:T(128)} %bitcast.first_ref, f32[64,256]{1,0:T(8,128)} %bitcast.9, f32[256,256]{1,0:T(8,128)} %hid_ref.3, s32[1,256]{1,0:T(1,128)} %bitcast.10), custom_call_target="tpu_custom_call" | custom-call | tf_op jit(solution)/shard_map/pallas_call | solution.py:39
  6.4 6.4 %all-to-all-start = ((f32[8,32,256]{2,1,0:T(8,128)}), f32[8,32,256]{2,1,0:T(8,128)S(1)}, u32[]{:S(2)}, u32[]{:S(2)}) async-start(f32[8,32,256]{2,1,0:T(8,128)} %bitcast.8), calls=%async_computation | async-start | bytes 524288 | tf_op jit(solution)/shard_map/all_to_all | solution.py:405
  12.8 4.6 %shard_map.60 = (f32[16,256]{1,0:T(8,128)S(1)}, f32[8,8192]{1,0:T(8,128)S(1)}) custom-call(f32[16384,256]{1,0:T(8,128)} %rows_ref.3), custom_call_target="tpu_custom_call" | custom-call | flops 33554432 | bytes 8388608 | tf_op jit(solution)/shard_map/pallas_call | solution.py:157
  17.4 0.0 copy-done.3
  17.4 0.1 dynamic-slice_bitcast_fusion
  17.5 0.1 copy.6.len_ref
  17.6 2.4 %all-to-all-done.parts_ref = f32[8,32,256]{2,1,0:T(8,128)S(1)} async-done(((f32[8,32,256]{2,1,0:T(8,128)}), f32[8,32,256]{2,1,0:T(8,128)S(1)}, u32[]{:S(2)}, u32[]{:S(2)}) %all-to-all-start) | async-done | bytes 262176 | tf_op jit(solution)/shard_map/all_to_all | solution.py:405
  20.0 0.8 shard_map.61.own_ref
  20.8 6.6 %all-to-all-start.1 = ((f32[8,32,256]{2,1,0:T(8,128)}), f32[8,32,256]{2,1,0:T(8,128)S(1)}, u32[]{:S(2)}, u32[]{:S(2)}) async-start(f32[8,32,256]{2,1,0:T(8,128)} %shard_map.61.own_ref), calls=%async_computation.1 | async-start | bytes 524288 | tf_op jit(solution)/shard_map/all_to_all | solution.py:405
  27.4 4.6 %shard_map.62 = (f32[16,256]{1,0:T(8,128)S(1)}, f32[8,8192]{1,0:T(8,128)S(1)}) custom-call(f32[16384,256]{1,0:T(8,128)} %rows_ref.3), custom_call_target="tpu_custom_call" | custom-call | flops 33554432 | bytes 8388608 | tf_op jit(solution)/shard_map/pallas_call | solution.py:157
  32.1 0.0 copy-start
  32.1 0.0 copy-start.1
  32.1 0.0 copy-start.2
  32.1 3.8 %all-to-all-done.1.others_ref = f32[8,32,256]{2,1,0:T(8,128)S(1)} async-done(((f32[8,32,256]{2,1,0:T(8,128)}), f32[8,32,256]{2,1,0:T(8,128)S(1)}, u32[]{:S(2)}, u32[]{:S(2)}) %all-to-all-start.1) | async-done | bytes 262176 | tf_op jit(solution)/shard_map/all_to_all | solution.py:405
  35.9 0.0 collective-permute-start
  35.9 1.5 %collective-permute-done.more_ref = f32[8,32,256]{2,1,0:T(8,128)S(1)} collective-permute-done((f32[8,32,256]{2,1,0:T(8,128)S(1)}, f32[8,32,256]{2,1,0:T(8,128)S(1)}, u32[]{:S(2)}, u32[]{:S(2)}) %collective-permute-start) | collective-permute-done | bytes 262176 | tf_op jit(solution)/shard_map/ppermute | solution.py:434
  37.4 1.1 shard_map.63
  38.5 11.1 %all_to_all.30.hall_ref = f32[8,40,256]{2,1,0:T(8,128)S(1)} all-to-all(f32[8,40,256]{2,1,0:T(8,128)S(1)} %shard_map.63), channel_id=1, replica_groups=mesh['real'=8,'gen'=16] {'real'}, dimensions={0} | all-to-all | bytes 655360 | tf_op jit(solution)/shard_map/all_to_all | solution.py:405
  49.5 17.9 %shard_map.64 = f32[8,40,256]{2,1,0:T(8,128)S(1)} custom-call(f32[8,40,256]{2,1,0:T(8,128)S(1)} %all_to_all.30.hall_ref, f32[8,32,256]{2,1,0:T(8,128)S(1)} %all-to-all-done.1.others_ref, f32[8,32,256]{2,1,0:T(8,128)S(1)} %collective-permute-done.more_ref, f32[16384,256]{1,0:T(8,128)} %rows_ref.3, f32[8,8192]{1,0:T(8,128)S(1)} %get-tuple-element.30.front_ref, ...), custom_call_target="tpu_custom_call" | custom-call | flops 6442450944 | bytes 16777216 | tf_op jit(solution)/shard_map/pallas_call | solution.py:346
  67.4 10.4 %all_to_all.31.parts_ref = f32[8,40,256]{2,1,0:T(8,128)S(1)} all-to-all(f32[8,40,256]{2,1,0:T(8,128)S(1)} %shard_map.64), channel_id=1, replica_groups=mesh['real'=8,'gen'=16] {'real'}, dimensions={0} | all-to-all | bytes 655360 | tf_op jit(solution)/shard_map/all_to_all | solution.py:405
  77.8 10.2 %all_to_all.32.gh_ref = f32[8,40,256]{2,1,0:T(8,128)S(1)} all-to-all(f32[8,40,256]{2,1,0:T(8,128)S(1)} %shard_map.65), channel_id=1, replica_groups=mesh['real'=8,'gen'=16] {'real'}, dimensions={0} | all-to-all | bytes 655360 | tf_op jit(solution)/shard_map/all_to_all | solution.py:405
  88.0 0.0 copy-done
  88.0 0.0 copy-done.1
  88.0 0.0 copy-done.2
  88.0 4.5 %shard_map.66 = f32[72,256]{1,0:T(8,128)S(1)} custom-call(f32[8,40,256]{2,1,0:T(8,128)S(1)} %all_to_all.32.gh_ref, f32[64,256]{1,0:T(8,128)S(1)} %copy-done.1, f32[64,256]{1,0:T(8,128)S(1)} %copy-done.2, f32[256,256]{1,0:T(8,128)S(1)} %copy-done), custom_call_target="tpu_custom_call" | custom-call | tf_op jit(solution)/shard_map/pallas_call | solution.py:114
  92.5 0.1 collective-permute-start.1
  92.6 1.3 %collective-permute-done.1 = f32[72,256]{1,0:T(8,128)S(1)} collective-permute-done((f32[72,256]{1,0:T(8,128)S(1)}, f32[72,256]{1,0:T(8,128)S(1)}, u32[]{:S(2)}, u32[]{:S(2)}) %collective-permute-start.1) | collective-permute-done | bytes 73760 | tf_op jit(solution)/shard_map/ppermute | solution.py:398
  93.8 1.5 %collective-permute-start.2 = (f32[72,256]{1,0:T(8,128)S(1)}, f32[72,256]{1,0:T(8,128)S(1)}, u32[]{:S(2)}, u32[]{:S(2)}) collective-permute-start(f32[72,256]{1,0:T(8,128)S(1)} %add.19), channel_id=1, source_target_pairs={{0,2},{1,3},{2,0},{3,1},{4,6},{5,7},{6,4},{7,5},{8,10},{9,11},{10,... | collective-permute-start | bytes 221192 | tf_op jit(solution)/shard_map/ppermute | solution.py:398
  95.3 4.5 %collective-permute-done.2 = f32[72,256]{1,0:T(8,128)S(1)} collective-permute-done((f32[72,256]{1,0:T(8,128)S(1)}, f32[72,256]{1,0:T(8,128)S(1)}, u32[]{:S(2)}, u32[]{:S(2)}) %collective-permute-start.2) | collective-permute-done | bytes 73760 | tf_op jit(solution)/shard_map/ppermute | solution.py:398
  99.8 1.1 collective-permute-start.5
  100.8 1.3 %collective-permute-start.4 = (f32[72,256]{1,0:T(8,128)S(1)}, f32[72,256]{1,0:T(8,128)S(1)}, u32[]{:S(2)}, u32[]{:S(2)}) collective-permute-start(f32[72,256]{1,0:T(8,128)S(1)} %add.20), channel_id=1, source_target_pairs={{0,8},{1,9},{2,10},{3,11},{4,12},{5,13},{6,14},{7,15},{8,0},{9,1},... | collective-permute-start | bytes 221192 | tf_op jit(solution)/shard_map/ppermute | solution.py:398
  102.2 1.8 %collective-permute-start.3 = (f32[72,256]{1,0:T(8,128)S(1)}, f32[72,256]{1,0:T(8,128)S(1)}, u32[]{:S(2)}, u32[]{:S(2)}) collective-permute-start(f32[72,256]{1,0:T(8,128)S(1)} %add.20), channel_id=1, source_target_pairs={{0,4},{1,5},{2,6},{3,7},{4,0},{5,1},{6,2},{7,3},{8,12},{9,13},{10,... | collective-permute-start | bytes 221192 | tf_op jit(solution)/shard_map/ppermute | solution.py:398
  104.0 1.5 %collective-permute-done.5 = f32[72,256]{1,0:T(8,128)S(1)} collective-permute-done((f32[72,256]{1,0:T(8,128)S(1)}, f32[72,256]{1,0:T(8,128)S(1)}, u32[]{:S(2)}, u32[]{:S(2)}) %collective-permute-start.5) | collective-permute-done | bytes 73760 | tf_op jit(solution)/shard_map/ppermute | solution.py:398
  105.4 1.3 %collective-permute-done.4 = f32[72,256]{1,0:T(8,128)S(1)} collective-permute-done((f32[72,256]{1,0:T(8,128)S(1)}, f32[72,256]{1,0:T(8,128)S(1)}, u32[]{:S(2)}, u32[]{:S(2)}) %collective-permute-start.4) | collective-permute-done | bytes 73760 | tf_op jit(solution)/shard_map/ppermute | solution.py:398
  106.7 0.4 collective-permute-done.3
  107.1 0.1 shard_map.67
  107.2 8.7 %all_to_all.33.sq_ref = f32[8,8,128]{2,1,0:T(8,128)S(1)} all-to-all(f32[8,8,128]{2,1,0:T(8,128)S(1)} %shard_map.67), channel_id=1, replica_groups=mesh['real'=8,'gen'=16] {'real'}, dimensions={0} | all-to-all | bytes 65536 | tf_op jit(solution)/shard_map/all_to_all | solution.py:405
  115.9 0.7 shard_map.68
  (4 shorter events, 0.1 us)
Async XLA Ops:
  0.6 16.8 %copy-start.3 = (s32[256]{0:T(256)S(1)}, s32[256]{0:T(256)}, u32[]{:S(2)}) copy-start(s32[256]{0:T(256)} %param.6) | copy-start | bytes 3076
  6.4 13.6 %all-to-all-start = ((f32[8,32,256]{2,1,0:T(8,128)}), f32[8,32,256]{2,1,0:T(8,128)S(1)}, u32[]{:S(2)}, u32[]{:S(2)}) async-start(f32[8,32,256]{2,1,0:T(8,128)} %bitcast.8), calls=%async_computation | async-start | bytes 524288 | tf_op jit(solution)/shard_map/all_to_all | solution.py:405
  20.8 15.1 %all-to-all-start.1 = ((f32[8,32,256]{2,1,0:T(8,128)}), f32[8,32,256]{2,1,0:T(8,128)S(1)}, u32[]{:S(2)}, u32[]{:S(2)}) async-start(f32[8,32,256]{2,1,0:T(8,128)} %shard_map.61.own_ref), calls=%async_computation.1 | async-start | bytes 524288 | tf_op jit(solution)/shard_map/all_to_all | solution.py:405
  32.1 55.9 %copy-start = (f32[256,256]{1,0:T(8,128)S(1)}, f32[256,256]{1,0:T(8,128)}, u32[]{:S(2)}) copy-start(f32[256,256]{1,0:T(8,128)} %hid_ref.3) | copy-start | bytes 786436
  32.1 55.9 %copy-start.1 = (f32[64,256]{1,0:T(8,128)S(1)}, f32[64,256]{1,0:T(8,128)}, u32[]{:S(2)}) copy-start(f32[64,256]{1,0:T(8,128)} %get-tuple-element.32.val_ref) | copy-start | bytes 196612
  32.1 55.9 %copy-start.2 = (f32[64,256]{1,0:T(8,128)S(1)}, f32[64,256]{1,0:T(8,128)}, u32[]{:S(2)}) copy-start(f32[64,256]{1,0:T(8,128)} %get-tuple-element.33.sig_ref) | copy-start | bytes 196612
  35.9 1.5 %collective-permute-start = (f32[8,32,256]{2,1,0:T(8,128)S(1)}, f32[8,32,256]{2,1,0:T(8,128)S(1)}, u32[]{:S(2)}, u32[]{:S(2)}) collective-permute-start(f32[8,32,256]{2,1,0:T(8,128)S(1)} %all-to-all-done.1.others_ref), channel_id=1, source_target_pairs={{0,1},{1,0},{2,3},{3,2},{4,5},{5,4},{6,7},{7,6},{8,9},{9,8},{10,11... | collective-permute-start | bytes 786440 | tf_op jit(solution)/shard_map/ppermute | solution.py:434
  92.5 1.3 %collective-permute-start.1 = (f32[72,256]{1,0:T(8,128)S(1)}, f32[72,256]{1,0:T(8,128)S(1)}, u32[]{:S(2)}, u32[]{:S(2)}) collective-permute-start(f32[72,256]{1,0:T(8,128)S(1)} %shard_map.66), channel_id=1, source_target_pairs={{0,1},{1,0},{2,3},{3,2},{4,5},{5,4},{6,7},{7,6},{8,9},{9,8},{10,11... | collective-permute-start | bytes 221192 | tf_op jit(solution)/shard_map/ppermute | solution.py:398
  93.8 5.9 %collective-permute-start.2 = (f32[72,256]{1,0:T(8,128)S(1)}, f32[72,256]{1,0:T(8,128)S(1)}, u32[]{:S(2)}, u32[]{:S(2)}) collective-permute-start(f32[72,256]{1,0:T(8,128)S(1)} %add.19), channel_id=1, source_target_pairs={{0,2},{1,3},{2,0},{3,1},{4,6},{5,7},{6,4},{7,5},{8,10},{9,11},{10,... | collective-permute-start | bytes 221192 | tf_op jit(solution)/shard_map/ppermute | solution.py:398
  99.8 5.6 %collective-permute-start.5 = (f32[72,256]{1,0:T(8,128)S(1)}, f32[72,256]{1,0:T(8,128)S(1)}, u32[]{:S(2)}, u32[]{:S(2)}) collective-permute-start(f32[72,256]{1,0:T(8,128)S(1)} %add.20), channel_id=1, source_target_pairs={{0,12},{1,13},{2,14},{3,15},{4,8},{5,9},{6,10},{7,11},{8,4},{9,5},... | collective-permute-start | bytes 221192 | tf_op jit(solution)/shard_map/ppermute | solution.py:398
  100.8 5.9 %collective-permute-start.4 = (f32[72,256]{1,0:T(8,128)S(1)}, f32[72,256]{1,0:T(8,128)S(1)}, u32[]{:S(2)}, u32[]{:S(2)}) collective-permute-start(f32[72,256]{1,0:T(8,128)S(1)} %add.20), channel_id=1, source_target_pairs={{0,8},{1,9},{2,10},{3,11},{4,12},{5,13},{6,14},{7,15},{8,0},{9,1},... | collective-permute-start | bytes 221192 | tf_op jit(solution)/shard_map/ppermute | solution.py:398
  102.2 4.9 %collective-permute-start.3 = (f32[72,256]{1,0:T(8,128)S(1)}, f32[72,256]{1,0:T(8,128)S(1)}, u32[]{:S(2)}, u32[]{:S(2)}) collective-permute-start(f32[72,256]{1,0:T(8,128)S(1)} %add.20), channel_id=1, source_target_pairs={{0,4},{1,5},{2,6},{3,7},{4,0},{5,1},{6,2},{7,3},{8,12},{9,13},{10,... | collective-permute-start | bytes 221192 | tf_op jit(solution)/shard_map/ppermute | solution.py:398

commit v4 on v3

--- a/solution.py
+++ b/solution.py
@@ -17,6 +17,8 @@
 STEP = UNIT * SPACING
 FAR = 1.0e6
 EXTRA = 8
+ROOT_2 = math.sqrt(1.0 / 2.0)
+ROOT_8 = math.sqrt(1.0 / 8.0)
 
 highest = lax.Precision.HIGHEST
 f32 = jnp.float32
@@ -29,6 +31,10 @@
 
 def params(limit=48 << 20):
     return pltpu.CompilerParams(vmem_limit_bytes=limit)
+
+
+def whole():
+    return pl.BlockSpec(memory_space=VMEM)
 
 
 def fixed(shape):
@@ -173,6 +179,25 @@
     )(rows)
 
 
+def near_kernel(rows_ref, out_ref):
+    out_ref[...] = rows_ref[...].astype(bf16)
+
+
+def near_rows_of(rows, block, count):
+    w = rows.shape[1]
+    return pl.pallas_call(
+        near_kernel,
+        grid=(count,),
+        out_shape=jax.ShapeDtypeStruct((count * block, w), bf16),
+        in_specs=[pl.BlockSpec((block, w), lambda i: (i, 0))],
+        out_specs=pl.BlockSpec((block, w), lambda i: (i, 0)),
+        compiler_params=params(),
+        cost_estimate=pl.CostEstimate(
+            flops=count * block * w, bytes_accessed=4 * count * block * w, transcendentals=0
+        ),
+    )(rows)
+
+
 def share_kernel(parts_ref, len_ref, out_ref):
     count = jnp.sum(parts_ref[...], 0)
     hist = count / len_ref[...].astype(f32)
@@ -199,15 +224,24 @@
 
 
 def pair_kernel(
-    cols, total_flows, total_real, hall_ref, others_ref, more_ref, rows_ref, front_ref, back_ref, out_ref,
-    rate_ref, h_ref, hc_ref, hs_ref, ip_ref, wh_ref, mat_ref, sum_ref, kacc_ref, near_ref, sq_ref,
+    cols, total_flows, total_real, hall_ref, others_ref, more_ref, front_ref, rows_ref,
+    front_sq_ref, back_sq_ref, out_ref,
+    rate_ref, h_ref, hc_ref, hs_ref, ip_ref, wh_ref, mat_ref, sum_ref, kacc_ref, held_ref, near_ref, sems,
 ):
     parts, tall, width = hall_ref.shape
     share = tall - EXTRA
     flows = parts * share
-
-    @pl.when(pl.program_id(0) == 0)
-    def _():
+    front = front_ref.shape[0]
+    rest = [
+        pltpu.make_async_copy(
+            rows_ref.at[pl.ds(at, at), :], held_ref.at[pl.ds(at - front, at), :], sems.at[c]
+        )
+        for c, at in enumerate((front, 2 * front, 4 * front))
+    ]
+    rest[0].start()
+    rest[1].start()
+
+    def prepare():
         h = jnp.concatenate([hall_ref[p, :share, :] for p in range(parts)], 0)
         h_ref[...] = h
         stats = hall_ref[0, share:, :]
@@ -225,83 +259,111 @@
         hh, hl = split(h * (2.0 * one))
         hc_ref[...] = jnp.concatenate([hh, hl], 1)
         hs_ref[...] = jnp.broadcast_to(
-            jnp.sum(h * h, 1, keepdims=True) * one, hs_ref.shape
+            jnp.sum(h * h, 1, keepdims=True) * one - 1.0, hs_ref.shape
         )
         mat_ref[...] = jnp.zeros_like(mat_ref)
         sum_ref[...] = jnp.zeros_like(sum_ref)
         kacc_ref[...] = jnp.zeros_like(kacc_ref)
 
+    prepare()
     rate = rate_ref[0:1, 0:1]
 
-    def weigh(x, at, kacc):
-        u = jnp.exp2(x)
-        u2 = u * u
-        u4 = u2 * u2
-        u8 = u4 * u4
-        u16 = u8 * u8
-        t4 = u16 + u16 + u8
-        t3 = t4 + t4 + u4
-        t2 = t3 + t3 + u2
-        w = t2 + t2 + u
-        k = (t4 + u16) + (t3 + t2)
-        ws = w[:, 0:128]
-        ks = k[:, 0:128]
-        for q in range(1, w.shape[1] // 128):
-            ws = ws + w[:, 128 * q : 128 * q + 128]
-            ks = ks + k[:, 128 * q : 128 * q + 128]
-        sum_ref[at, :] += ws
-        for q in range(ks.shape[0] // 8):
-            kacc = kacc + ks[8 * q : 8 * q + 8]
-        return w, kacc
-
-    early = pl.program_id(0) < pl.num_programs(0) // 2
-    sq_ref[...] = jnp.where(early, front_ref[0:1, :], back_ref[0:1, :]) * rate
+    def weigh(x, at, sums):
+        a = jnp.exp2(x)
+        a2 = a * a
+        b = a2 * ROOT_2
+        b = b * b
+        c = b * 0.5
+        c = c * c
+        d = c * ROOT_8
+        d = d * d
+        w = (a + a2) + (b + c) + d
+
+        def fold(v):
+            t = v[:, 0:128]
+            for q in range(1, v.shape[1] // 128):
+                t = t + v[:, 128 * q : 128 * q + 128]
+            return t
+
+        sum_ref[at, :] += fold(w)
+        out = []
+        for v, total in zip((a2, b, c, d), sums):
+            t = fold(v)
+            for q in range(t.shape[0] // 8):
+                total = total + t[8 * q : 8 * q + 8]
+            out.append(total)
+        return w, tuple(out)
+
+    early = front // cols
 
     def first(p):
-        r = rows_ref[p * cols : (p + 1) * cols, :].astype(bf16)
-        near_ref[p % 3] = r
+        if p < early:
+            r = front_ref[p * cols : (p + 1) * cols, :]
+        else:
+            r = held_ref[(p - early) * cols : (p - early + 1) * cols, :].astype(bf16)
+            near_ref[p % 3] = r
         ip_ref[p % 2] = dot(hc_ref[...], jnp.concatenate([r, r], 1), NT)
 
-    def second(p, kacc):
-        sq = sq_ref[0:1, p * cols : (p + 1) * cols]
+    def second(p, sums):
+        ref, q = (front_sq_ref, p) if p < 4 * early else (back_sq_ref, p - 4 * early)
+        sq = ref[0:1, q * cols : (q + 1) * cols] * rate
         for c in range(flows // 16):
             at = slice(16 * c, 16 * c + 16)
             x = (ip_ref[p % 2, at, :] - sq) - jnp.tile(hs_ref[at, :], (1, cols // 128))
-            w, kacc = weigh(x, at, kacc)
+            w, sums = weigh(x, at, sums)
             wh_ref[p % 2, at, :] = w.astype(bf16)
-        return kacc
+        return sums
 
     def third(p):
-        mat_ref[...] += dot(wh_ref[p % 2], near_ref[p % 3], NN)
-
-    count = rows_ref.shape[0] // cols
-    kacc = jnp.zeros((8, 128), f32)
+        if p < early:
+            r = front_ref[p * cols : (p + 1) * cols, :]
+        else:
+            r = near_ref[p % 3]
+        mat_ref[...] += dot(wh_ref[p % 2], r, NN)
+
+    def keep(sums):
+        for q in range(4):
+            kacc_ref[8 * q : 8 * q + 8, :] += sums[q]
+
+    zeros = (jnp.zeros((8, 128), f32),) * 4
+    count = early + held_ref.shape[0] // cols
+    sums = zeros
     first(0)
     for p in range(count):
+        if p + 1 == early:
+            rest[0].wait()
+            rest[2].start()
+        if p + 1 == 2 * early:
+            rest[1].wait()
+        if p + 1 == 4 * early:
+            rest[2].wait()
         if p + 1 < count:
             first(p + 1)
-        kacc = second(p, kacc)
+        sums = second(p, sums)
+        if p % 16 == 15:
+            keep(sums)
+            sums = zeros
         if p > 0:
             third(p - 1)
     third(count - 1)
-    kacc_ref[...] += kacc
-
-    @pl.when(pl.program_id(0) == pl.num_programs(0) - 1)
-    def _():
+    keep(sums)
+
+    def complete():
         h = h_ref[...]
 
         def finish(scale):
             total = jnp.sum(sum_ref[...], 1, keepdims=True)
-            grad = (total * h - mat_ref[...]) * (rate * scale)
-            lanes = jnp.sum(sum_ref[...], 0, keepdims=True) - jnp.sum(
-                kacc_ref[...], 0, keepdims=True
-            )
+            grad = (total * h - mat_ref[...]) * (rate * (0.5 * scale))
+            lanes = 0.5 * jnp.sum(sum_ref[...], 0, keepdims=True)
+            for q, part in enumerate((1 / 4, 3 / 8, 7 / 16, 15 / 32)):
+                lanes = lanes - part * jnp.sum(kacc_ref[8 * q : 8 * q + 8, :], 0, keepdims=True)
             return grad, jnp.sum(lanes, 1, keepdims=True)
 
         cross_g, cross_k = finish(4.0 / (total_real * LOG2E))
         mat_ref[...] = jnp.zeros_like(mat_ref)
         sum_ref[...] = jnp.zeros_like(sum_ref)
-        kacc = jnp.zeros((8, 128), f32)
+        kacc_ref[...] = jnp.zeros_like(kacc_ref)
+        sums = zeros
         rows_all = jnp.concatenate(
             [r[...].reshape(-1, width) for r in (others_ref, more_ref)], 0
         )
@@ -315,11 +377,10 @@
                 NT,
             )
             sq = row_squares(rows * rows)[0:1, :] * rate
-            lows = []
             for c in range(flows // 16):
                 at = slice(16 * c, 16 * c + 16)
                 x = (ip_ref[0, at, :] - sq) - jnp.tile(hs_ref[at, :], (1, cols // 128))
-                w, kacc = weigh(x, at, kacc)
+                w, sums = weigh(x, at, sums)
                 wh, wl = split(w)
                 wh_ref[0, at, :] = wh
                 wh_ref[1, at, :] = wl
@@ -327,7 +388,7 @@
             mat_ref[...] += dot(
                 jnp.concatenate([wh, wl, wh], 1), jnp.concatenate([rh, rh, rl], 0), NN
             )
-        kacc_ref[...] = kacc
+        keep(sums)
         pair_g, pair_k = finish(-4.0 / (total_flows * LOG2E))
         grad = cross_g + pair_g
         loss = pair_k / (float(total_flows) * total_flows) - 2.0 * cross_k / (
@@ -338,22 +399,24 @@
             out_ref[p, :share, :] = grad[p * share : (p + 1) * share]
             out_ref[p, share:, :] = line
 
-
-def pair_sums(hall, others, more, rows, front, back, total_flows, total_real, block, cols):
+    complete()
+
+
+def pair_sums(hall, others, more, front, rows, front_sq, back_sq, total_flows, total_real, cols):
     n, w = rows.shape
     flows = hall.shape[0] * (hall.shape[1] - EXTRA)
-    half = n // block // 2
     return pl.pallas_call(
         functools.partial(pair_kernel, cols, total_flows, total_real),
-        grid=(2 * half,),
+        grid=(1,),
         out_shape=jax.ShapeDtypeStruct(hall.shape, f32),
         in_specs=[
             fixed(hall.shape),
             fixed(others.shape),
             fixed(more.shape),
-            pl.BlockSpec((block, w), lambda i: (i, 0)),
-            pl.BlockSpec((8, block), lambda i: (0, jnp.minimum(i, half - 1))),
-            pl.BlockSpec((8, block), lambda i: (0, jnp.maximum(i - half, 0))),
+            whole(),
+            pl.BlockSpec(memory_space=pl.ANY),
+            fixed(front_sq.shape),
+            fixed(back_sq.shape),
         ],
         out_specs=fixed(hall.shape),
         scratch_shapes=[
@@ -365,15 +428,16 @@
             VMEM((2, flows, cols), bf16),
             VMEM((flows, w), f32),
             VMEM((flows, 128), f32),
-            VMEM((8, 128), f32),
+            VMEM((32, 128), f32),
+            VMEM((n - front.shape[0], w), f32),
             VMEM((3, cols, w), bf16),
-            VMEM((1, block), f32),
+            pltpu.SemaphoreType.DMA((3,)),
         ],
         compiler_params=params(),
         cost_estimate=pl.CostEstimate(
             flops=6 * n * w * flows, bytes_accessed=4 * n * w, transcendentals=n * flows
         ),
-    )(hall, others, more, rows, front, back)
+    )(hall, others, more, front, rows, front_sq, back_sq)
 
 
 def sum_kernel(parts_ref, out_ref):
@@ -437,9 +501,12 @@
         [(real_count, share + EXTRA, NUM_BINS)],
         near_rows, far_rows, own, front_sums, back_sums,
     )
+    rows_near, load = lax.optimization_barrier((real_rows, load))
     hall = trade(load, "real")
+    front = near_rows_of(rows_near, real_rows.shape[0] // 8, 1)
+    hall, front = lax.optimization_barrier((hall, front))
     grad_part = pair_sums(
-        hall, near_rows, far_rows, real_rows, front_sq, back_sq, total_flows, total_real, block, 256
+        hall, near_rows, far_rows, front, real_rows, front_sq, back_sq, total_flows, total_real, 256
     )
     (grad_own,) = call_once(sum_kernel, [grad_part.shape], trade(grad_part, "real"))
     part = back_steps(trade(grad_own, "real"), val, sig, hidden)

time: 117 us -> 116 us (level)
  blocking collectives: 40.3 us -> 30 us
  waiting for transfers between devices: 16.6 us -> 23.1 us
  starting transfers between devices: 18.8 us -> 22.2 us
    all_to_all x4 -> x3, blocking collectives: 40.3 us -> 30 us  [trade(): return lax.all_to_all(x, axis, 0, 0, axis_index_groups=groups, tiled=True)]
    all_to_all x2 -> x3, waiting for transfers between devices: 6.26 us -> 12.5 us  [trade(): return lax.all_to_all(x, axis, 0, 0, axis_index_groups=groups, tiled=True)]
    all_to_all x2 -> x3, starting transfers between devices: 13.1 us -> 16.7 us  [trade(): return lax.all_to_all(x, axis, 0, 0, axis_index_groups=groups, tiled=True)]
    pallas_call x1, Pallas kernels: 17.9 us -> 14.4 us  [pair_sums(): pl.pallas_call(functools.partial(pair_kernel, cols, total_flows, total_re...]
    pallas_call x0 -> x1, Pallas kernels: none -> 1.7 us  [near_rows_of(): pl.pallas_call(near_kernel, grid=(count,), out_shape=jax.ShapeDtypeStruct...]
  transfers between devices with their start and end apart: 8 -> 9, of which waited for: 8 -> 9; matrix products, arithmetic and copies ran while one was open for 0% -> 0% of each run, Pallas kernels for 8% -> 9%
where the time goes in v4:
time: 116 us; the launch traced here: 115 us
  Pallas kernels  38.9 us (34%)
  blocking collectives  30 us (26%)
  waiting for transfers between devices  23.1 us (20%)
  starting transfers between devices  22.2 us (19%)
    all_to_all x3, blocking collectives, trade(): return lax.all_to_all(x, axis, 0, 0, axis_index_groups=groups, tiled=True)  30 us
    all_to_all x3, starting transfers between devices, trade(): return lax.all_to_all(x, axis, 0, 0, axis_index_groups=groups, tiled=True)  16.7 us
    pallas_call x1, Pallas kernels, pair_sums(): pl.pallas_call(functools.partial(pair_kernel, cols, total_flows, total_re...  14.4 us
    all_to_all x3, waiting for transfers between devices, trade(): return lax.all_to_all(x, axis, 0, 0, axis_index_groups=groups, tiled=True)  12.5 us
    pallas_call x2, Pallas kernels, row_stats(): pl.pallas_call(stat_kernel, grid=(count,), out_shape=[jax.ShapeDtypeStruc...  9.21 us
    ppermute x5, waiting for transfers between devices, swap_sum(): lax.ppermute(x, axis, [(i, i ^ hop) for i in range(count)])  9.02 us
    pallas_call x5, Pallas kernels, call_once(): pl.pallas_call(kernel, grid=(1,), out_shape=[jax.ShapeDtypeStruct(s, f32)...  8.44 us
    ppermute x5, starting transfers between devices, swap_sum(): lax.ppermute(x, axis, [(i, i ^ hop) for i in range(count)])  5.55 us
  transfers between devices with their start and end apart: 9, of which 9 were waited for; matrix products, arithmetic and copies ran while one was open for 0% of the time, Pallas kernels for 9%

profile of v4, /device:TPU:0, one launch (start us, length us, event | category | flops | bytes accessed | tf_op | source)
XLA Modules:
  0.0 115.3 jit_solution(8886089248569858079)
XLA Ops:
  0.6 0.0 copy-start.3
  0.6 5.7 %shard_map.59 = (f32[256,256]{1,0:T(8,128)}, f32[64,256]{1,0:T(8,128)}, f32[64,256]{1,0:T(8,128)}) custom-call(s32[1]{0:T(128)} %bitcast.first_ref, f32[64,256]{1,0:T(8,128)} %bitcast.9, f32[256,256]{1,0:T(8,128)} %hid_ref.3, s32[1,256]{1,0:T(1,128)} %bitcast.10), custom_call_target="tpu_custom_call" | custom-call | tf_op jit(solution)/shard_map/pallas_call | solution.py:45
  6.4 6.4 %all-to-all-start = ((f32[8,32,256]{2,1,0:T(8,128)}), f32[8,32,256]{2,1,0:T(8,128)S(1)}, u32[]{:S(2)}, u32[]{:S(2)}) async-start(f32[8,32,256]{2,1,0:T(8,128)} %bitcast.8), calls=%async_computation | async-start | bytes 524288 | tf_op jit(solution)/shard_map/all_to_all | solution.py:469
  12.8 4.6 %shard_map.60 = (f32[16,256]{1,0:T(8,128)S(1)}, f32[8,8192]{1,0:T(8,128)S(1)}) custom-call(f32[16384,256]{1,0:T(8,128)} %rows_ref.4), custom_call_target="tpu_custom_call" | custom-call | flops 33554432 | bytes 8388608 | tf_op jit(solution)/shard_map/pallas_call | solution.py:163
  17.4 0.0 copy-done.3
  17.4 0.1 dynamic-slice_bitcast_fusion
  17.5 0.1 copy.6.len_ref
  17.6 2.4 %all-to-all-done.parts_ref = f32[8,32,256]{2,1,0:T(8,128)S(1)} async-done(((f32[8,32,256]{2,1,0:T(8,128)}), f32[8,32,256]{2,1,0:T(8,128)S(1)}, u32[]{:S(2)}, u32[]{:S(2)}) %all-to-all-start) | async-done | bytes 262176 | tf_op jit(solution)/shard_map/all_to_all | solution.py:469
  20.0 0.8 shard_map.61.own_ref
  20.8 6.6 %all-to-all-start.1 = ((f32[8,32,256]{2,1,0:T(8,128)}), f32[8,32,256]{2,1,0:T(8,128)S(1)}, u32[]{:S(2)}, u32[]{:S(2)}) async-start(f32[8,32,256]{2,1,0:T(8,128)} %shard_map.61.own_ref), calls=%async_computation.1 | async-start | bytes 524288 | tf_op jit(solution)/shard_map/all_to_all | solution.py:469
  27.5 4.6 %shard_map.62 = (f32[16,256]{1,0:T(8,128)S(1)}, f32[8,8192]{1,0:T(8,128)S(1)}) custom-call(f32[16384,256]{1,0:T(8,128)} %rows_ref.4), custom_call_target="tpu_custom_call" | custom-call | flops 33554432 | bytes 8388608 | tf_op jit(solution)/shard_map/pallas_call | solution.py:163
  32.1 3.8 %all-to-all-done.1.others_ref = f32[8,32,256]{2,1,0:T(8,128)S(1)} async-done(((f32[8,32,256]{2,1,0:T(8,128)}), f32[8,32,256]{2,1,0:T(8,128)S(1)}, u32[]{:S(2)}, u32[]{:S(2)}) %all-to-all-start.1) | async-done | bytes 262176 | tf_op jit(solution)/shard_map/all_to_all | solution.py:469
  35.9 0.0 collective-permute-start
  35.9 1.5 %collective-permute-done.more_ref = f32[8,32,256]{2,1,0:T(8,128)S(1)} collective-permute-done((f32[8,32,256]{2,1,0:T(8,128)S(1)}, f32[8,32,256]{2,1,0:T(8,128)S(1)}, u32[]{:S(2)}, u32[]{:S(2)}) %collective-permute-start) | collective-permute-done | bytes 262176 | tf_op jit(solution)/shard_map/ppermute | solution.py:498
  37.4 1.8 %shard_map.63 = f32[8,40,256]{2,1,0:T(8,128)} custom-call(f32[8,32,256]{2,1,0:T(8,128)S(1)} %all-to-all-done.1.others_ref, f32[8,32,256]{2,1,0:T(8,128)S(1)} %collective-permute-done.more_ref, f32[8,32,256]{2,1,0:T(8,128)} %shard_map.61.own_ref, f32[16,256]{1,0:T(8,128)S(1)} %get-tuple-element.32.front_ref, f32[16,256]{1,0:T(8,128)S(1)} %get-tuple-element.33.back_ref), custom_call_target="tpu_custom_call" | custom-call | tf_op jit(solution)/shard_map/pallas_call | solution.py:45
  39.2 3.6 %all-to-all-start.2 = ((f32[8,40,256]{2,1,0:T(8,128)}), f32[8,40,256]{2,1,0:T(8,128)S(1)}, u32[]{:S(2)}, u32[]{:S(2)}) async-start(f32[8,40,256]{2,1,0:T(8,128)} %shard_map.63), calls=%async_computation.2 | async-start | bytes 655360 | tf_op jit(solution)/shard_map/all_to_all | solution.py:469
  42.8 1.7 %shard_map.64.front_ref = bf16[2048,256]{1,0:T(8,128)(2,1)S(1)} custom-call(f32[16384,256]{1,0:T(8,128)} %rows_ref.4), custom_call_target="tpu_custom_call" | custom-call | flops 524288 | bytes 2097152 | tf_op jit(solution)/shard_map/pallas_call | solution.py:188
  44.5 0.0 copy-start
  44.5 0.0 copy-start.1
  44.5 0.0 copy-start.2
  44.6 6.2 %all-to-all-done.2.hall_ref = f32[8,40,256]{2,1,0:T(8,128)S(1)} async-done(((f32[8,40,256]{2,1,0:T(8,128)}), f32[8,40,256]{2,1,0:T(8,128)S(1)}, u32[]{:S(2)}, u32[]{:S(2)}) %all-to-all-start.2) | async-done | bytes 327712 | tf_op jit(solution)/shard_map/all_to_all | solution.py:469
  50.8 14.4 %shard_map.65 = f32[8,40,256]{2,1,0:T(8,128)S(1)} custom-call(f32[8,40,256]{2,1,0:T(8,128)S(1)} %all-to-all-done.2.hall_ref, f32[8,32,256]{2,1,0:T(8,128)S(1)} %all-to-all-done.1.others_ref, f32[8,32,256]{2,1,0:T(8,128)S(1)} %collective-permute-done.more_ref, bf16[2048,256]{1,0:T(8,128)(2,1)S(1)} %shard_map.64.front_ref, f32[16384,256]{1,0:T(8,128)} %rows_ref.4, ...), custom_call_target="tpu_custom_call" | custom-call | flops 6442450944 | bytes 16777216 | tf_op jit(solution)/shard_map/pallas_call | solution.py:408
  65.1 11.1 %all_to_all.30.parts_ref = f32[8,40,256]{2,1,0:T(8,128)S(1)} all-to-all(f32[8,40,256]{2,1,0:T(8,128)S(1)} %shard_map.65), channel_id=1, replica_groups=mesh['real'=8,'gen'=16] {'real'}, dimensions={0} | all-to-all | bytes 655360 | tf_op jit(solution)/shard_map/all_to_all | solution.py:469
  76.3 10.2 %all_to_all.31.gh_ref = f32[8,40,256]{2,1,0:T(8,128)S(1)} all-to-all(f32[8,40,256]{2,1,0:T(8,128)S(1)} %shard_map.66), channel_id=1, replica_groups=mesh['real'=8,'gen'=16] {'real'}, dimensions={0} | all-to-all | bytes 655360 | tf_op jit(solution)/shard_map/all_to_all | solution.py:469
  86.5 0.0 copy-done
  86.5 0.0 copy-done.1
  86.5 0.0 copy-done.2
  86.5 4.5 %shard_map.67 = f32[72,256]{1,0:T(8,128)S(1)} custom-call(f32[8,40,256]{2,1,0:T(8,128)S(1)} %all_to_all.31.gh_ref, f32[64,256]{1,0:T(8,128)S(1)} %copy-done.1, f32[64,256]{1,0:T(8,128)S(1)} %copy-done.2, f32[256,256]{1,0:T(8,128)S(1)} %copy-done), custom_call_target="tpu_custom_call" | custom-call | tf_op jit(solution)/shard_map/pallas_call | solution.py:120
  91.0 0.1 collective-permute-start.1
  91.1 1.3 %collective-permute-done.1 = f32[72,256]{1,0:T(8,128)S(1)} collective-permute-done((f32[72,256]{1,0:T(8,128)S(1)}, f32[72,256]{1,0:T(8,128)S(1)}, u32[]{:S(2)}, u32[]{:S(2)}) %collective-permute-start.1) | collective-permute-done | bytes 73760 | tf_op jit(solution)/shard_map/ppermute | solution.py:462
  92.3 1.3 %collective-permute-start.2 = (f32[72,256]{1,0:T(8,128)S(1)}, f32[72,256]{1,0:T(8,128)S(1)}, u32[]{:S(2)}, u32[]{:S(2)}) collective-permute-start(f32[72,256]{1,0:T(8,128)S(1)} %add.19), channel_id=1, source_target_pairs={{0,2},{1,3},{2,0},{3,1},{4,6},{5,7},{6,4},{7,5},{8,10},{9,11},{10,... | collective-permute-start | bytes 221192 | tf_op jit(solution)/shard_map/ppermute | solution.py:462
  93.6 4.6 %collective-permute-done.2 = f32[72,256]{1,0:T(8,128)S(1)} collective-permute-done((f32[72,256]{1,0:T(8,128)S(1)}, f32[72,256]{1,0:T(8,128)S(1)}, u32[]{:S(2)}, u32[]{:S(2)}) %collective-permute-start.2) | collective-permute-done | bytes 73760 | tf_op jit(solution)/shard_map/ppermute | solution.py:462
  98.3 1.2 %collective-permute-start.5 = (f32[72,256]{1,0:T(8,128)S(1)}, f32[72,256]{1,0:T(8,128)S(1)}, u32[]{:S(2)}, u32[]{:S(2)}) collective-permute-start(f32[72,256]{1,0:T(8,128)S(1)} %add.20), channel_id=1, source_target_pairs={{0,12},{1,13},{2,14},{3,15},{4,8},{5,9},{6,10},{7,11},{8,4},{9,5},... | collective-permute-start | bytes 221192 | tf_op jit(solution)/shard_map/ppermute | solution.py:462
  99.5 1.2 %collective-permute-start.4 = (f32[72,256]{1,0:T(8,128)S(1)}, f32[72,256]{1,0:T(8,128)S(1)}, u32[]{:S(2)}, u32[]{:S(2)}) collective-permute-start(f32[72,256]{1,0:T(8,128)S(1)} %add.20), channel_id=1, source_target_pairs={{0,8},{1,9},{2,10},{3,11},{4,12},{5,13},{6,14},{7,15},{8,0},{9,1},... | collective-permute-start | bytes 221192 | tf_op jit(solution)/shard_map/ppermute | solution.py:462
  100.7 1.8 %collective-permute-start.3 = (f32[72,256]{1,0:T(8,128)S(1)}, f32[72,256]{1,0:T(8,128)S(1)}, u32[]{:S(2)}, u32[]{:S(2)}) collective-permute-start(f32[72,256]{1,0:T(8,128)S(1)} %add.20), channel_id=1, source_target_pairs={{0,4},{1,5},{2,6},{3,7},{4,0},{5,1},{6,2},{7,3},{8,12},{9,13},{10,... | collective-permute-start | bytes 221192 | tf_op jit(solution)/shard_map/ppermute | solution.py:462
  102.5 1.5 %collective-permute-done.5 = f32[72,256]{1,0:T(8,128)S(1)} collective-permute-done((f32[72,256]{1,0:T(8,128)S(1)}, f32[72,256]{1,0:T(8,128)S(1)}, u32[]{:S(2)}, u32[]{:S(2)}) %collective-permute-start.5) | collective-permute-done | bytes 73760 | tf_op jit(solution)/shard_map/ppermute | solution.py:462
  103.9 1.4 %collective-permute-done.4 = f32[72,256]{1,0:T(8,128)S(1)} collective-permute-done((f32[72,256]{1,0:T(8,128)S(1)}, f32[72,256]{1,0:T(8,128)S(1)}, u32[]{:S(2)}, u32[]{:S(2)}) %collective-permute-start.4) | collective-permute-done | bytes 73760 | tf_op jit(solution)/shard_map/ppermute | solution.py:462
  105.3 0.2 collective-permute-done.3
  105.6 0.1 shard_map.68
  105.7 8.7 %all_to_all.32.sq_ref = f32[8,8,128]{2,1,0:T(8,128)S(1)} all-to-all(f32[8,8,128]{2,1,0:T(8,128)S(1)} %shard_map.68), channel_id=1, replica_groups=mesh['real'=8,'gen'=16] {'real'}, dimensions={0} | all-to-all | bytes 65536 | tf_op jit(solution)/shard_map/all_to_all | solution.py:469
  114.4 0.7 shard_map.69
  (4 shorter events, 0.1 us)
Async XLA Ops:
  0.6 16.8 %copy-start.3 = (s32[256]{0:T(256)S(1)}, s32[256]{0:T(256)}, u32[]{:S(2)}) copy-start(s32[256]{0:T(256)} %param.6) | copy-start | bytes 3076
  6.4 13.6 %all-to-all-start = ((f32[8,32,256]{2,1,0:T(8,128)}), f32[8,32,256]{2,1,0:T(8,128)S(1)}, u32[]{:S(2)}, u32[]{:S(2)}) async-start(f32[8,32,256]{2,1,0:T(8,128)} %bitcast.8), calls=%async_computation | async-start | bytes 524288 | tf_op jit(solution)/shard_map/all_to_all | solution.py:469
  20.8 15.1 %all-to-all-start.1 = ((f32[8,32,256]{2,1,0:T(8,128)}), f32[8,32,256]{2,1,0:T(8,128)S(1)}, u32[]{:S(2)}, u32[]{:S(2)}) async-start(f32[8,32,256]{2,1,0:T(8,128)} %shard_map.61.own_ref), calls=%async_computation.1 | async-start | bytes 524288 | tf_op jit(solution)/shard_map/all_to_all | solution.py:469
  35.9 1.5 %collective-permute-start = (f32[8,32,256]{2,1,0:T(8,128)S(1)}, f32[8,32,256]{2,1,0:T(8,128)S(1)}, u32[]{:S(2)}, u32[]{:S(2)}) collective-permute-start(f32[8,32,256]{2,1,0:T(8,128)S(1)} %all-to-all-done.1.others_ref), channel_id=1, source_target_pairs={{0,1},{1,0},{2,3},{3,2},{4,5},{5,4},{6,7},{7,6},{8,9},{9,8},{10,11... | collective-permute-start | bytes 786440 | tf_op jit(solution)/shard_map/ppermute | solution.py:498
  39.2 11.6 %all-to-all-start.2 = ((f32[8,40,256]{2,1,0:T(8,128)}), f32[8,40,256]{2,1,0:T(8,128)S(1)}, u32[]{:S(2)}, u32[]{:S(2)}) async-start(f32[8,40,256]{2,1,0:T(8,128)} %shard_map.63), calls=%async_computation.2 | async-start | bytes 655360 | tf_op jit(solution)/shard_map/all_to_all | solution.py:469
  44.5 42.0 %copy-start = (f32[256,256]{1,0:T(8,128)S(1)}, f32[256,256]{1,0:T(8,128)}, u32[]{:S(2)}) copy-start(f32[256,256]{1,0:T(8,128)} %hid_ref.3) | copy-start | bytes 786436
  44.5 42.0 %copy-start.1 = (f32[64,256]{1,0:T(8,128)S(1)}, f32[64,256]{1,0:T(8,128)}, u32[]{:S(2)}) copy-start(f32[64,256]{1,0:T(8,128)} %get-tuple-element.40.val_ref) | copy-start | bytes 196612
  44.5 41.9 %copy-start.2 = (f32[64,256]{1,0:T(8,128)S(1)}, f32[64,256]{1,0:T(8,128)}, u32[]{:S(2)}) copy-start(f32[64,256]{1,0:T(8,128)} %get-tuple-element.41.sig_ref) | copy-start | bytes 196612
  91.0 1.3 %collective-permute-start.1 = (f32[72,256]{1,0:T(8,128)S(1)}, f32[72,256]{1,0:T(8,128)S(1)}, u32[]{:S(2)}, u32[]{:S(2)}) collective-permute-start(f32[72,256]{1,0:T(8,128)S(1)} %shard_map.67), channel_id=1, source_target_pairs={{0,1},{1,0},{2,3},{3,2},{4,5},{5,4},{6,7},{7,6},{8,9},{9,8},{10,11... | collective-permute-start | bytes 221192 | tf_op jit(solution)/shard_map/ppermute | solution.py:462
  92.3 5.9 %collective-permute-start.2 = (f32[72,256]{1,0:T(8,128)S(1)}, f32[72,256]{1,0:T(8,128)S(1)}, u32[]{:S(2)}, u32[]{:S(2)}) collective-permute-start(f32[72,256]{1,0:T(8,128)S(1)} %add.19), channel_id=1, source_target_pairs={{0,2},{1,3},{2,0},{3,1},{4,6},{5,7},{6,4},{7,5},{8,10},{9,11},{10,... | collective-permute-start | bytes 221192 | tf_op jit(solution)/shard_map/ppermute | solution.py:462
  98.3 5.6 %collective-permute-start.5 = (f32[72,256]{1,0:T(8,128)S(1)}, f32[72,256]{1,0:T(8,128)S(1)}, u32[]{:S(2)}, u32[]{:S(2)}) collective-permute-start(f32[72,256]{1,0:T(8,128)S(1)} %add.20), channel_id=1, source_target_pairs={{0,12},{1,13},{2,14},{3,15},{4,8},{5,9},{6,10},{7,11},{8,4},{9,5},... | collective-permute-start | bytes 221192 | tf_op jit(solution)/shard_map/ppermute | solution.py:462
  99.5 5.9 %collective-permute-start.4 = (f32[72,256]{1,0:T(8,128)S(1)}, f32[72,256]{1,0:T(8,128)S(1)}, u32[]{:S(2)}, u32[]{:S(2)}) collective-permute-start(f32[72,256]{1,0:T(8,128)S(1)} %add.20), channel_id=1, source_target_pairs={{0,8},{1,9},{2,10},{3,11},{4,12},{5,13},{6,14},{7,15},{8,0},{9,1},... | collective-permute-start | bytes 221192 | tf_op jit(solution)/shard_map/ppermute | solution.py:462
  100.7 4.9 %collective-permute-start.3 = (f32[72,256]{1,0:T(8,128)S(1)}, f32[72,256]{1,0:T(8,128)S(1)}, u32[]{:S(2)}, u32[]{:S(2)}) collective-permute-start(f32[72,256]{1,0:T(8,128)S(1)} %add.20), channel_id=1, source_target_pairs={{0,4},{1,5},{2,6},{3,7},{4,0},{5,1},{6,2},{7,3},{8,12},{9,13},{10,... | collective-permute-start | bytes 221192 | tf_op jit(solution)/shard_map/ppermute | solution.py:462

commit v5 on v4

--- a/solution.py
+++ b/solution.py
@@ -134,10 +134,17 @@
     return dot(ones, jnp.concatenate([hi, lo], 1), NT)
 
 
-def stat_kernel(rows_ref, sum_ref, sq_ref):
+def stat_kernel(rows_ref, sum_ref, sq_ref, *near_refs):
     rows = rows_ref[...]
     w = rows.shape[1]
-    near = rows.astype(bf16).astype(f32)
+    near = rows.astype(bf16)
+    for ref in near_refs:
+
+        @pl.when(pl.program_id(0) == 0)
+        def _():
+            ref[...] = near[: ref.shape[0]]
+
+    near = near.astype(f32)
     near = near * near
     half = w // 2
     sq_ref[...] = row_squares(near[:, :half] + near[:, half:])
@@ -158,42 +165,26 @@
         sum_ref[...] += part
 
 
-def row_stats(rows, block, start, count):
+def row_stats(rows, block, start, count, near=0):
     w = rows.shape[1]
+    extra = [near] if near else []
     return pl.pallas_call(
         stat_kernel,
         grid=(count,),
         out_shape=[
             jax.ShapeDtypeStruct((16, w), f32),
             jax.ShapeDtypeStruct((8, count * block), f32),
-        ],
+        ]
+        + [jax.ShapeDtypeStruct((n, w), bf16) for n in extra],
         in_specs=[pl.BlockSpec((block, w), lambda i: (start + i, 0))],
         out_specs=[
             fixed((16, w)),
             pl.BlockSpec((8, block), lambda i: (0, i)),
-        ],
+        ]
+        + [fixed((n, w)) for n in extra],
         compiler_params=params(),
         cost_estimate=pl.CostEstimate(
             flops=16 * count * block * w, bytes_accessed=4 * count * block * w, transcendentals=0
-        ),
-    )(rows)
-
-
-def near_kernel(rows_ref, out_ref):
-    out_ref[...] = rows_ref[...].astype(bf16)
-
-
-def near_rows_of(rows, block, count):
-    w = rows.shape[1]
-    return pl.pallas_call(
-        near_kernel,
-        grid=(count,),
-        out_shape=jax.ShapeDtypeStruct((count * block, w), bf16),
-        in_specs=[pl.BlockSpec((block, w), lambda i: (i, 0))],
-        out_specs=pl.BlockSpec((block, w), lambda i: (i, 0)),
-        compiler_params=params(),
-        cost_estimate=pl.CostEstimate(
-            flops=count * block * w, bytes_accessed=4 * count * block * w, transcendentals=0
         ),
     )(rows)
 
@@ -486,7 +477,9 @@
     )
     rows_early, counts = lax.optimization_barrier((real_rows, counts))
     parts = trade(counts.reshape(real_count, share, NUM_BINS), "real")
-    front_sums, front_sq = row_stats(rows_early, block, 0, half)
+    front_sums, front_sq, front = row_stats(
+        rows_early, block, 0, half, real_rows.shape[0] // 8
+    )
     own_len = lax.dynamic_slice_in_dim(lengths, real_index * share, share)[:, None]
     own_len, front_sums = lax.optimization_barrier((own_len, front_sums))
     (own,) = call_once(share_kernel, [(gen_count // 2, share, NUM_BINS)], parts, own_len)
@@ -501,10 +494,7 @@
         [(real_count, share + EXTRA, NUM_BINS)],
         near_rows, far_rows, own, front_sums, back_sums,
     )
-    rows_near, load = lax.optimization_barrier((real_rows, load))
     hall = trade(load, "real")
-    front = near_rows_of(rows_near, real_rows.shape[0] // 8, 1)
-    hall, front = lax.optimization_barrier((hall, front))
     grad_part = pair_sums(
         hall, near_rows, far_rows, front, real_rows, front_sq, back_sq, total_flows, total_real, 256
     )

time: 116 us -> 114 us (0.983)
  blocking collectives: 30 us -> 40.6 us
  waiting for transfers between devices: 23.1 us -> 15.4 us
  starting transfers between devices: 22.2 us -> 19.2 us
  Pallas kernels: 38.9 us -> 37.2 us
    all_to_all x3 -> x4, blocking collectives: 30 us -> 40.6 us  [trade(): return lax.all_to_all(x, axis, 0, 0, axis_index_groups=groups, tiled=True)]
    all_to_all x3 -> x2, waiting for transfers between devices: 12.5 us -> 5.48 us  [trade(): return lax.all_to_all(x, axis, 0, 0, axis_index_groups=groups, tiled=True)]
    all_to_all x3 -> x2, starting transfers between devices: 16.7 us -> 13 us  [trade(): return lax.all_to_all(x, axis, 0, 0, axis_index_groups=groups, tiled=True)]
    pallas_call x1 -> x0, Pallas kernels: 1.7 us -> none  [near_rows_of(): pl.pallas_call(near_kernel, grid=(count,), out_shape=jax.ShapeDtypeStruct...]
  transfers between devices with their start and end apart: 9 -> 8, of which waited for: 9 -> 8; matrix products, arithmetic and copies ran while one was open for 0% -> 0% of each run, Pallas kernels for 9% -> 9%
where the time goes in v5:
time: 114 us
  blocking collectives  40.6 us (36%)
  Pallas kernels  37.2 us (33%)
  starting transfers between devices  19.2 us (17%)
  waiting for transfers between devices  15.4 us (14%)
    all_to_all x4, blocking collectives, trade(): return lax.all_to_all(x, axis, 0, 0, axis_index_groups=groups, tiled=True)  40.6 us
    pallas_call x1, Pallas kernels, pair_sums(): pl.pallas_call(functools.partial(pair_kernel, cols, total_flows, total_re...  14.4 us
    all_to_all x2, starting transfers between devices, trade(): return lax.all_to_all(x, axis, 0, 0, axis_index_groups=groups, tiled=True)  13 us
    pallas_call x2, Pallas kernels, row_stats(): pl.pallas_call(stat_kernel, grid=(count,), out_shape=[jax.ShapeDtypeStruc...  9.97 us
    ppermute x5, waiting for transfers between devices, swap_sum(): lax.ppermute(x, axis, [(i, i ^ hop) for i in range(count)])  8.41 us
    pallas_call x5, Pallas kernels, call_once(): pl.pallas_call(kernel, grid=(1,), out_shape=[jax.ShapeDtypeStruct(s, f32)...  7.7 us
    ppermute x5, starting transfers between devices, swap_sum(): lax.ppermute(x, axis, [(i, i ^ hop) for i in range(count)])  6.15 us
    all_to_all x2, waiting for transfers between devices, trade(): return lax.all_to_all(x, axis, 0, 0, axis_index_groups=groups, tiled=True)  5.48 us
  transfers between devices with their start and end apart: 8, of which 8 were waited for; matrix products, arithmetic and copies ran while one was open for 0% of the time, Pallas kernels for 9%

profile of v5, /device:TPU:0, one launch (start us, length us, event | category | flops | bytes accessed | tf_op | source)
XLA Modules:
  0.0 113.6 jit_solution(9447395202711418970)
XLA Ops:
  0.6 0.0 copy-start.3
  0.6 5.7 %shard_map.59 = (f32[256,256]{1,0:T(8,128)}, f32[64,256]{1,0:T(8,128)}, f32[64,256]{1,0:T(8,128)}) custom-call(s32[1]{0:T(128)} %bitcast.first_ref, f32[64,256]{1,0:T(8,128)} %bitcast.9, f32[256,256]{1,0:T(8,128)} %hid_ref.3, s32[1,256]{1,0:T(1,128)} %bitcast.10), custom_call_target="tpu_custom_call" | custom-call | tf_op jit(solution)/shard_map/pallas_call | solution.py:45
  6.4 6.4 %all-to-all-start = ((f32[8,32,256]{2,1,0:T(8,128)}), f32[8,32,256]{2,1,0:T(8,128)S(1)}, u32[]{:S(2)}, u32[]{:S(2)}) async-start(f32[8,32,256]{2,1,0:T(8,128)} %bitcast.8), calls=%async_computation | async-start | bytes 524288 | tf_op jit(solution)/shard_map/all_to_all | solution.py:460
  12.8 5.4 %shard_map.60 = (f32[16,256]{1,0:T(8,128)S(1)}, f32[8,8192]{1,0:T(8,128)S(1)}, bf16[2048,256]{1,0:T(8,128)(2,1)S(1)}) custom-call(f32[16384,256]{1,0:T(8,128)} %rows_ref.3), custom_call_target="tpu_custom_call" | custom-call | flops 33554432 | bytes 8388608 | tf_op jit(solution)/shard_map/pallas_call | solution.py:171
  18.2 0.0 copy-done.3
  18.2 0.1 dynamic-slice_bitcast_fusion
  18.3 0.1 copy.6.len_ref
  18.4 1.7 %all-to-all-done.parts_ref = f32[8,32,256]{2,1,0:T(8,128)S(1)} async-done(((f32[8,32,256]{2,1,0:T(8,128)}), f32[8,32,256]{2,1,0:T(8,128)S(1)}, u32[]{:S(2)}, u32[]{:S(2)}) %all-to-all-start) | async-done | bytes 262176 | tf_op jit(solution)/shard_map/all_to_all | solution.py:460
  20.0 0.8 shard_map.61.own_ref
  20.8 6.6 %all-to-all-start.1 = ((f32[8,32,256]{2,1,0:T(8,128)}), f32[8,32,256]{2,1,0:T(8,128)S(1)}, u32[]{:S(2)}, u32[]{:S(2)}) async-start(f32[8,32,256]{2,1,0:T(8,128)} %shard_map.61.own_ref), calls=%async_computation.1 | async-start | bytes 524288 | tf_op jit(solution)/shard_map/all_to_all | solution.py:460
  27.4 4.6 %shard_map.62 = (f32[16,256]{1,0:T(8,128)S(1)}, f32[8,8192]{1,0:T(8,128)S(1)}) custom-call(f32[16384,256]{1,0:T(8,128)} %rows_ref.3), custom_call_target="tpu_custom_call" | custom-call | flops 33554432 | bytes 8388608 | tf_op jit(solution)/shard_map/pallas_call | solution.py:171
  32.1 0.0 copy-start
  32.1 0.0 copy-start.1
  32.1 0.0 copy-start.2
  32.1 3.8 %all-to-all-done.1.others_ref = f32[8,32,256]{2,1,0:T(8,128)S(1)} async-done(((f32[8,32,256]{2,1,0:T(8,128)}), f32[8,32,256]{2,1,0:T(8,128)S(1)}, u32[]{:S(2)}, u32[]{:S(2)}) %all-to-all-start.1) | async-done | bytes 262176 | tf_op jit(solution)/shard_map/all_to_all | solution.py:460
  35.9 0.0 collective-permute-start
  35.9 1.5 %collective-permute-done.more_ref = f32[8,32,256]{2,1,0:T(8,128)S(1)} collective-permute-done((f32[8,32,256]{2,1,0:T(8,128)S(1)}, f32[8,32,256]{2,1,0:T(8,128)S(1)}, u32[]{:S(2)}, u32[]{:S(2)}) %collective-permute-start) | collective-permute-done | bytes 262176 | tf_op jit(solution)/shard_map/ppermute | solution.py:491
  37.4 1.1 shard_map.63
  38.5 11.6 %all_to_all.30.hall_ref = f32[8,40,256]{2,1,0:T(8,128)S(1)} all-to-all(f32[8,40,256]{2,1,0:T(8,128)S(1)} %shard_map.63), channel_id=1, replica_groups=mesh['real'=8,'gen'=16] {'real'}, dimensions={0} | all-to-all | bytes 655360 | tf_op jit(solution)/shard_map/all_to_all | solution.py:460
  50.1 14.4 %shard_map.64 = f32[8,40,256]{2,1,0:T(8,128)S(1)} custom-call(f32[8,40,256]{2,1,0:T(8,128)S(1)} %all_to_all.30.hall_ref, f32[8,32,256]{2,1,0:T(8,128)S(1)} %all-to-all-done.1.others_ref, f32[8,32,256]{2,1,0:T(8,128)S(1)} %collective-permute-done.more_ref, bf16[2048,256]{1,0:T(8,128)(2,1)S(1)} %get-tuple-element.31.front_ref, f32[16384,256]{1,0:T(8,128)} %rows_ref.3, ...), custom_call_target="tpu_custom_call" | custom-call | flops 6442450944 | bytes 16777216 | tf_op jit(solution)/shard_map/pallas_call | solution.py:399
  64.5 10.2 %all_to_all.31.parts_ref = f32[8,40,256]{2,1,0:T(8,128)S(1)} all-to-all(f32[8,40,256]{2,1,0:T(8,128)S(1)} %shard_map.64), channel_id=1, replica_groups=mesh['real'=8,'gen'=16] {'real'}, dimensions={0} | all-to-all | bytes 655360 | tf_op jit(solution)/shard_map/all_to_all | solution.py:460
  74.7 10.2 %all_to_all.32.gh_ref = f32[8,40,256]{2,1,0:T(8,128)S(1)} all-to-all(f32[8,40,256]{2,1,0:T(8,128)S(1)} %shard_map.65), channel_id=1, replica_groups=mesh['real'=8,'gen'=16] {'real'}, dimensions={0} | all-to-all | bytes 655360 | tf_op jit(solution)/shard_map/all_to_all | solution.py:460
  84.8 0.0 copy-done
  84.8 0.0 copy-done.1
  84.9 0.0 copy-done.2
  84.9 4.5 %shard_map.66 = f32[72,256]{1,0:T(8,128)S(1)} custom-call(f32[8,40,256]{2,1,0:T(8,128)S(1)} %all_to_all.32.gh_ref, f32[64,256]{1,0:T(8,128)S(1)} %copy-done.1, f32[64,256]{1,0:T(8,128)S(1)} %copy-done.2, f32[256,256]{1,0:T(8,128)S(1)} %copy-done), custom_call_target="tpu_custom_call" | custom-call | tf_op jit(solution)/shard_map/pallas_call | solution.py:120
  89.3 0.1 collective-permute-start.1
  89.4 1.3 %collective-permute-done.1 = f32[72,256]{1,0:T(8,128)S(1)} collective-permute-done((f32[72,256]{1,0:T(8,128)S(1)}, f32[72,256]{1,0:T(8,128)S(1)}, u32[]{:S(2)}, u32[]{:S(2)}) %collective-permute-start.1) | collective-permute-done | bytes 73760 | tf_op jit(solution)/shard_map/ppermute | solution.py:453
  90.7 1.9 %collective-permute-start.2 = (f32[72,256]{1,0:T(8,128)S(1)}, f32[72,256]{1,0:T(8,128)S(1)}, u32[]{:S(2)}, u32[]{:S(2)}) collective-permute-start(f32[72,256]{1,0:T(8,128)S(1)} %add.19), channel_id=1, source_target_pairs={{0,2},{1,3},{2,0},{3,1},{4,6},{5,7},{6,4},{7,5},{8,10},{9,11},{10,... | collective-permute-start | bytes 221192 | tf_op jit(solution)/shard_map/ppermute | solution.py:453
  92.6 4.0 %collective-permute-done.2 = f32[72,256]{1,0:T(8,128)S(1)} collective-permute-done((f32[72,256]{1,0:T(8,128)S(1)}, f32[72,256]{1,0:T(8,128)S(1)}, u32[]{:S(2)}, u32[]{:S(2)}) %collective-permute-start.2) | collective-permute-done | bytes 73760 | tf_op jit(solution)/shard_map/ppermute | solution.py:453
  96.7 1.3 %collective-permute-start.5 = (f32[72,256]{1,0:T(8,128)S(1)}, f32[72,256]{1,0:T(8,128)S(1)}, u32[]{:S(2)}, u32[]{:S(2)}) collective-permute-start(f32[72,256]{1,0:T(8,128)S(1)} %add.20), channel_id=1, source_target_pairs={{0,12},{1,13},{2,14},{3,15},{4,8},{5,9},{6,10},{7,11},{8,4},{9,5},... | collective-permute-start | bytes 221192 | tf_op jit(solution)/shard_map/ppermute | solution.py:453
  98.0 1.1 collective-permute-start.4
  99.1 1.7 %collective-permute-start.3 = (f32[72,256]{1,0:T(8,128)S(1)}, f32[72,256]{1,0:T(8,128)S(1)}, u32[]{:S(2)}, u32[]{:S(2)}) collective-permute-start(f32[72,256]{1,0:T(8,128)S(1)} %add.20), channel_id=1, source_target_pairs={{0,4},{1,5},{2,6},{3,7},{4,0},{5,1},{6,2},{7,3},{8,12},{9,13},{10,... | collective-permute-start | bytes 221192 | tf_op jit(solution)/shard_map/ppermute | solution.py:453
  100.8 1.6 %collective-permute-done.5 = f32[72,256]{1,0:T(8,128)S(1)} collective-permute-done((f32[72,256]{1,0:T(8,128)S(1)}, f32[72,256]{1,0:T(8,128)S(1)}, u32[]{:S(2)}, u32[]{:S(2)}) %collective-permute-start.5) | collective-permute-done | bytes 73760 | tf_op jit(solution)/shard_map/ppermute | solution.py:453
  102.4 1.5 %collective-permute-done.4 = f32[72,256]{1,0:T(8,128)S(1)} collective-permute-done((f32[72,256]{1,0:T(8,128)S(1)}, f32[72,256]{1,0:T(8,128)S(1)}, u32[]{:S(2)}, u32[]{:S(2)}) %collective-permute-start.4) | collective-permute-done | bytes 73760 | tf_op jit(solution)/shard_map/ppermute | solution.py:453
  103.8 0.1 collective-permute-done.3
  104.0 0.1 shard_map.67
  104.1 8.7 %all_to_all.33.sq_ref = f32[8,8,128]{2,1,0:T(8,128)S(1)} all-to-all(f32[8,8,128]{2,1,0:T(8,128)S(1)} %shard_map.67), channel_id=1, replica_groups=mesh['real'=8,'gen'=16] {'real'}, dimensions={0} | all-to-all | bytes 65536 | tf_op jit(solution)/shard_map/all_to_all | solution.py:460
  112.7 0.7 shard_map.68
  (4 shorter events, 0.1 us)
Async XLA Ops:
  0.6 17.5 %copy-start.3 = (s32[256]{0:T(256)S(1)}, s32[256]{0:T(256)}, u32[]{:S(2)}) copy-start(s32[256]{0:T(256)} %param.6) | copy-start | bytes 3076
  6.4 13.6 %all-to-all-start = ((f32[8,32,256]{2,1,0:T(8,128)}), f32[8,32,256]{2,1,0:T(8,128)S(1)}, u32[]{:S(2)}, u32[]{:S(2)}) async-start(f32[8,32,256]{2,1,0:T(8,128)} %bitcast.8), calls=%async_computation | async-start | bytes 524288 | tf_op jit(solution)/shard_map/all_to_all | solution.py:460
  20.8 15.1 %all-to-all-start.1 = ((f32[8,32,256]{2,1,0:T(8,128)}), f32[8,32,256]{2,1,0:T(8,128)S(1)}, u32[]{:S(2)}, u32[]{:S(2)}) async-start(f32[8,32,256]{2,1,0:T(8,128)} %shard_map.61.own_ref), calls=%async_computation.1 | async-start | bytes 524288 | tf_op jit(solution)/shard_map/all_to_all | solution.py:460
  32.1 52.8 %copy-start = (f32[256,256]{1,0:T(8,128)S(1)}, f32[256,256]{1,0:T(8,128)}, u32[]{:S(2)}) copy-start(f32[256,256]{1,0:T(8,128)} %hid_ref.3) | copy-start | bytes 786436
  32.1 52.8 %copy-start.1 = (f32[64,256]{1,0:T(8,128)S(1)}, f32[64,256]{1,0:T(8,128)}, u32[]{:S(2)}) copy-start(f32[64,256]{1,0:T(8,128)} %get-tuple-element.34.val_ref) | copy-start | bytes 196612
  32.1 52.8 %copy-start.2 = (f32[64,256]{1,0:T(8,128)S(1)}, f32[64,256]{1,0:T(8,128)}, u32[]{:S(2)}) copy-start(f32[64,256]{1,0:T(8,128)} %get-tuple-element.35.sig_ref) | copy-start | bytes 196612
  35.9 1.5 %collective-permute-start = (f32[8,32,256]{2,1,0:T(8,128)S(1)}, f32[8,32,256]{2,1,0:T(8,128)S(1)}, u32[]{:S(2)}, u32[]{:S(2)}) collective-permute-start(f32[8,32,256]{2,1,0:T(8,128)S(1)} %all-to-all-done.1.others_ref), channel_id=1, source_target_pairs={{0,1},{1,0},{2,3},{3,2},{4,5},{5,4},{6,7},{7,6},{8,9},{9,8},{10,11... | collective-permute-start | bytes 786440 | tf_op jit(solution)/shard_map/ppermute | solution.py:491
  89.3 1.3 %collective-permute-start.1 = (f32[72,256]{1,0:T(8,128)S(1)}, f32[72,256]{1,0:T(8,128)S(1)}, u32[]{:S(2)}, u32[]{:S(2)}) collective-permute-start(f32[72,256]{1,0:T(8,128)S(1)} %shard_map.66), channel_id=1, source_target_pairs={{0,1},{1,0},{2,3},{3,2},{4,5},{5,4},{6,7},{7,6},{8,9},{9,8},{10,11... | collective-permute-start | bytes 221192 | tf_op jit(solution)/shard_map/ppermute | solution.py:453
  90.7 5.9 %collective-permute-start.2 = (f32[72,256]{1,0:T(8,128)S(1)}, f32[72,256]{1,0:T(8,128)S(1)}, u32[]{:S(2)}, u32[]{:S(2)}) collective-permute-start(f32[72,256]{1,0:T(8,128)S(1)} %add.19), channel_id=1, source_target_pairs={{0,2},{1,3},{2,0},{3,1},{4,6},{5,7},{6,4},{7,5},{8,10},{9,11},{10,... | collective-permute-start | bytes 221192 | tf_op jit(solution)/shard_map/ppermute | solution.py:453
  96.7 5.7 %collective-permute-start.5 = (f32[72,256]{1,0:T(8,128)S(1)}, f32[72,256]{1,0:T(8,128)S(1)}, u32[]{:S(2)}, u32[]{:S(2)}) collective-permute-start(f32[72,256]{1,0:T(8,128)S(1)} %add.20), channel_id=1, source_target_pairs={{0,12},{1,13},{2,14},{3,15},{4,8},{5,9},{6,10},{7,11},{8,4},{9,5},... | collective-permute-start | bytes 221192 | tf_op jit(solution)/shard_map/ppermute | solution.py:453
  98.0 5.9 %collective-permute-start.4 = (f32[72,256]{1,0:T(8,128)S(1)}, f32[72,256]{1,0:T(8,128)S(1)}, u32[]{:S(2)}, u32[]{:S(2)}) collective-permute-start(f32[72,256]{1,0:T(8,128)S(1)} %add.20), channel_id=1, source_target_pairs={{0,8},{1,9},{2,10},{3,11},{4,12},{5,13},{6,14},{7,15},{8,0},{9,1},... | collective-permute-start | bytes 221192 | tf_op jit(solution)/shard_map/ppermute | solution.py:453
  99.1 4.9 %collective-permute-start.3 = (f32[72,256]{1,0:T(8,128)S(1)}, f32[72,256]{1,0:T(8,128)S(1)}, u32[]{:S(2)}, u32[]{:S(2)}) collective-permute-start(f32[72,256]{1,0:T(8,128)S(1)} %add.20), channel_id=1, source_target_pairs={{0,4},{1,5},{2,6},{3,7},{4,0},{5,1},{6,2},{7,3},{8,12},{9,13},{10,... | collective-permute-start | bytes 221192 | tf_op jit(solution)/shard_map/ppermute | solution.py:453

commit v6 on v5

--- a/solution.py
+++ b/solution.py
@@ -17,6 +17,7 @@
 STEP = UNIT * SPACING
 FAR = 1.0e6
 EXTRA = 8
+TURN = 32
 ROOT_2 = math.sqrt(1.0 / 2.0)
 ROOT_8 = math.sqrt(1.0 / 8.0)
 
@@ -78,16 +79,18 @@
     sig_ref[...] = sig / (lens.astype(f32) * (UNIT * SPACING * SPACING))
 
     def bins(i, carry):
-        base = (8 * i).astype(f32) + 0.5
-        rows = []
-        for j in range(8):
-            off = (base + j) * STEP - val
-            e = jnp.exp2(-(off * off))
-            rows.append(jnp.sum(e, 0, keepdims=True))
-        out_ref[pl.ds(pl.multiple_of(8 * i, 8), 8), :] = jnp.concatenate(rows, 0)
+        base = (TURN * i).astype(f32) + 0.5
+        for k in range(0, TURN, 8):
+            rows = []
+            for j in range(k, k + 8):
+                off = (base + j) * STEP - val
+                e = jnp.exp2(-(off * off))
+                rows.append(jnp.sum(e, 0, keepdims=True))
+            at = pl.multiple_of(TURN * i + k, 8)
+            out_ref[pl.ds(at, 8), :] = jnp.concatenate(rows, 0)
         return carry
 
-    lax.fori_loop(0, NUM_BINS // 8, bins, 0)
+    lax.fori_loop(0, NUM_BINS // TURN, bins, 0)
     out_ref[...] = out_ref[...].T
 
 
@@ -99,15 +102,15 @@
     val = val_ref[...]
 
     def bins(i, acc):
-        base = (8 * i).astype(f32) + 0.5
-        rows = ght_ref[pl.ds(pl.multiple_of(8 * i, 8), 8), :]
-        for j in range(8):
+        base = (TURN * i).astype(f32) + 0.5
+        rows = ght_ref[pl.ds(pl.multiple_of(TURN * i, TURN), TURN), :]
+        for j in range(TURN):
             off = (base + j) * STEP - val
             e = jnp.exp2(-(off * off))
             acc = acc + (e * off) * rows[j : j + 1, :]
         return acc
 
-    slope = lax.fori_loop(0, NUM_BINS // 8, bins, jnp.zeros_like(val))
+    slope = lax.fori_loop(0, NUM_BINS // TURN, bins, jnp.zeros_like(val))
     out_ref[0:tall, :] = lax.dot_general(
         slope * sig_ref[...], hid_ref[...], NN, precision=highest, preferred_element_type=f32
     )

time: 114 us -> 114 us (level)
  no operation moved by 1% of the time
where the time goes in v6:
time: 114 us; the launch traced here: 113 us
  blocking collectives  40.6 us (36%)
  Pallas kernels  36.7 us (32%)
  starting transfers between devices  19.2 us (17%)
  waiting for transfers between devices  15.4 us (14%)
    all_to_all x4, blocking collectives, trade(): return lax.all_to_all(x, axis, 0, 0, axis_index_groups=groups, tiled=True)  40.6 us
    pallas_call x1, Pallas kernels, pair_sums(): pl.pallas_call(functools.partial(pair_kernel, cols, total_flows, total_re...  14.4 us
    all_to_all x2, starting transfers between devices, trade(): return lax.all_to_all(x, axis, 0, 0, axis_index_groups=groups, tiled=True)  13 us
    pallas_call x2, Pallas kernels, row_stats(): pl.pallas_call(stat_kernel, grid=(count,), out_shape=[jax.ShapeDtypeStruc...  9.97 us
    ppermute x5, waiting for transfers between devices, swap_sum(): lax.ppermute(x, axis, [(i, i ^ hop) for i in range(count)])  8.41 us
    pallas_call x5, Pallas kernels, call_once(): pl.pallas_call(kernel, grid=(1,), out_shape=[jax.ShapeDtypeStruct(s, f32)...  7.38 us
    ppermute x5, starting transfers between devices, swap_sum(): lax.ppermute(x, axis, [(i, i ^ hop) for i in range(count)])  6.15 us
    all_to_all x2, waiting for transfers between devices, trade(): return lax.all_to_all(x, axis, 0, 0, axis_index_groups=groups, tiled=True)  5.48 us
  transfers between devices with their start and end apart: 8, of which 8 were waited for; matrix products, arithmetic and copies ran while one was open for 0% of the time, Pallas kernels for 9%

profile of v6, /device:TPU:0, one launch (start us, length us, event | category | flops | bytes accessed | tf_op | source)
XLA Modules:
  0.0 113.1 jit_solution(4221743694616303826)
XLA Ops:
  0.6 0.0 copy-start.3
  0.6 5.4 %shard_map.59 = (f32[256,256]{1,0:T(8,128)}, f32[64,256]{1,0:T(8,128)}, f32[64,256]{1,0:T(8,128)}) custom-call(s32[1]{0:T(128)} %bitcast.first_ref, f32[64,256]{1,0:T(8,128)} %bitcast.9, f32[256,256]{1,0:T(8,128)} %hid_ref.3, s32[1,256]{1,0:T(1,128)} %bitcast.10), custom_call_target="tpu_custom_call" | custom-call | tf_op jit(solution)/shard_map/pallas_call | solution.py:46
  6.1 6.4 %all-to-all-start = ((f32[8,32,256]{2,1,0:T(8,128)}), f32[8,32,256]{2,1,0:T(8,128)S(1)}, u32[]{:S(2)}, u32[]{:S(2)}) async-start(f32[8,32,256]{2,1,0:T(8,128)} %bitcast.8), calls=%async_computation | async-start | bytes 524288 | tf_op jit(solution)/shard_map/all_to_all | solution.py:463
  12.5 5.4 %shard_map.60 = (f32[16,256]{1,0:T(8,128)S(1)}, f32[8,8192]{1,0:T(8,128)S(1)}, bf16[2048,256]{1,0:T(8,128)(2,1)S(1)}) custom-call(f32[16384,256]{1,0:T(8,128)} %rows_ref.3), custom_call_target="tpu_custom_call" | custom-call | flops 33554432 | bytes 8388608 | tf_op jit(solution)/shard_map/pallas_call | solution.py:174
  17.9 0.0 copy-done.3
  17.9 0.1 dynamic-slice_bitcast_fusion
  17.9 0.1 copy.6.len_ref
  18.0 1.7 %all-to-all-done.parts_ref = f32[8,32,256]{2,1,0:T(8,128)S(1)} async-done(((f32[8,32,256]{2,1,0:T(8,128)}), f32[8,32,256]{2,1,0:T(8,128)S(1)}, u32[]{:S(2)}, u32[]{:S(2)}) %all-to-all-start) | async-done | bytes 262176 | tf_op jit(solution)/shard_map/all_to_all | solution.py:463
  19.7 0.8 shard_map.61.own_ref
  20.5 6.6 %all-to-all-start.1 = ((f32[8,32,256]{2,1,0:T(8,128)}), f32[8,32,256]{2,1,0:T(8,128)S(1)}, u32[]{:S(2)}, u32[]{:S(2)}) async-start(f32[8,32,256]{2,1,0:T(8,128)} %shard_map.61.own_ref), calls=%async_computation.1 | async-start | bytes 524288 | tf_op jit(solution)/shard_map/all_to_all | solution.py:463
  27.1 4.6 %shard_map.62 = (f32[16,256]{1,0:T(8,128)S(1)}, f32[8,8192]{1,0:T(8,128)S(1)}) custom-call(f32[16384,256]{1,0:T(8,128)} %rows_ref.3), custom_call_target="tpu_custom_call" | custom-call | flops 33554432 | bytes 8388608 | tf_op jit(solution)/shard_map/pallas_call | solution.py:174
  31.7 0.0 copy-start
  31.7 0.0 copy-start.1
  31.7 0.0 copy-start.2
  31.8 3.8 %all-to-all-done.1.others_ref = f32[8,32,256]{2,1,0:T(8,128)S(1)} async-done(((f32[8,32,256]{2,1,0:T(8,128)}), f32[8,32,256]{2,1,0:T(8,128)S(1)}, u32[]{:S(2)}, u32[]{:S(2)}) %all-to-all-start.1) | async-done | bytes 262176 | tf_op jit(solution)/shard_map/all_to_all | solution.py:463
  35.6 0.0 collective-permute-start
  35.6 1.5 %collective-permute-done.more_ref = f32[8,32,256]{2,1,0:T(8,128)S(1)} collective-permute-done((f32[8,32,256]{2,1,0:T(8,128)S(1)}, f32[8,32,256]{2,1,0:T(8,128)S(1)}, u32[]{:S(2)}, u32[]{:S(2)}) %collective-permute-start) | collective-permute-done | bytes 262176 | tf_op jit(solution)/shard_map/ppermute | solution.py:494
  37.1 1.1 shard_map.63
  38.2 11.6 %all_to_all.30.hall_ref = f32[8,40,256]{2,1,0:T(8,128)S(1)} all-to-all(f32[8,40,256]{2,1,0:T(8,128)S(1)} %shard_map.63), channel_id=1, replica_groups=mesh['real'=8,'gen'=16] {'real'}, dimensions={0} | all-to-all | bytes 655360 | tf_op jit(solution)/shard_map/all_to_all | solution.py:463
  49.8 14.4 %shard_map.64 = f32[8,40,256]{2,1,0:T(8,128)S(1)} custom-call(f32[8,40,256]{2,1,0:T(8,128)S(1)} %all_to_all.30.hall_ref, f32[8,32,256]{2,1,0:T(8,128)S(1)} %all-to-all-done.1.others_ref, f32[8,32,256]{2,1,0:T(8,128)S(1)} %collective-permute-done.more_ref, bf16[2048,256]{1,0:T(8,128)(2,1)S(1)} %get-tuple-element.31.front_ref, f32[16384,256]{1,0:T(8,128)} %rows_ref.3, ...), custom_call_target="tpu_custom_call" | custom-call | flops 6442450944 | bytes 16777216 | tf_op jit(solution)/shard_map/pallas_call | solution.py:402
  64.1 10.2 %all_to_all.31.parts_ref = f32[8,40,256]{2,1,0:T(8,128)S(1)} all-to-all(f32[8,40,256]{2,1,0:T(8,128)S(1)} %shard_map.64), channel_id=1, replica_groups=mesh['real'=8,'gen'=16] {'real'}, dimensions={0} | all-to-all | bytes 655360 | tf_op jit(solution)/shard_map/all_to_all | solution.py:463
  74.4 10.2 %all_to_all.32.gh_ref = f32[8,40,256]{2,1,0:T(8,128)S(1)} all-to-all(f32[8,40,256]{2,1,0:T(8,128)S(1)} %shard_map.65), channel_id=1, replica_groups=mesh['real'=8,'gen'=16] {'real'}, dimensions={0} | all-to-all | bytes 655360 | tf_op jit(solution)/shard_map/all_to_all | solution.py:463
  84.5 0.0 copy-done
  84.5 0.0 copy-done.1
  84.5 0.0 copy-done.2
  84.5 4.3 %shard_map.66 = f32[72,256]{1,0:T(8,128)S(1)} custom-call(f32[8,40,256]{2,1,0:T(8,128)S(1)} %all_to_all.32.gh_ref, f32[64,256]{1,0:T(8,128)S(1)} %copy-done.1, f32[64,256]{1,0:T(8,128)S(1)} %copy-done.2, f32[256,256]{1,0:T(8,128)S(1)} %copy-done), custom_call_target="tpu_custom_call" | custom-call | tf_op jit(solution)/shard_map/pallas_call | solution.py:123
  88.8 0.1 collective-permute-start.1
  88.9 1.3 %collective-permute-done.1 = f32[72,256]{1,0:T(8,128)S(1)} collective-permute-done((f32[72,256]{1,0:T(8,128)S(1)}, f32[72,256]{1,0:T(8,128)S(1)}, u32[]{:S(2)}, u32[]{:S(2)}) %collective-permute-start.1) | collective-permute-done | bytes 73760 | tf_op jit(solution)/shard_map/ppermute | solution.py:456
  90.2 1.9 %collective-permute-start.2 = (f32[72,256]{1,0:T(8,128)S(1)}, f32[72,256]{1,0:T(8,128)S(1)}, u32[]{:S(2)}, u32[]{:S(2)}) collective-permute-start(f32[72,256]{1,0:T(8,128)S(1)} %add.19), channel_id=1, source_target_pairs={{0,2},{1,3},{2,0},{3,1},{4,6},{5,7},{6,4},{7,5},{8,10},{9,11},{10,... | collective-permute-start | bytes 221192 | tf_op jit(solution)/shard_map/ppermute | solution.py:456
  92.1 4.0 %collective-permute-done.2 = f32[72,256]{1,0:T(8,128)S(1)} collective-permute-done((f32[72,256]{1,0:T(8,128)S(1)}, f32[72,256]{1,0:T(8,128)S(1)}, u32[]{:S(2)}, u32[]{:S(2)}) %collective-permute-start.2) | collective-permute-done | bytes 73760 | tf_op jit(solution)/shard_map/ppermute | solution.py:456
  96.1 1.3 %collective-permute-start.5 = (f32[72,256]{1,0:T(8,128)S(1)}, f32[72,256]{1,0:T(8,128)S(1)}, u32[]{:S(2)}, u32[]{:S(2)}) collective-permute-start(f32[72,256]{1,0:T(8,128)S(1)} %add.20), channel_id=1, source_target_pairs={{0,12},{1,13},{2,14},{3,15},{4,8},{5,9},{6,10},{7,11},{8,4},{9,5},... | collective-permute-start | bytes 221192 | tf_op jit(solution)/shard_map/ppermute | solution.py:456
  97.4 1.1 collective-permute-start.4
  98.5 1.7 %collective-permute-start.3 = (f32[72,256]{1,0:T(8,128)S(1)}, f32[72,256]{1,0:T(8,128)S(1)}, u32[]{:S(2)}, u32[]{:S(2)}) collective-permute-start(f32[72,256]{1,0:T(8,128)S(1)} %add.20), channel_id=1, source_target_pairs={{0,4},{1,5},{2,6},{3,7},{4,0},{5,1},{6,2},{7,3},{8,12},{9,13},{10,... | collective-permute-start | bytes 221192 | tf_op jit(solution)/shard_map/ppermute | solution.py:456
  100.3 1.6 %collective-permute-done.5 = f32[72,256]{1,0:T(8,128)S(1)} collective-permute-done((f32[72,256]{1,0:T(8,128)S(1)}, f32[72,256]{1,0:T(8,128)S(1)}, u32[]{:S(2)}, u32[]{:S(2)}) %collective-permute-start.5) | collective-permute-done | bytes 73760 | tf_op jit(solution)/shard_map/ppermute | solution.py:456
  101.8 1.5 %collective-permute-done.4 = f32[72,256]{1,0:T(8,128)S(1)} collective-permute-done((f32[72,256]{1,0:T(8,128)S(1)}, f32[72,256]{1,0:T(8,128)S(1)}, u32[]{:S(2)}, u32[]{:S(2)}) %collective-permute-start.4) | collective-permute-done | bytes 73760 | tf_op jit(solution)/shard_map/ppermute | solution.py:456
  103.3 0.1 collective-permute-done.3
  103.4 0.1 shard_map.67
  103.5 8.7 %all_to_all.33.sq_ref = f32[8,8,128]{2,1,0:T(8,128)S(1)} all-to-all(f32[8,8,128]{2,1,0:T(8,128)S(1)} %shard_map.67), channel_id=1, replica_groups=mesh['real'=8,'gen'=16] {'real'}, dimensions={0} | all-to-all | bytes 65536 | tf_op jit(solution)/shard_map/all_to_all | solution.py:463
  112.2 0.7 shard_map.68
  (4 shorter events, 0.1 us)
Async XLA Ops:
  0.6 17.2 %copy-start.3 = (s32[256]{0:T(256)S(1)}, s32[256]{0:T(256)}, u32[]{:S(2)}) copy-start(s32[256]{0:T(256)} %param.6) | copy-start | bytes 3076
  6.1 13.6 %all-to-all-start = ((f32[8,32,256]{2,1,0:T(8,128)}), f32[8,32,256]{2,1,0:T(8,128)S(1)}, u32[]{:S(2)}, u32[]{:S(2)}) async-start(f32[8,32,256]{2,1,0:T(8,128)} %bitcast.8), calls=%async_computation | async-start | bytes 524288 | tf_op jit(solution)/shard_map/all_to_all | solution.py:463
  20.5 15.1 %all-to-all-start.1 = ((f32[8,32,256]{2,1,0:T(8,128)}), f32[8,32,256]{2,1,0:T(8,128)S(1)}, u32[]{:S(2)}, u32[]{:S(2)}) async-start(f32[8,32,256]{2,1,0:T(8,128)} %shard_map.61.own_ref), calls=%async_computation.1 | async-start | bytes 524288 | tf_op jit(solution)/shard_map/all_to_all | solution.py:463
  31.7 52.8 %copy-start = (f32[256,256]{1,0:T(8,128)S(1)}, f32[256,256]{1,0:T(8,128)}, u32[]{:S(2)}) copy-start(f32[256,256]{1,0:T(8,128)} %hid_ref.3) | copy-start | bytes 786436
  31.7 52.8 %copy-start.1 = (f32[64,256]{1,0:T(8,128)S(1)}, f32[64,256]{1,0:T(8,128)}, u32[]{:S(2)}) copy-start(f32[64,256]{1,0:T(8,128)} %get-tuple-element.34.val_ref) | copy-start | bytes 196612
  31.7 52.8 %copy-start.2 = (f32[64,256]{1,0:T(8,128)S(1)}, f32[64,256]{1,0:T(8,128)}, u32[]{:S(2)}) copy-start(f32[64,256]{1,0:T(8,128)} %get-tuple-element.35.sig_ref) | copy-start | bytes 196612
  35.6 1.5 %collective-permute-start = (f32[8,32,256]{2,1,0:T(8,128)S(1)}, f32[8,32,256]{2,1,0:T(8,128)S(1)}, u32[]{:S(2)}, u32[]{:S(2)}) collective-permute-start(f32[8,32,256]{2,1,0:T(8,128)S(1)} %all-to-all-done.1.others_ref), channel_id=1, source_target_pairs={{0,1},{1,0},{2,3},{3,2},{4,5},{5,4},{6,7},{7,6},{8,9},{9,8},{10,11... | collective-permute-start | bytes 786440 | tf_op jit(solution)/shard_map/ppermute | solution.py:494
  88.8 1.3 %collective-permute-start.1 = (f32[72,256]{1,0:T(8,128)S(1)}, f32[72,256]{1,0:T(8,128)S(1)}, u32[]{:S(2)}, u32[]{:S(2)}) collective-permute-start(f32[72,256]{1,0:T(8,128)S(1)} %shard_map.66), channel_id=1, source_target_pairs={{0,1},{1,0},{2,3},{3,2},{4,5},{5,4},{6,7},{7,6},{8,9},{9,8},{10,11... | collective-permute-start | bytes 221192 | tf_op jit(solution)/shard_map/ppermute | solution.py:456
  90.2 5.9 %collective-permute-start.2 = (f32[72,256]{1,0:T(8,128)S(1)}, f32[72,256]{1,0:T(8,128)S(1)}, u32[]{:S(2)}, u32[]{:S(2)}) collective-permute-start(f32[72,256]{1,0:T(8,128)S(1)} %add.19), channel_id=1, source_target_pairs={{0,2},{1,3},{2,0},{3,1},{4,6},{5,7},{6,4},{7,5},{8,10},{9,11},{10,... | collective-permute-start | bytes 221192 | tf_op jit(solution)/shard_map/ppermute | solution.py:456
  96.1 5.7 %collective-permute-start.5 = (f32[72,256]{1,0:T(8,128)S(1)}, f32[72,256]{1,0:T(8,128)S(1)}, u32[]{:S(2)}, u32[]{:S(2)}) collective-permute-start(f32[72,256]{1,0:T(8,128)S(1)} %add.20), channel_id=1, source_target_pairs={{0,12},{1,13},{2,14},{3,15},{4,8},{5,9},{6,10},{7,11},{8,4},{9,5},... | collective-permute-start | bytes 221192 | tf_op jit(solution)/shard_map/ppermute | solution.py:456
  97.4 5.9 %collective-permute-start.4 = (f32[72,256]{1,0:T(8,128)S(1)}, f32[72,256]{1,0:T(8,128)S(1)}, u32[]{:S(2)}, u32[]{:S(2)}) collective-permute-start(f32[72,256]{1,0:T(8,128)S(1)} %add.20), channel_id=1, source_target_pairs={{0,8},{1,9},{2,10},{3,11},{4,12},{5,13},{6,14},{7,15},{8,0},{9,1},... | collective-permute-start | bytes 221192 | tf_op jit(solution)/shard_map/ppermute | solution.py:456
  98.5 4.9 %collective-permute-start.3 = (f32[72,256]{1,0:T(8,128)S(1)}, f32[72,256]{1,0:T(8,128)S(1)}, u32[]{:S(2)}, u32[]{:S(2)}) collective-permute-start(f32[72,256]{1,0:T(8,128)S(1)} %add.20), channel_id=1, source_target_pairs={{0,4},{1,5},{2,6},{3,7},{4,0},{5,1},{6,2},{7,3},{8,12},{9,13},{10,... | collective-permute-start | bytes 221192 | tf_op jit(solution)/shard_map/ppermute | solution.py:456

commit v7 on v6

--- a/solution.py
+++ b/solution.py
@@ -17,7 +17,7 @@
 STEP = UNIT * SPACING
 FAR = 1.0e6
 EXTRA = 8
-TURN = 32
+TURN = 64
 ROOT_2 = math.sqrt(1.0 / 2.0)
 ROOT_8 = math.sqrt(1.0 / 8.0)
 
@@ -124,8 +124,8 @@
         back_kernel,
         grid=(1,),
         out_shape=jax.ShapeDtypeStruct((t + EXTRA, z), f32),
-        in_specs=[fixed(gh.shape), fixed((t, g)), fixed((t, g)), fixed((g, z))],
-        out_specs=fixed((t + EXTRA, z)),
+        in_specs=[whole()] * 4,
+        out_specs=whole(),
         scratch_shapes=[VMEM((NUM_BINS, g), f32)],
         compiler_params=params(),
     )(gh, val, sig, hidden)

time: 114 us -> 113 us (level)
  no operation moved by 1% of the time
where the time goes in v7:
time: 113 us
  blocking collectives  40.6 us (36%)
  Pallas kernels  36.6 us (32%)
  starting transfers between devices  19.2 us (17%)
  waiting for transfers between devices  15.4 us (14%)
    all_to_all x4, blocking collectives, trade(): return lax.all_to_all(x, axis, 0, 0, axis_index_groups=groups, tiled=True)  40.6 us
    pallas_call x1, Pallas kernels, pair_sums(): pl.pallas_call(functools.partial(pair_kernel, cols, total_flows, total_re...  14.4 us
    all_to_all x2, starting transfers between devices, trade(): return lax.all_to_all(x, axis, 0, 0, axis_index_groups=groups, tiled=True)  13 us
    pallas_call x2, Pallas kernels, row_stats(): pl.pallas_call(stat_kernel, grid=(count,), out_shape=[jax.ShapeDtypeStruc...  9.97 us
    ppermute x5, waiting for transfers between devices, swap_sum(): lax.ppermute(x, axis, [(i, i ^ hop) for i in range(count)])  8.41 us
    pallas_call x5, Pallas kernels, call_once(): pl.pallas_call(kernel, grid=(1,), out_shape=[jax.ShapeDtypeStruct(s, f32)...  7.33 us
    ppermute x5, starting transfers between devices, swap_sum(): lax.ppermute(x, axis, [(i, i ^ hop) for i in range(count)])  6.15 us
    all_to_all x2, waiting for transfers between devices, trade(): return lax.all_to_all(x, axis, 0, 0, axis_index_groups=groups, tiled=True)  5.48 us
  transfers between devices with their start and end apart: 8, of which 8 were waited for; matrix products, arithmetic and copies ran while one was open for 0% of the time, Pallas kernels for 9%

profile of v7, /device:TPU:0, one launch (start us, length us, event | category | flops | bytes accessed | tf_op | source)
XLA Modules:
  0.0 113.0 jit_solution(11801533131987755411)
XLA Ops:
  0.6 0.0 copy-start.3
  0.6 5.4 %shard_map.59 = (f32[256,256]{1,0:T(8,128)}, f32[64,256]{1,0:T(8,128)}, f32[64,256]{1,0:T(8,128)}) custom-call(s32[1]{0:T(128)} %bitcast.first_ref, f32[64,256]{1,0:T(8,128)} %bitcast.9, f32[256,256]{1,0:T(8,128)} %hid_ref.3, s32[1,256]{1,0:T(1,128)} %bitcast.10), custom_call_target="tpu_custom_call" | custom-call | tf_op jit(solution)/shard_map/pallas_call | solution.py:46
  6.0 6.4 %all-to-all-start = ((f32[8,32,256]{2,1,0:T(8,128)}), f32[8,32,256]{2,1,0:T(8,128)S(1)}, u32[]{:S(2)}, u32[]{:S(2)}) async-start(f32[8,32,256]{2,1,0:T(8,128)} %bitcast.8), calls=%async_computation | async-start | bytes 524288 | tf_op jit(solution)/shard_map/all_to_all | solution.py:463
  12.4 5.4 %shard_map.60 = (f32[16,256]{1,0:T(8,128)S(1)}, f32[8,8192]{1,0:T(8,128)S(1)}, bf16[2048,256]{1,0:T(8,128)(2,1)S(1)}) custom-call(f32[16384,256]{1,0:T(8,128)} %rows_ref.3), custom_call_target="tpu_custom_call" | custom-call | flops 33554432 | bytes 8388608 | tf_op jit(solution)/shard_map/pallas_call | solution.py:174
  17.8 0.0 copy-done.3
  17.8 0.1 dynamic-slice_bitcast_fusion
  17.9 0.1 copy.6.len_ref
  18.0 1.7 %all-to-all-done.parts_ref = f32[8,32,256]{2,1,0:T(8,128)S(1)} async-done(((f32[8,32,256]{2,1,0:T(8,128)}), f32[8,32,256]{2,1,0:T(8,128)S(1)}, u32[]{:S(2)}, u32[]{:S(2)}) %all-to-all-start) | async-done | bytes 262176 | tf_op jit(solution)/shard_map/all_to_all | solution.py:463
  19.7 0.8 shard_map.61.own_ref
  20.4 6.6 %all-to-all-start.1 = ((f32[8,32,256]{2,1,0:T(8,128)}), f32[8,32,256]{2,1,0:T(8,128)S(1)}, u32[]{:S(2)}, u32[]{:S(2)}) async-start(f32[8,32,256]{2,1,0:T(8,128)} %shard_map.61.own_ref), calls=%async_computation.1 | async-start | bytes 524288 | tf_op jit(solution)/shard_map/all_to_all | solution.py:463
  27.1 4.6 %shard_map.62 = (f32[16,256]{1,0:T(8,128)S(1)}, f32[8,8192]{1,0:T(8,128)S(1)}) custom-call(f32[16384,256]{1,0:T(8,128)} %rows_ref.3), custom_call_target="tpu_custom_call" | custom-call | flops 33554432 | bytes 8388608 | tf_op jit(solution)/shard_map/pallas_call | solution.py:174
  31.7 0.0 copy-start
  31.7 0.0 copy-start.1
  31.7 0.0 copy-start.2
  31.7 3.8 %all-to-all-done.1.others_ref = f32[8,32,256]{2,1,0:T(8,128)S(1)} async-done(((f32[8,32,256]{2,1,0:T(8,128)}), f32[8,32,256]{2,1,0:T(8,128)S(1)}, u32[]{:S(2)}, u32[]{:S(2)}) %all-to-all-start.1) | async-done | bytes 262176 | tf_op jit(solution)/shard_map/all_to_all | solution.py:463
  35.5 0.0 collective-permute-start
  35.5 1.5 %collective-permute-done.more_ref = f32[8,32,256]{2,1,0:T(8,128)S(1)} collective-permute-done((f32[8,32,256]{2,1,0:T(8,128)S(1)}, f32[8,32,256]{2,1,0:T(8,128)S(1)}, u32[]{:S(2)}, u32[]{:S(2)}) %collective-permute-start) | collective-permute-done | bytes 262176 | tf_op jit(solution)/shard_map/ppermute | solution.py:494
  37.0 1.1 shard_map.63
  38.1 11.6 %all_to_all.30.hall_ref = f32[8,40,256]{2,1,0:T(8,128)S(1)} all-to-all(f32[8,40,256]{2,1,0:T(8,128)S(1)} %shard_map.63), channel_id=1, replica_groups=mesh['real'=8,'gen'=16] {'real'}, dimensions={0} | all-to-all | bytes 655360 | tf_op jit(solution)/shard_map/all_to_all | solution.py:463
  49.7 14.4 %shard_map.64 = f32[8,40,256]{2,1,0:T(8,128)S(1)} custom-call(f32[8,40,256]{2,1,0:T(8,128)S(1)} %all_to_all.30.hall_ref, f32[8,32,256]{2,1,0:T(8,128)S(1)} %all-to-all-done.1.others_ref, f32[8,32,256]{2,1,0:T(8,128)S(1)} %collective-permute-done.more_ref, bf16[2048,256]{1,0:T(8,128)(2,1)S(1)} %get-tuple-element.31.front_ref, f32[16384,256]{1,0:T(8,128)} %rows_ref.3, ...), custom_call_target="tpu_custom_call" | custom-call | flops 6442450944 | bytes 16777216 | tf_op jit(solution)/shard_map/pallas_call | solution.py:402
  64.1 10.2 %all_to_all.31.parts_ref = f32[8,40,256]{2,1,0:T(8,128)S(1)} all-to-all(f32[8,40,256]{2,1,0:T(8,128)S(1)} %shard_map.64), channel_id=1, replica_groups=mesh['real'=8,'gen'=16] {'real'}, dimensions={0} | all-to-all | bytes 655360 | tf_op jit(solution)/shard_map/all_to_all | solution.py:463
  74.3 10.2 %all_to_all.32.gh_ref = f32[8,40,256]{2,1,0:T(8,128)S(1)} all-to-all(f32[8,40,256]{2,1,0:T(8,128)S(1)} %shard_map.65), channel_id=1, replica_groups=mesh['real'=8,'gen'=16] {'real'}, dimensions={0} | all-to-all | bytes 655360 | tf_op jit(solution)/shard_map/all_to_all | solution.py:463
  84.5 0.0 copy-done
  84.5 0.0 copy-done.1
  84.5 0.0 copy-done.2
  84.5 4.2 %shard_map.66 = f32[72,256]{1,0:T(8,128)S(1)} custom-call(f32[8,40,256]{2,1,0:T(8,128)S(1)} %all_to_all.32.gh_ref, f32[64,256]{1,0:T(8,128)S(1)} %copy-done.1, f32[64,256]{1,0:T(8,128)S(1)} %copy-done.2, f32[256,256]{1,0:T(8,128)S(1)} %copy-done), custom_call_target="tpu_custom_call" | custom-call | tf_op jit(solution)/shard_map/pallas_call | solution.py:123
  88.7 0.1 collective-permute-start.1
  88.8 1.3 %collective-permute-done.1 = f32[72,256]{1,0:T(8,128)S(1)} collective-permute-done((f32[72,256]{1,0:T(8,128)S(1)}, f32[72,256]{1,0:T(8,128)S(1)}, u32[]{:S(2)}, u32[]{:S(2)}) %collective-permute-start.1) | collective-permute-done | bytes 73760 | tf_op jit(solution)/shard_map/ppermute | solution.py:456
  90.1 1.9 %collective-permute-start.2 = (f32[72,256]{1,0:T(8,128)S(1)}, f32[72,256]{1,0:T(8,128)S(1)}, u32[]{:S(2)}, u32[]{:S(2)}) collective-permute-start(f32[72,256]{1,0:T(8,128)S(1)} %add.19), channel_id=1, source_target_pairs={{0,2},{1,3},{2,0},{3,1},{4,6},{5,7},{6,4},{7,5},{8,10},{9,11},{10,... | collective-permute-start | bytes 221192 | tf_op jit(solution)/shard_map/ppermute | solution.py:456
  92.0 4.0 %collective-permute-done.2 = f32[72,256]{1,0:T(8,128)S(1)} collective-permute-done((f32[72,256]{1,0:T(8,128)S(1)}, f32[72,256]{1,0:T(8,128)S(1)}, u32[]{:S(2)}, u32[]{:S(2)}) %collective-permute-start.2) | collective-permute-done | bytes 73760 | tf_op jit(solution)/shard_map/ppermute | solution.py:456
  96.0 1.3 %collective-permute-start.5 = (f32[72,256]{1,0:T(8,128)S(1)}, f32[72,256]{1,0:T(8,128)S(1)}, u32[]{:S(2)}, u32[]{:S(2)}) collective-permute-start(f32[72,256]{1,0:T(8,128)S(1)} %add.20), channel_id=1, source_target_pairs={{0,12},{1,13},{2,14},{3,15},{4,8},{5,9},{6,10},{7,11},{8,4},{9,5},... | collective-permute-start | bytes 221192 | tf_op jit(solution)/shard_map/ppermute | solution.py:456
  97.3 1.1 collective-permute-start.4
  98.5 1.7 %collective-permute-start.3 = (f32[72,256]{1,0:T(8,128)S(1)}, f32[72,256]{1,0:T(8,128)S(1)}, u32[]{:S(2)}, u32[]{:S(2)}) collective-permute-start(f32[72,256]{1,0:T(8,128)S(1)} %add.20), channel_id=1, source_target_pairs={{0,4},{1,5},{2,6},{3,7},{4,0},{5,1},{6,2},{7,3},{8,12},{9,13},{10,... | collective-permute-start | bytes 221192 | tf_op jit(solution)/shard_map/ppermute | solution.py:456
  100.2 1.6 %collective-permute-done.5 = f32[72,256]{1,0:T(8,128)S(1)} collective-permute-done((f32[72,256]{1,0:T(8,128)S(1)}, f32[72,256]{1,0:T(8,128)S(1)}, u32[]{:S(2)}, u32[]{:S(2)}) %collective-permute-start.5) | collective-permute-done | bytes 73760 | tf_op jit(solution)/shard_map/ppermute | solution.py:456
  101.8 1.5 %collective-permute-done.4 = f32[72,256]{1,0:T(8,128)S(1)} collective-permute-done((f32[72,256]{1,0:T(8,128)S(1)}, f32[72,256]{1,0:T(8,128)S(1)}, u32[]{:S(2)}, u32[]{:S(2)}) %collective-permute-start.4) | collective-permute-done | bytes 73760 | tf_op jit(solution)/shard_map/ppermute | solution.py:456
  103.2 0.1 collective-permute-done.3
  103.3 0.1 shard_map.67
  103.4 8.7 %all_to_all.33.sq_ref = f32[8,8,128]{2,1,0:T(8,128)S(1)} all-to-all(f32[8,8,128]{2,1,0:T(8,128)S(1)} %shard_map.67), channel_id=1, replica_groups=mesh['real'=8,'gen'=16] {'real'}, dimensions={0} | all-to-all | bytes 65536 | tf_op jit(solution)/shard_map/all_to_all | solution.py:463
  112.1 0.7 shard_map.68
  (4 shorter events, 0.1 us)
Async XLA Ops:
  0.6 17.2 %copy-start.3 = (s32[256]{0:T(256)S(1)}, s32[256]{0:T(256)}, u32[]{:S(2)}) copy-start(s32[256]{0:T(256)} %param.6) | copy-start | bytes 3076
  6.0 13.6 %all-to-all-start = ((f32[8,32,256]{2,1,0:T(8,128)}), f32[8,32,256]{2,1,0:T(8,128)S(1)}, u32[]{:S(2)}, u32[]{:S(2)}) async-start(f32[8,32,256]{2,1,0:T(8,128)} %bitcast.8), calls=%async_computation | async-start | bytes 524288 | tf_op jit(solution)/shard_map/all_to_all | solution.py:463
  20.4 15.1 %all-to-all-start.1 = ((f32[8,32,256]{2,1,0:T(8,128)}), f32[8,32,256]{2,1,0:T(8,128)S(1)}, u32[]{:S(2)}, u32[]{:S(2)}) async-start(f32[8,32,256]{2,1,0:T(8,128)} %shard_map.61.own_ref), calls=%async_computation.1 | async-start | bytes 524288 | tf_op jit(solution)/shard_map/all_to_all | solution.py:463
  31.7 52.8 %copy-start = (f32[256,256]{1,0:T(8,128)S(1)}, f32[256,256]{1,0:T(8,128)}, u32[]{:S(2)}) copy-start(f32[256,256]{1,0:T(8,128)} %hid_ref.3) | copy-start | bytes 786436
  31.7 52.8 %copy-start.1 = (f32[64,256]{1,0:T(8,128)S(1)}, f32[64,256]{1,0:T(8,128)}, u32[]{:S(2)}) copy-start(f32[64,256]{1,0:T(8,128)} %get-tuple-element.34.val_ref) | copy-start | bytes 196612
  31.7 52.8 %copy-start.2 = (f32[64,256]{1,0:T(8,128)S(1)}, f32[64,256]{1,0:T(8,128)}, u32[]{:S(2)}) copy-start(f32[64,256]{1,0:T(8,128)} %get-tuple-element.35.sig_ref) | copy-start | bytes 196612
  35.5 1.5 %collective-permute-start = (f32[8,32,256]{2,1,0:T(8,128)S(1)}, f32[8,32,256]{2,1,0:T(8,128)S(1)}, u32[]{:S(2)}, u32[]{:S(2)}) collective-permute-start(f32[8,32,256]{2,1,0:T(8,128)S(1)} %all-to-all-done.1.others_ref), channel_id=1, source_target_pairs={{0,1},{1,0},{2,3},{3,2},{4,5},{5,4},{6,7},{7,6},{8,9},{9,8},{10,11... | collective-permute-start | bytes 786440 | tf_op jit(solution)/shard_map/ppermute | solution.py:494
  88.7 1.3 %collective-permute-start.1 = (f32[72,256]{1,0:T(8,128)S(1)}, f32[72,256]{1,0:T(8,128)S(1)}, u32[]{:S(2)}, u32[]{:S(2)}) collective-permute-start(f32[72,256]{1,0:T(8,128)S(1)} %shard_map.66), channel_id=1, source_target_pairs={{0,1},{1,0},{2,3},{3,2},{4,5},{5,4},{6,7},{7,6},{8,9},{9,8},{10,11... | collective-permute-start | bytes 221192 | tf_op jit(solution)/shard_map/ppermute | solution.py:456
  90.1 5.9 %collective-permute-start.2 = (f32[72,256]{1,0:T(8,128)S(1)}, f32[72,256]{1,0:T(8,128)S(1)}, u32[]{:S(2)}, u32[]{:S(2)}) collective-permute-start(f32[72,256]{1,0:T(8,128)S(1)} %add.19), channel_id=1, source_target_pairs={{0,2},{1,3},{2,0},{3,1},{4,6},{5,7},{6,4},{7,5},{8,10},{9,11},{10,... | collective-permute-start | bytes 221192 | tf_op jit(solution)/shard_map/ppermute | solution.py:456
  96.0 5.7 %collective-permute-start.5 = (f32[72,256]{1,0:T(8,128)S(1)}, f32[72,256]{1,0:T(8,128)S(1)}, u32[]{:S(2)}, u32[]{:S(2)}) collective-permute-start(f32[72,256]{1,0:T(8,128)S(1)} %add.20), channel_id=1, source_target_pairs={{0,12},{1,13},{2,14},{3,15},{4,8},{5,9},{6,10},{7,11},{8,4},{9,5},... | collective-permute-start | bytes 221192 | tf_op jit(solution)/shard_map/ppermute | solution.py:456
  97.3 5.9 %collective-permute-start.4 = (f32[72,256]{1,0:T(8,128)S(1)}, f32[72,256]{1,0:T(8,128)S(1)}, u32[]{:S(2)}, u32[]{:S(2)}) collective-permute-start(f32[72,256]{1,0:T(8,128)S(1)} %add.20), channel_id=1, source_target_pairs={{0,8},{1,9},{2,10},{3,11},{4,12},{5,13},{6,14},{7,15},{8,0},{9,1},... | collective-permute-start | bytes 221192 | tf_op jit(solution)/shard_map/ppermute | solution.py:456
  98.5 4.8 %collective-permute-start.3 = (f32[72,256]{1,0:T(8,128)S(1)}, f32[72,256]{1,0:T(8,128)S(1)}, u32[]{:S(2)}, u32[]{:S(2)}) collective-permute-start(f32[72,256]{1,0:T(8,128)S(1)} %add.20), channel_id=1, source_target_pairs={{0,4},{1,5},{2,6},{3,7},{4,0},{5,1},{6,2},{7,3},{8,12},{9,13},{10,... | collective-permute-start | bytes 221192 | tf_op jit(solution)/shard_map/ppermute | solution.py:456
